TPU v7x, 128 devices: a whole 4x4x4 slice. The times are simulated.
128 devices in a mesh: section: 4 (over x), dp: 32 (over z, y, core).
Axes of the slice: x: 4, y: 4, z: 4, core: 2. Of those that a mesh axis runs over, the one named last changes fastest.
Arguments:
- tokens: bfloat16 [4096, 8192], P('dp'), may hold values from -6 to 6
- blocks_in: bfloat16 [4, 160, 128, 128], P('section', 'dp'), may hold values from -0.078125 to 0.078125
- blocks_out: bfloat16 [4, 160, 128, 128], P('section', 'dp'), may hold values from -0.3125 to 0.3125
- pos_in: int32 [4, 160], P('section', 'dp'), may hold values from 0 to 256, as said below
- pos_out: int32 [4, 160], P('section', 'dp'), may hold values from 0 to 256, as said below
- cotangent: bfloat16 [4096, 8192], P('dp'), may hold values from -0.08984375 to 0.08984375
Outputs:
- grad_in: bfloat16 [4, 160, 128, 128], P('section', 'dp')
- grad_out: bfloat16 [4, 160, 128, 128], P('section', 'dp')
Inputs may be any that keep to these rules, and one draw needn't show every extreme that they name: For each layer the first k slots (k from 110 to 160) hold distinct block numbers and the other slots hold 256, marking an empty slot; in each of pos_in and pos_out some layer fills all 160 slots. `pos_out`: as for pos_in, drawn independently.
All inputs are finite; a program needn't handle non-finite values.
Results may differ from a plain program's by a relative error of at most 0.023.
Values may be sent and summed in bfloat16 or wider, within the bound.
No kernel may reach another device: no remote copies, remote signals or barrier semaphores. Data moves between devices by JAX's collectives and lax.ppermute only.
A program may use at most 128 MiB of HBM per device.

v0:
```python
import jax
import jax.numpy as jnp
from jax import lax
from jax.sharding import PartitionSpec as P

D = 8192
RANK = 512
BLOCK = 128
MICRO = 2


EPS = 1e-05


def from_behind(block, axis, distance):
    devices = range(lax.axis_size(axis))
    route = [(i - distance, i) for i in devices if i - distance in devices]
    return lax.ppermute(block, axis, route)


def expand(blocks, places, rows_b, cols_b):
    flat = jnp.zeros((rows_b * cols_b, BLOCK, BLOCK), blocks.dtype)
    flat = flat.at[places].set(blocks, mode="drop")
    return (
        flat.reshape(rows_b, cols_b, BLOCK, BLOCK)
        .transpose(0, 2, 1, 3)
        .reshape(rows_b * BLOCK, cols_b * BLOCK)
    )


def slot_grads(left, right, places, rows_b, cols_b):
    count = left.shape[0]
    valid = places < rows_b * cols_b
    row_block = jnp.where(valid, places // cols_b, 0).astype(jnp.int32)
    col_block = jnp.where(valid, places % cols_b, 0).astype(jnp.int32)
    left_blocks = jnp.take(left.reshape(count, rows_b, BLOCK), row_block, axis=1)
    right_blocks = jnp.take(right.reshape(count, cols_b, BLOCK), col_block, axis=1)
    result = jnp.einsum(
        "tjb,tjc->jbc", left_blocks, right_blocks, preferred_element_type=jnp.float32
    )
    return jnp.where(valid[:, None, None], result, 0.0)


def norm_parts(hidden):
    wide = hidden.astype(jnp.float32)
    scale = jnp.sqrt(jnp.mean(wide * wide, axis=-1, keepdims=True) + EPS)
    return (wide, scale)


def forward_layer(hidden, mat_a, mat_b):
    wide, scale = norm_parts(hidden)
    normed = (wide / scale).astype(jnp.bfloat16)
    pre = jnp.dot(normed, mat_a, preferred_element_type=jnp.float32)
    act = (pre * jax.nn.sigmoid(pre)).astype(jnp.bfloat16)
    return (wide + jnp.dot(act, mat_b, preferred_element_type=jnp.float32)).astype(jnp.bfloat16)


def backward_layer(hidden, upstream, mat_a, mat_b):
    wide, scale = norm_parts(hidden)
    unit = wide / scale
    normed = unit.astype(jnp.bfloat16)
    pre = jnp.dot(normed, mat_a, preferred_element_type=jnp.float32)
    sig = jax.nn.sigmoid(pre)
    act = (pre * sig).astype(jnp.bfloat16)
    dact = lax.dot_general(
        upstream, mat_b, (((1,), (1,)), ((), ())), preferred_element_type=jnp.float32
    )
    dpre = (dact * sig * (1.0 + pre * (1.0 - sig))).astype(jnp.bfloat16)
    dnorm = lax.dot_general(
        dpre, mat_a, (((1,), (1,)), ((), ())), preferred_element_type=jnp.float32
    )
    inner = jnp.mean(dnorm * unit, axis=-1, keepdims=True)
    earlier = (upstream.astype(jnp.float32) + (dnorm - unit * inner) / scale).astype(jnp.bfloat16)
    return (earlier, normed, dpre, act)


def store(stack, value, picked, active):
    updated = lax.dynamic_update_slice_in_dim(stack, value[None], picked, 0)
    return jnp.where(active, updated, stack)


def per_device(tokens, blocks_in, blocks_out, pos_in, pos_out, cotangent):
    sections = lax.axis_size("section")
    here = lax.axis_index("section")
    rows_d = D // BLOCK
    rows_k = RANK // BLOCK
    full_in, full_out, all_in, all_out = (
        lax.all_gather(blocks_in, "dp", axis=1, tiled=True),
        lax.all_gather(blocks_out, "dp", axis=1, tiled=True),
        lax.all_gather(pos_in, "dp", axis=1, tiled=True),
        lax.all_gather(pos_out, "dp", axis=1, tiled=True),
    )
    mat_a = expand(full_in[0], all_in[0], rows_d, rows_k)
    mat_b = expand(full_out[0], all_out[0], rows_k, rows_d)
    micro_rows = tokens.shape[0] // MICRO
    turns = MICRO + sections - 1
    saved = jnp.zeros((MICRO, micro_rows, D), jnp.bfloat16)
    carried = jnp.zeros((micro_rows, D), jnp.bfloat16)
    for turn in range(turns):
        micro = turn - here
        active = (micro >= 0) & (micro < MICRO)
        picked = jnp.clip(micro, 0, MICRO - 1)
        first = lax.dynamic_slice_in_dim(tokens, picked * micro_rows, micro_rows, 0)
        entering = jnp.where(here == 0, first, carried)
        saved = store(saved, entering, picked, active)
        if turn < turns - 1:
            leaving = lax.cond(
                active, lambda x: forward_layer(x, mat_a, mat_b), lambda x: x, entering
            )
            carried = from_behind(leaving, "section", 1)
    kept_normed = jnp.zeros((MICRO, micro_rows, D), jnp.bfloat16)
    kept_dpre = jnp.zeros((MICRO, micro_rows, RANK), jnp.bfloat16)
    kept_act = jnp.zeros((MICRO, micro_rows, RANK), jnp.bfloat16)
    kept_upper = jnp.zeros((MICRO, micro_rows, D), jnp.bfloat16)
    carried_grad = jnp.zeros((micro_rows, D), jnp.bfloat16)
    for turn in range(turns):
        micro = turn - (sections - 1 - here)
        active = (micro >= 0) & (micro < MICRO)
        picked = jnp.clip(micro, 0, MICRO - 1)
        last = lax.dynamic_slice_in_dim(cotangent, picked * micro_rows, micro_rows, 0)
        upstream = jnp.where(here == sections - 1, last, carried_grad)
        hidden = lax.dynamic_index_in_dim(saved, picked, 0, keepdims=False)

        def run_layer():
            return backward_layer(hidden, upstream, mat_a, mat_b)

        def skip_layer():
            return (
                upstream,
                jnp.zeros((micro_rows, D), jnp.bfloat16),
                jnp.zeros((micro_rows, RANK), jnp.bfloat16),
                jnp.zeros((micro_rows, RANK), jnp.bfloat16),
            )

        earlier, normed, dpre, act = lax.cond(active, run_layer, skip_layer)
        kept_normed = store(kept_normed, normed, picked, active)
        kept_dpre = store(kept_dpre, dpre, picked, active)
        kept_act = store(kept_act, act, picked, active)
        kept_upper = store(kept_upper, upstream, picked, active)
        if turn < turns - 1:
            carried_grad = from_behind(earlier, "section", -1)
    all_rows = MICRO * micro_rows
    terms_in = slot_grads(
        kept_normed.reshape(all_rows, D),
        kept_dpre.reshape(all_rows, RANK),
        all_in[0],
        rows_d,
        rows_k,
    )[None]
    terms_out = slot_grads(
        kept_act.reshape(all_rows, RANK),
        kept_upper.reshape(all_rows, D),
        all_out[0],
        rows_k,
        rows_d,
    )[None]
    sums_in, sums_out = (
        lax.psum_scatter(
            terms_in.astype(jnp.bfloat16), "dp", scatter_dimension=1, tiled=True
        ).astype(jnp.float32),
        lax.psum_scatter(
            terms_out.astype(jnp.bfloat16), "dp", scatter_dimension=1, tiled=True
        ).astype(jnp.float32),
    )
    return (sums_in.astype(jnp.bfloat16), sums_out.astype(jnp.bfloat16))


def solution(mesh):
    in_specs = (
        P("dp", None),
        P("section", "dp", None, None),
        P("section", "dp", None, None),
        P("section", "dp"),
        P("section", "dp"),
        P("dp", None),
    )
    out_specs = (P("section", "dp", None, None), P("section", "dp", None, None))
    return jax.shard_map(
        per_device, mesh=mesh, in_specs=in_specs, out_specs=out_specs, check_vma=False
    )
```

profile of v0, /device:TPU:0, one launch (start us, length us, event | category | flops | bytes accessed | tf_op | source)
XLA Modules:
  0.0 731.6 jit_solution(17489583742107642907)
XLA Ops:
  12.1 18.3 %all-reduce.2 = (s32[160]{0:T(256)S(1)}, s32[160]{0:T(256)S(1)}) all-reduce(s32[160]{0:T(256)S(1)} %bitcast_dynamic-update-slice_fusion.3, s32[160]{0:T(256)S(1)} %bitcast_dynamic-update-slice_fusion.2), channel_id=1, replica_groups=mesh['section'=4,'dp'=32] {'dp'}, use_global_device_ids=true, to_apply=%add | all-reduce | flops 320 | bytes 2560 | tf_op jit(solution)/shard_map/squeeze | solution.py:146
  33.3 27.0 %all-gather.3.cloned.1.call-done = bf16[1,160,128,128]{3,2,0,1:T(8,128)(2,1)} async-done(((bf16[1,5,128,128]{3,2,0,1:T(8,128)(2,1)}), bf16[1,160,128,128]{3,2,0,1:T(8,128)(2,1)}) %all-gather.3.cloned.1.call-update) | async-done | bytes 5242896 | tf_op jit(solution)/shard_map/all_gather | solution.py:89
  65.7 24.5 %scatter_fusion = bf16[256,128,128]{2,1,0:T(8,128)(2,1)} fusion(bf16[256,128,128]{2,1,0:T(8,128)(2,1)} %broadcast.405.clone.1, s32[160]{0:T(256)S(1)} %bitcast.233, bf16[160,128,128]{2,1,0:T(8,128)(2,1)} %bitcast.224), kind=kCustom, calls=%fused_computation.4 | custom fusion | bytes 15729280 | tf_op jit(solution)/shard_map/scatter | solution.py:23
  90.3 12.5 %copy.28 = bf16[4,128,64,128]{3,2,1,0:T(8,128)(2,1)} copy(bf16[4,128,64,128]{3,1,2,0:T(8,128)(2,1)} %bitcast.213) | data formatting | bytes 16777216 | tf_op jit(solution)/shard_map/transpose | solution.py:26
  102.8 6.7 all-gather.5.cloned.1.call-done
  114.9 24.2 %scatter_fusion.1 = bf16[256,128,128]{2,1,0:T(8,128)(2,1)} fusion(bf16[256,128,128]{2,1,0:T(8,128)(2,1)} %broadcast.405.clone, s32[160]{0:T(256)S(1)} %bitcast.232, bf16[160,128,128]{2,1,0:T(8,128)(2,1)} %bitcast.225), kind=kCustom, calls=%fused_computation.5 | custom fusion | bytes 15729280 | tf_op jit(solution)/shard_map/scatter | solution.py:23
  139.0 12.1 %copy.30 = bf16[64,128,4,128]{1,0,3,2:T(8,128)(2,1)} copy(bf16[64,128,4,128]{3,1,2,0:T(8,128)(2,1)} %bitcast.214) | data formatting | bytes 16777216 | tf_op jit(solution)/shard_map/transpose | solution.py:26
  151.1 39.6 %copy_bitcast_fusion = (bf16[8192,512]{0,1:T(8,128)(2,1)}, bf16[512,8192]{1,0:T(8,128)(2,1)}) fusion(bf16[64,8,64,128]{3,2,1,0:T(8,128)(2,1)} %bitcast.217, bf16[64,8,64,128]{3,2,1,0:T(8,128)(2,1)} %bitcast.216), kind=kLoop, calls=%fused_computation.147 | loop fusion | bytes 33554432 | tf_op jit(solution)/shard_map/reshape | solution.py:27
  190.7 12.9 %conditional.9 = (bf16[64,8192]{1,0:T(8,128)(2,1)}) conditional(s32[]{:T(128)} %convert_element_type.259, bf16[64,8192]{1,0:T(8,128)(2,1)} %get-tuple-element.354, (bf16[64,8192]{1,0:T(8,128)(2,1)}, bf16[8192,512]{0,1:T(8,128)(2,1)}, bf16[512,8192]{1,0:T(8,128)(2,1)}) %tuple.114), branch_computations={%region_2.3_spmd, %region_3.5_spmd} | conditional | flops 1078624256 | bytes 22021128 | solution.py:107
  192.2 11.0 %fusion = bf16[64,8192]{1,0:T(8,128)(2,1)} fusion(bf16[512,8192]{1,0:T(8,128)(2,1)} %get-tuple-element.178, bf16[64,8192]{1,0:T(8,128)(2,1)S(1)} %copy.175, bf16[8192,512]{0,1:T(8,128)(2,1)} %get-tuple-element.291, f32[64]{0:T(128)S(1)} %add_sqrt_fusion), kind=kOutput, calls=%fused_computation.7 | convolution fusion | flops 1077051392 | bytes 18874624 | tf_op jit(solution)/shard_map/cond/branch_1_fun/dot_general | solution.py:55
  205.0 23.3 %collective-permute-done = bf16[64,8192]{1,0:T(8,128)(2,1)S(1)} collective-permute-done((bf16[64,8192]{1,0:T(8,128)(2,1)}, bf16[64,8192]{1,0:T(8,128)(2,1)S(1)}, u32[]{:S(2)}, u32[]{:S(2)}) %collective-permute-start) | collective-permute-done | bytes 1048608 | tf_op jit(solution)/shard_map/ppermute | solution.py:18
  231.1 11.8 %conditional.10 = (bf16[64,8192]{1,0:T(8,128)(2,1)S(1)}) conditional(s32[]{:T(128)} %convert_element_type.260, bf16[64,8192]{1,0:T(8,128)(2,1)S(1)} %get-tuple-element.352, (bf16[64,8192]{1,0:T(8,128)(2,1)S(1)}, bf16[8192,512]{0,1:T(8,128)(2,1)}, bf16[512,8192]{1,0:T(8,128)(2,1)}) %tuple.115), branch_computations={%region_5.6_spmd, %region_6.8_spmd} | conditional | flops 1078624256 | bytes 26215460 | solution.py:107
  232.2 10.7 %fusion.12 = bf16[64,8192]{1,0:T(8,128)(2,1)S(1)} fusion(bf16[512,8192]{1,0:T(8,128)(2,1)} %get-tuple-element.181, bf16[64,8192]{1,0:T(8,128)(2,1)} %copy-done.9, bf16[8192,512]{0,1:T(8,128)(2,1)} %get-tuple-element.294, f32[64]{0:T(128)S(1)} %add_sqrt_fusion.1), kind=kOutput, calls=%fused_computation.19 | convolution fusion | flops 1077051392 | bytes 18874624 | tf_op jit(solution)/shard_map/cond/branch_1_fun/dot_general | solution.py:55
  248.5 21.3 %collective-permute-done.1 = bf16[64,8192]{1,0:T(8,128)(2,1)} collective-permute-done((bf16[64,8192]{1,0:T(8,128)(2,1)S(1)}, bf16[64,8192]{1,0:T(8,128)(2,1)}, u32[]{:S(2)}, u32[]{:S(2)}) %collective-permute-start.1) | collective-permute-done | bytes 1048608 | tf_op jit(solution)/shard_map/ppermute | solution.py:18
  271.6 17.6 %collective-permute-start.2 = (bf16[64,8192]{1,0:T(8,128)(2,1)S(1)}, bf16[64,8192]{1,0:T(8,128)(2,1)}, u32[]{:S(2)}, u32[]{:S(2)}) collective-permute-start(bf16[64,8192]{1,0:T(8,128)(2,1)S(1)} %get-tuple-element.416), channel_id=1, source_target_pairs={{0,32},{32,64},{64,96},{1,33},{33,65},{65,97},{2,34},{34,66},{66,9... | collective-permute-start | bytes 3145736 | tf_op jit(solution)/shard_map/ppermute | solution.py:18
  289.1 20.4 %collective-permute-done.2 = bf16[64,8192]{1,0:T(8,128)(2,1)} collective-permute-done((bf16[64,8192]{1,0:T(8,128)(2,1)S(1)}, bf16[64,8192]{1,0:T(8,128)(2,1)}, u32[]{:S(2)}, u32[]{:S(2)}) %collective-permute-start.2) | collective-permute-done | bytes 1048608 | tf_op jit(solution)/shard_map/ppermute | solution.py:18
  320.2 17.9 %collective-permute-done.3 = bf16[64,8192]{1,0:T(8,128)(2,1)} collective-permute-done((bf16[64,8192]{1,0:T(8,128)(2,1)}, bf16[64,8192]{1,0:T(8,128)(2,1)}, u32[]{:S(2)}, u32[]{:S(2)}) %collective-permute-start.3) | collective-permute-done | bytes 1048608 | tf_op jit(solution)/shard_map/ppermute | solution.py:18
  343.5 35.1 %collective-permute-done.4 = bf16[64,8192]{1,0:T(8,128)(2,1)} collective-permute-done((bf16[64,8192]{1,0:T(8,128)(2,1)S(1)}, bf16[64,8192]{1,0:T(8,128)(2,1)}, u32[]{:S(2)}, u32[]{:S(2)}) %collective-permute-start.4) | collective-permute-done | bytes 1048608 | tf_op jit(solution)/shard_map/ppermute | solution.py:18
  385.4 22.5 %collective-permute-done.5 = bf16[64,8192]{1,0:T(8,128)(2,1)} collective-permute-done((bf16[64,8192]{1,0:T(8,128)(2,1)S(1)}, bf16[64,8192]{1,0:T(8,128)(2,1)}, u32[]{:S(2)}, u32[]{:S(2)}) %collective-permute-start.5) | collective-permute-done | bytes 1048608 | tf_op jit(solution)/shard_map/ppermute | solution.py:18
  416.1 54.8 %collective-permute-done.6 = bf16[64,8192]{1,0:T(8,128)(2,1)S(1)} collective-permute-done((bf16[64,8192]{1,0:T(8,128)(2,1)S(1)}, bf16[64,8192]{1,0:T(8,128)(2,1)S(1)}, u32[]{:S(2)}, u32[]{:S(2)}) %collective-permute-start.6) | collective-permute-done | bytes 1048608 | tf_op jit(solution)/shard_map/ppermute | solution.py:18
  473.9 12.3 %conditional.16 = (bf16[64,8192]{1,0:T(8,128)(2,1)S(1)}, bf16[1,64,8192]{2,1,0:T(8,128)(2,1)S(1)}, bf16[1,64,512]{2,1,0:T(8,128)(2,1)}, bf16[1,64,512]{2,1,0:T(8,128)(2,1)S(1)}) conditional(s32[]{:T(128)} %convert_element_type.265, bf16[64,8192]{1,0:T(8,128)(2,1)S(1)} %get-tuple-element.336, (bf16[64,8192]{1,0:T(8,128)(2,1)S(1)}, ...), branch_computations={%region_26.27_spmd, %region_27.30_spmd} | conditional | flops 1622081536 | bytes 64818304 | solution.py:135
  474.4 6.2 fusion.84
  488.5 20.3 %collective-permute-done.7 = bf16[64,8192]{1,0:T(8,128)(2,1)S(1)} collective-permute-done((bf16[64,8192]{1,0:T(8,128)(2,1)S(1)}, bf16[64,8192]{1,0:T(8,128)(2,1)S(1)}, u32[]{:S(2)}, u32[]{:S(2)}) %collective-permute-start.7) | collective-permute-done | bytes 1048608 | tf_op jit(solution)/shard_map/ppermute | solution.py:18
  511.8 10.8 %conditional.17 = (bf16[1,64,8192]{2,1,0:T(8,128)(2,1)}, bf16[1,64,512]{2,1,0:T(8,128)(2,1)S(1)}, bf16[1,64,512]{2,1,0:T(8,128)(2,1)S(1)}) conditional(s32[]{:T(128)} %convert_element_type.266, () %tuple.122, (bf16[2,64,8192]{2,1,0:T(8,128)(2,1)S(1)}, s32[]{:T(128)}, bf16[64,8192]{1,0:T(8,128)(2,1)S(1)}, bf16[512,8192]{1,0:T(8,128)(2,1)}, ...), branch_computations={%region_30.31_spmd, %region_31.33_spmd} | conditional | flops 1078919168 | bytes 56100416 | solution.py:135
  527.5 7.6 %gather_fusion.2 = bf16[160,128,128]{2,1,0:T(8,128)(2,1)} fusion(bf16[128,4,128]{2,0,1:T(8,128)(2,1)S(1)} %copy.43, s32[1024]{0:T(1024)S(1)} %pad_clamp_fusion.1), kind=kCustom, calls=%fused_computation.3.clone | custom fusion | bytes 10486400 | tf_op jit(solution)/shard_map/jit(_take)/gather | solution.py:36
  535.1 9.4 %gather_fusion.3 = bf16[160,128,128]{2,1,0:T(8,128)(2,1)} fusion(bf16[128,64,128]{2,0,1:T(8,128)(2,1)} %copy.44, s32[1024]{0:T(1024)S(1)} %pad_clamp_fusion), kind=kCustom, calls=%fused_computation.2.clone | custom fusion | bytes 10486400 | tf_op jit(solution)/shard_map/jit(_take)/gather | solution.py:37
  544.5 9.5 %fusion.103 = bf16[1,160,128,128]{3,2,1,0:T(8,128)(2,1)} fusion(pred[160]{0:T(512)(128)(4,1)S(1)} %copy-done.34, bf16[160,128,128]{2,1,0:T(8,128)(2,1)} %gather_fusion.3, pred[160]{0:T(512)(128)(4,1)S(1)} %copy-done.35, bf16[160,128,128]{2,1,0:T(8,128)(2,1)} %gather_fusion.2, pred[160]{0:T(512)(128)(4,1)S(1)} %copy-done.33), kind=kOutput, calls=%fused_computation.150 | convolution fusion | flops 681574400 | bytes 15729120 | tf_op jit(solution)/shard_map/tjb,tjc->jbc/dot_general | solution.py:38
  570.7 9.4 %gather_fusion = bf16[160,128,128]{2,1,0:T(8,128)(2,1)} fusion(bf16[128,64,128]{2,0,1:T(8,128)(2,1)} %copy.40, s32[1024]{0:T(1024)S(1)} %pad_clamp_fusion.3), kind=kCustom, calls=%fused_computation.clone | custom fusion | bytes 10486400 | tf_op jit(solution)/shard_map/jit(_take)/gather | solution.py:36
  580.2 7.6 %gather_fusion.1 = bf16[160,128,128]{2,1,0:T(8,128)(2,1)} fusion(bf16[128,4,128]{2,0,1:T(8,128)(2,1)S(1)} %copy.41, s32[1024]{0:T(1024)S(1)} %pad_clamp_fusion.2), kind=kCustom, calls=%fused_computation.1.clone | custom fusion | bytes 10486400 | tf_op jit(solution)/shard_map/jit(_take)/gather | solution.py:37
  587.8 9.4 %fusion.102 = bf16[1,160,128,128]{3,2,1,0:T(8,128)(2,1)} fusion(pred[160]{0:T(512)(128)(4,1)S(1)} %copy-done.31, bf16[160,128,128]{2,1,0:T(8,128)(2,1)} %gather_fusion.1, pred[160]{0:T(512)(128)(4,1)S(1)} %copy-done.30, bf16[160,128,128]{2,1,0:T(8,128)(2,1)} %gather_fusion, pred[160]{0:T(512)(128)(4,1)S(1)} %copy-done.32), kind=kOutput, calls=%fused_computation.149 | convolution fusion | flops 681574400 | bytes 15729120 | tf_op jit(solution)/shard_map/tjb,tjc->jbc/dot_general | solution.py:38
  597.2 38.8 %reduce-scatter.5.cloned.1.call-done = bf16[1,5,128,128]{3,2,1,0:T(8,128)(2,1)} async-done(((bf16[1,160,128,128]{3,2,1,0:T(8,128)(2,1)}), bf16[1,5,128,128]{3,2,1,0:T(8,128)(2,1)}) %reduce-scatter.5.cloned.1.call-update) | async-done | bytes 163856 | tf_op jit(solution)/shard_map/reduce_scatter | solution.py:161
  636.0 88.6 %reduce-scatter.3.cloned.1.call-done = bf16[1,5,128,128]{3,2,1,0:T(8,128)(2,1)} async-done(((bf16[1,160,128,128]{3,2,1,0:T(8,128)(2,1)}), bf16[1,5,128,128]{3,2,1,0:T(8,128)(2,1)}) %reduce-scatter.3.cloned.1.call-update) | async-done | bytes 163856 | tf_op jit(solution)/shard_map/reduce_scatter | solution.py:158
  (160 shorter events, 110.7 us)
Async XLA Ops:
  7.2 53.2 %all-gather.3.cloned.1.call-start = ((), (), s32[]{:S(2)}) async-start(), calls=%async_computation.2 | async-start | bytes 5406720 | tf_op jit(solution)/shard_map/all_gather | solution.py:89
  7.9 101.5 %all-gather.5.cloned.1.call-start = ((), (), s32[]{:S(2)}) async-start(), calls=%async_computation.3 | async-start | bytes 5406720 | tf_op jit(solution)/shard_map/all_gather | solution.py:88
  8.6 627.4 %reduce-scatter.5.cloned.1.call-start = ((), (), s32[]{:S(2)}) async-start(), calls=%async_computation.5 | async-start | bytes 5406720 | tf_op jit(solution)/shard_map/reduce_scatter | solution.py:161
  203.6 24.7 %collective-permute-start = (bf16[64,8192]{1,0:T(8,128)(2,1)}, bf16[64,8192]{1,0:T(8,128)(2,1)S(1)}, u32[]{:S(2)}, u32[]{:S(2)}) collective-permute-start(bf16[64,8192]{1,0:T(8,128)(2,1)} %get-tuple-element.414), channel_id=1, source_target_pairs={{0,32},{32,64},{64,96},{1,33},{33,65},{65,97},{2,34},{34,66},{66,9... | collective-permute-start | bytes 3145736 | tf_op jit(solution)/shard_map/ppermute | solution.py:18
  242.9 26.9 %collective-permute-start.1 = (bf16[64,8192]{1,0:T(8,128)(2,1)S(1)}, bf16[64,8192]{1,0:T(8,128)(2,1)}, u32[]{:S(2)}, u32[]{:S(2)}) collective-permute-start(bf16[64,8192]{1,0:T(8,128)(2,1)S(1)} %get-tuple-element.415), channel_id=1, source_target_pairs={{0,32},{32,64},{64,96},{1,33},{33,65},{65,97},{2,34},{34,66},{66,9... | collective-permute-start | bytes 3145736 | tf_op jit(solution)/shard_map/ppermute | solution.py:18
  271.6 38.0 %collective-permute-start.2 = (bf16[64,8192]{1,0:T(8,128)(2,1)S(1)}, bf16[64,8192]{1,0:T(8,128)(2,1)}, u32[]{:S(2)}, u32[]{:S(2)}) collective-permute-start(bf16[64,8192]{1,0:T(8,128)(2,1)S(1)} %get-tuple-element.416), channel_id=1, source_target_pairs={{0,32},{32,64},{64,96},{1,33},{33,65},{65,97},{2,34},{34,66},{66,9... | collective-permute-start | bytes 3145736 | tf_op jit(solution)/shard_map/ppermute | solution.py:18
  312.5 25.6 %collective-permute-start.3 = (bf16[64,8192]{1,0:T(8,128)(2,1)}, bf16[64,8192]{1,0:T(8,128)(2,1)}, u32[]{:S(2)}, u32[]{:S(2)}) collective-permute-start(bf16[64,8192]{1,0:T(8,128)(2,1)} %get-tuple-element.417), channel_id=1, source_target_pairs={{0,32},{32,64},{64,96},{1,33},{33,65},{65,97},{2,34},{34,66},{66,9... | collective-permute-start | bytes 3145736 | tf_op jit(solution)/shard_map/ppermute | solution.py:18
  318.3 21.6 %copy-start = (bf16[512,8192]{1,0:T(8,128)(2,1)S(1)}, bf16[512,8192]{1,0:T(8,128)(2,1)}, u32[]{:S(2)}) copy-start(bf16[512,8192]{1,0:T(8,128)(2,1)} %get-tuple-element.375) | copy-start | bytes 25165828
  320.2 17.9 %copy-start.5 = (bf16[2,64,8192]{2,1,0:T(8,128)(2,1)}, bf16[2,64,8192]{2,1,0:T(8,128)(2,1)S(1)}, u32[]{:S(2)}) copy-start(bf16[2,64,8192]{2,1,0:T(8,128)(2,1)S(1)} %get-tuple-element.341) | copy-start | bytes 6291460
  342.2 36.4 %collective-permute-start.4 = (bf16[64,8192]{1,0:T(8,128)(2,1)S(1)}, bf16[64,8192]{1,0:T(8,128)(2,1)}, u32[]{:S(2)}, u32[]{:S(2)}) collective-permute-start(bf16[64,8192]{1,0:T(8,128)(2,1)S(1)} %get-tuple-element.235), channel_id=1, source_target_pairs={{32,0},{64,32},{96,64},{33,1},{65,33},{97,65},{34,2},{66,34},{98,6... | collective-permute-start | bytes 3145736 | tf_op jit(solution)/shard_map/ppermute | solution.py:18
  383.4 24.5 %collective-permute-start.5 = (bf16[64,8192]{1,0:T(8,128)(2,1)S(1)}, bf16[64,8192]{1,0:T(8,128)(2,1)}, u32[]{:S(2)}, u32[]{:S(2)}) collective-permute-start(bf16[64,8192]{1,0:T(8,128)(2,1)S(1)} %get-tuple-element.237), channel_id=1, source_target_pairs={{32,0},{64,32},{96,64},{33,1},{65,33},{97,65},{34,2},{66,34},{98,6... | collective-permute-start | bytes 3145736 | tf_op jit(solution)/shard_map/ppermute | solution.py:18
  411.9 4.1 copy-start.13
  411.9 4.1 copy-start.24
  411.9 3.0 copy-start.18
  412.0 58.9 %collective-permute-start.6 = (bf16[64,8192]{1,0:T(8,128)(2,1)S(1)}, bf16[64,8192]{1,0:T(8,128)(2,1)S(1)}, u32[]{:S(2)}, u32[]{:S(2)}) collective-permute-start(bf16[64,8192]{1,0:T(8,128)(2,1)S(1)} %get-tuple-element.239), channel_id=1, source_target_pairs={{32,0},{64,32},{96,64},{33,1},{65,33},{97,65},{34,2},{66,34},{98,6... | collective-permute-start | bytes 3145736 | tf_op jit(solution)/shard_map/ppermute | solution.py:18
  413.4 60.5 %copy-start.1 = (bf16[512,8192]{1,0:T(8,128)(2,1)S(1)}, bf16[512,8192]{1,0:T(8,128)(2,1)}, u32[]{:S(2)}) copy-start(bf16[512,8192]{1,0:T(8,128)(2,1)} %get-tuple-element.375) | copy-start | bytes 25165828
  474.0 9.3 %slice-start.2 = ((s8[8388608]{0:T(1024)(128)(4,1)}), s8[4194304]{0:T(1024)(128)(4,1)S(1)}, s32[]{:S(2)}) async-start(s8[8388608]{0:T(1024)(128)(4,1)} %bitcast.222), calls=%async_computation.8 | async-start | bytes 8388608 | tf_op jit(solution)/shard_map/cond
  474.3 8.9 %slice-start.3 = ((s8[8388608]{0:T(1024)(128)(4,1)}), s8[4194304]{0:T(1024)(128)(4,1)S(1)}, s32[]{:S(2)}) async-start(s8[8388608]{0:T(1024)(128)(4,1)} %bitcast.222), calls=%async_computation.9 | async-start | bytes 8388608 | tf_op jit(solution)/shard_map/cond
  486.2 25.6 %copy-start.15 = (bf16[1,64,8192]{2,1,0:T(8,128)(2,1)}, bf16[1,64,8192]{2,1,0:T(8,128)(2,1)S(1)}, u32[]{:S(2)}) copy-start(bf16[1,64,8192]{2,1,0:T(8,128)(2,1)S(1)} %get-tuple-element.240) | copy-start | bytes 3145732
  486.2 22.6 %collective-permute-start.7 = (bf16[64,8192]{1,0:T(8,128)(2,1)S(1)}, bf16[64,8192]{1,0:T(8,128)(2,1)S(1)}, u32[]{:S(2)}, u32[]{:S(2)}) collective-permute-start(bf16[64,8192]{1,0:T(8,128)(2,1)S(1)} %get-tuple-element.241), channel_id=1, source_target_pairs={{32,0},{64,32},{96,64},{33,1},{65,33},{97,65},{34,2},{66,34},{98,6... | collective-permute-start | bytes 3145736 | tf_op jit(solution)/shard_map/ppermute | solution.py:18
  512.1 6.3 copy-start.4
  535.1 9.4 %copy-start.33 = (pred[160]{0:T(512)(128)(4,1)S(1)}, pred[160]{0:T(512)(128)(4,1)}, u32[]{:S(2)}) copy-start(pred[160]{0:T(512)(128)(4,1)} %get-tuple-element.329) | copy-start | bytes 484
  535.1 9.4 %copy-start.34 = (pred[160]{0:T(512)(128)(4,1)S(1)}, pred[160]{0:T(512)(128)(4,1)}, u32[]{:S(2)}) copy-start(pred[160]{0:T(512)(128)(4,1)} %get-tuple-element.363) | copy-start | bytes 484
  535.1 9.4 %copy-start.35 = (pred[160]{0:T(512)(128)(4,1)S(1)}, pred[160]{0:T(512)(128)(4,1)}, u32[]{:S(2)}) copy-start(pred[160]{0:T(512)(128)(4,1)} %get-tuple-element.364) | copy-start | bytes 484
  554.0 3.7 copy-start.23
  554.0 3.7 copy-start.14
  554.0 170.6 %reduce-scatter.3.cloned.1.call-start = ((), (), s32[]{:S(2)}) async-start(), calls=%async_computation.4 | async-start | bytes 5406720 | tf_op jit(solution)/shard_map/reduce_scatter | solution.py:158
  557.6 2.6 copy-start.26
  557.6 2.6 copy-start.16
  580.2 7.6 %copy-start.30 = (pred[160]{0:T(512)(128)(4,1)S(1)}, pred[160]{0:T(512)(128)(4,1)}, u32[]{:S(2)}) copy-start(pred[160]{0:T(512)(128)(4,1)} %get-tuple-element.369) | copy-start | bytes 484
  580.2 7.6 %copy-start.31 = (pred[160]{0:T(512)(128)(4,1)S(1)}, pred[160]{0:T(512)(128)(4,1)}, u32[]{:S(2)}) copy-start(pred[160]{0:T(512)(128)(4,1)} %get-tuple-element.371) | copy-start | bytes 484
  580.2 7.6 %copy-start.32 = (pred[160]{0:T(512)(128)(4,1)S(1)}, pred[160]{0:T(512)(128)(4,1)}, u32[]{:S(2)}) copy-start(pred[160]{0:T(512)(128)(4,1)} %get-tuple-element.372) | copy-start | bytes 484
  (9 other events, 10.6 us)
Sparse Core Ops, SparseCore 0:
  10.2 50.0 all-gather.2
  62.6 46.8 all-gather.4
  554.1 81.8 reduce-scatter.4
  640.7 83.9 reduce-scatter.2
where the time goes:
time: 741 us; the launch traced here: 732 us
  waiting for transfers between devices  378 us (51%)
  local copies, waits for them, and re-layouts  182 us (25%)
  matrix products  60.1 us (8%)
  other arithmetic  40.5 us (5%)
  starting transfers between devices  36 us (5%)
  blocking collectives  18.3 us (2%)
  between operations  15.4 us (2%)
    ppermute x8, waiting for transfers between devices, from_behind(): return lax.ppermute(block, axis, route)  216 us
    reduce_scatter x1, waiting for transfers between devices, per_device(): lax.psum_scatter(terms_in.astype(jnp.bfloat16), 'dp', scatter_dimension=1...  88.6 us
    scatter x2, local copies, waits for them, and re-layouts, expand(): flat = flat.at[places].set(blocks, mode='drop')  48.7 us
    reshape x1, local copies, waits for them, and re-layouts, expand(): return flat.reshape(rows_b, cols_b, BLOCK, BLOCK).transpose(0, 2, 1, 3).r...  39.6 us
    reduce_scatter x1, waiting for transfers between devices, per_device(): lax.psum_scatter(terms_out.astype(jnp.bfloat16), 'dp', scatter_dimension=...  38.8 us
    select_n x25, other arithmetic, store(): return jnp.where(active, updated, stack)  36.2 us
    ppermute x8, starting transfers between devices, from_behind(): return lax.ppermute(block, axis, route)  35.6 us
    all_gather x1, waiting for transfers between devices, per_device(): lax.all_gather(blocks_out, 'dp', axis=1, tiled=True)  27 us
  transfers between devices with their start and end apart: 12, of which 12 were waited for; matrix products, arithmetic and copies ran while one was open for 13% of the time, Pallas kernels for 0%

commit v1 on v0

v1 whole, which is shorter than its diff:
```python
import functools

import jax
import jax.numpy as jnp
from jax import lax
from jax.experimental import pallas as pl
from jax.experimental.pallas import tpu as pltpu
from jax.sharding import PartitionSpec as P

D = 8192
RANK = 512
BLOCK = 128
ROWS_D = D // BLOCK
ROWS_K = RANK // BLOCK
NBLK = ROWS_D * ROWS_K
EPS = 1e-05
CHUNK = 1024
BLOCKS = CHUNK // BLOCK
NT = (((1,), (1,)), ((), ()))
NN = (((1,), (0,)), ((), ()))
TN = (((0,), (0,)), ((), ()))
PAIR = [(0, 1), (1, 0), (2, 3), (3, 2)]
UP = [(0, 3), (1, 2)]
DOWN = [(3, 0), (2, 1)]


def dot(left, right, dims):
    return lax.dot_general(left, right, dims, preferred_element_type=jnp.float32)


def fetch(where_ref, weights_ref, base, number):
    code = where_ref[base + number]
    safe = jnp.maximum(code, 0)
    block = weights_ref[safe >> 3, 0, 0, safe & 7]
    return lax.select(code >= 0, block, jnp.zeros_like(block))


def assemble_in(where_ref, weights_ref, dense_ref, base, chunk):
    for row in range(BLOCKS):
        for col in range(ROWS_K):
            dense_ref[row * BLOCK : (row + 1) * BLOCK, col * BLOCK : (col + 1) * BLOCK] = fetch(
                where_ref, weights_ref, base, (chunk * BLOCKS + row) * ROWS_K + col
            )


def assemble_out(where_ref, weights_ref, dense_ref, base, chunk):
    for row in range(ROWS_K):
        for col in range(BLOCKS):
            dense_ref[row * BLOCK : (row + 1) * BLOCK, col * BLOCK : (col + 1) * BLOCK] = fetch(
                where_ref, weights_ref, base, row * ROWS_D + chunk * BLOCKS + col
            )


def columns(chunk):
    return pl.ds(pl.multiple_of(chunk * CHUNK, CHUNK), CHUNK)


def root(hidden_ref):
    def step(chunk, total):
        wide = hidden_ref[:, columns(chunk)].astype(jnp.float32)
        return total + jnp.sum(wide * wide, axis=-1, keepdims=True)

    total = lax.fori_loop(0, D // CHUNK, step, jnp.zeros((hidden_ref.shape[0], 1), jnp.float32))
    return jnp.sqrt(total / D + EPS)


def forward_kernel(swap_ref, where_ref, first_ref, weights_ref, second_ref, last_ref, pre_ref, act_ref, scale_ref, dense_in, dense_out):
    step = pl.program_id(0)

    def down(layer, hidden_ref):
        base = ((layer ^ swap_ref[0]) * 2) * NBLK
        scale = root(hidden_ref)
        scale_ref[layer] = jnp.broadcast_to(scale, scale_ref.shape[1:])
        pre_ref[layer] = jnp.zeros(pre_ref.shape[1:], jnp.float32)

        @pl.loop(0, D // CHUNK)
        def _(chunk):
            assemble_in(where_ref, weights_ref, dense_in, base, chunk)
            normed = (hidden_ref[:, columns(chunk)].astype(jnp.float32) / scale).astype(jnp.bfloat16)
            pre_ref[layer] += dot(normed, dense_in[...], NN)

    def up(layer, hidden_ref, next_ref):
        base = ((layer ^ swap_ref[0]) * 2 + 1) * NBLK
        pre = pre_ref[layer]
        act = (pre * jax.nn.sigmoid(pre)).astype(jnp.bfloat16)
        act_ref[layer] = act

        @pl.loop(0, D // CHUNK)
        def _(chunk):
            assemble_out(where_ref, weights_ref, dense_out, base, chunk)
            moved = dot(act_ref[layer], dense_out[...], NN)
            next_ref[:, columns(chunk)] = (hidden_ref[:, columns(chunk)].astype(jnp.float32) + moved).astype(jnp.bfloat16)

    pl.when(step == 0)(lambda: down(0, first_ref))
    pl.when(step == 1)(lambda: up(0, first_ref, second_ref))
    pl.when(step == 2)(lambda: down(1, second_ref))
    pl.when(step == 3)(lambda: up(1, second_ref, last_ref))


def backward_kernel(
    swap_ref, where_ref, first_ref, second_ref, grad_ref, pre_ref, scale_ref, weights_ref, middle_ref, earlier_ref, dpre_ref, total, inner, dense_in, dense_out
):
    step = pl.program_id(0)

    def up(layer, upstream_ref):
        base = ((layer ^ swap_ref[0]) * 2 + 1) * NBLK
        total[...] = jnp.zeros(total.shape, jnp.float32)

        @pl.loop(0, D // CHUNK)
        def _(chunk):
            assemble_out(where_ref, weights_ref, dense_out, base, chunk)
            total[...] += dot(upstream_ref[:, columns(chunk)], dense_out[...], NT)

        pre = pre_ref[layer]
        sig = jax.nn.sigmoid(pre)
        dpre = (total[...] * sig * (1.0 + pre * (1.0 - sig))).astype(jnp.bfloat16)
        dpre_ref[layer] = dpre
        mean = jnp.sum(dpre.astype(jnp.float32) * pre, axis=-1, keepdims=True) / D
        inner[...] = jnp.broadcast_to(mean, inner.shape)

    def down(layer, hidden_ref, upstream_ref, out_ref):
        base = ((layer ^ swap_ref[0]) * 2) * NBLK
        scale = scale_ref[layer][:, :1]
        mean = inner[:, :1]

        @pl.loop(0, D // CHUNK)
        def _(chunk):
            assemble_in(where_ref, weights_ref, dense_in, base, chunk)
            dnorm = dot(dpre_ref[layer], dense_in[...], NT)
            unit = hidden_ref[:, columns(chunk)].astype(jnp.float32) / scale
            out_ref[:, columns(chunk)] = (
                upstream_ref[:, columns(chunk)].astype(jnp.float32) + (dnorm - unit * mean) / scale
            ).astype(jnp.bfloat16)

    pl.when(step == 0)(lambda: up(1, grad_ref))
    pl.when(step == 1)(lambda: down(1, second_ref, grad_ref, middle_ref))
    pl.when(step == 2)(lambda: up(0, middle_ref))
    pl.when(step == 3)(lambda: down(0, first_ref, middle_ref, earlier_ref))


def gradient_kernel(
    swap_ref, places_ref, first_ref, second_ref, grad_ref, middle_ref, dpre_ref, act_ref, scale_ref, out_ref, dense, turned
):
    step = pl.program_id(0)
    owners, slots = out_ref.shape[0], out_ref.shape[3]
    dense[NBLK] = jnp.zeros((BLOCK, BLOCK), jnp.bfloat16)

    def pick(base):
        @pl.loop(0, owners)
        def _(owner):
            for slot in range(slots):
                out_ref[owner, 0, 0, slot] = dense[places_ref[base + owner * slots + slot]]

    def down(layer, hidden_ref):
        scale = scale_ref[layer][:, :1]

        @pl.loop(0, ROWS_D)
        def _(row):
            block = pl.ds(pl.multiple_of(row * BLOCK, BLOCK), BLOCK)
            normed = (hidden_ref[:, block].astype(jnp.float32) / scale).astype(jnp.bfloat16)
            part = dot(normed, dpre_ref[layer], TN).astype(jnp.bfloat16)
            for col in range(ROWS_K):
                dense[row * ROWS_K + col] = part[:, col * BLOCK : (col + 1) * BLOCK]

        pick(((layer ^ swap_ref[0]) * 2) * owners * slots)

    def up(layer, upstream_ref):
        turned[...] = act_ref[layer].astype(jnp.float32).T.astype(jnp.bfloat16)

        @pl.loop(0, ROWS_D // 2)
        def _(pair):
            block = pl.ds(pl.multiple_of(pair * 2 * BLOCK, 2 * BLOCK), 2 * BLOCK)
            part = dot(turned[...], upstream_ref[:, block], NN).astype(jnp.bfloat16)
            for row in range(ROWS_K):
                for col in range(2):
                    dense[row * ROWS_D + pair * 2 + col] = part[
                        row * BLOCK : (row + 1) * BLOCK, col * BLOCK : (col + 1) * BLOCK
                    ]

        pick(((layer ^ swap_ref[0]) * 2 + 1) * owners * slots)

    pl.when(step == 0)(lambda: up(1, grad_ref))
    pl.when(step == 1)(lambda: down(1, second_ref))
    pl.when(step == 2)(lambda: up(0, middle_ref))
    pl.when(step == 3)(lambda: down(0, first_ref))


def whole(*shape):
    return pl.BlockSpec(shape, lambda step, *_: (0,) * len(shape))


def params(flops, moved):
    return dict(
        compiler_params=pltpu.CompilerParams(
            dimension_semantics=("arbitrary",), vmem_limit_bytes=56 * 1024 * 1024
        ),
        cost_estimate=pl.CostEstimate(flops=flops, bytes_accessed=moved, transcendentals=0),
    )


def per_device(tokens, blocks_in, blocks_out, pos_in, pos_out, cotangent):
    here = lax.axis_index("section")
    owners = lax.axis_size("dp")
    slots = blocks_in.shape[1]
    rows = tokens.shape[0] // 2
    swap = (here % 2).astype(jnp.int32).reshape(1)
    upper = here >= 2
    half = jnp.where((here == 1) | (here == 2), rows, 0)

    own = jnp.stack([blocks_in[0], blocks_out[0]])
    both = jnp.stack([own, lax.ppermute(own, "section", PAIR)])
    weights = lax.all_gather(both, "dp", axis=0)
    own_places = jnp.stack([pos_in[0], pos_out[0]])
    both_places = jnp.stack([own_places, lax.ppermute(own_places, "section", PAIR)])
    places = lax.all_gather(both_places, "dp", axis=0).transpose(1, 2, 0, 3)
    codes = jnp.arange(owners, dtype=jnp.int32)[:, None] * 8 + jnp.arange(slots, dtype=jnp.int32)
    named = places[..., None] == jnp.arange(NBLK, dtype=jnp.int32)
    where = jnp.max(jnp.where(named, codes[..., None], -1), axis=(2, 3)).reshape(-1)
    places = places.reshape(-1)

    first_tokens = lax.dynamic_slice_in_dim(tokens, half, rows, 0)
    last_grads = lax.dynamic_slice_in_dim(cotangent, half, rows, 0)

    wide = jax.ShapeDtypeStruct((rows, D), jnp.bfloat16)
    narrow = jax.ShapeDtypeStruct((2, rows, RANK), jnp.bfloat16)
    narrow32 = jax.ShapeDtypeStruct((2, rows, RANK), jnp.float32)
    lane32 = jax.ShapeDtypeStruct((2, rows, BLOCK), jnp.float32)
    piece = (owners, 1, 1, slots, BLOCK, BLOCK)
    moved = weights.size * 2
    dense = [pltpu.VMEM((CHUNK, RANK), jnp.bfloat16), pltpu.VMEM((RANK, CHUNK), jnp.bfloat16)]

    forward = pl.pallas_call(
        forward_kernel,
        out_shape=(wide, wide, narrow32, narrow, lane32),
        grid_spec=pltpu.PrefetchScalarGridSpec(
            num_scalar_prefetch=2,
            grid=(4,),
            in_specs=[
                whole(rows, D),
                pl.BlockSpec(piece, lambda step, swap, _: (0, (step // 2) ^ swap[0], step % 2, 0, 0, 0)),
            ],
            out_specs=[
                whole(rows, D),
                whole(rows, D),
                whole(2, rows, RANK),
                whole(2, rows, RANK),
                whole(2, rows, BLOCK),
            ],
            scratch_shapes=dense,
        ),
        name="forward_layers",
        **params(8 * rows * D * RANK, moved),
    )
    backward = pl.pallas_call(
        backward_kernel,
        out_shape=(wide, wide, narrow),
        grid_spec=pltpu.PrefetchScalarGridSpec(
            num_scalar_prefetch=2,
            grid=(4,),
            in_specs=[
                whole(rows, D),
                whole(rows, D),
                whole(rows, D),
                whole(2, rows, RANK),
                whole(2, rows, BLOCK),
                pl.BlockSpec(
                    piece, lambda step, swap, _: (0, (1 - step // 2) ^ swap[0], 1 - step % 2, 0, 0, 0)
                ),
            ],
            out_specs=[whole(rows, D), whole(rows, D), whole(2, rows, RANK)],
            scratch_shapes=[
                pltpu.VMEM((rows, RANK), jnp.float32),
                pltpu.VMEM((rows, BLOCK), jnp.float32),
            ]
            + dense,
        ),
        name="backward_layers",
        **params(8 * rows * D * RANK, moved),
    )
    gradient = pl.pallas_call(
        gradient_kernel,
        out_shape=jax.ShapeDtypeStruct(weights.shape, jnp.bfloat16),
        grid_spec=pltpu.PrefetchScalarGridSpec(
            num_scalar_prefetch=2,
            grid=(4,),
            in_specs=[
                whole(rows, D),
                whole(rows, D),
                whole(rows, D),
                whole(rows, D),
                whole(2, rows, RANK),
                whole(2, rows, RANK),
                whole(2, rows, BLOCK),
            ],
            out_specs=pl.BlockSpec(
                piece, lambda step, swap, _: (0, (1 - step // 2) ^ swap[0], 1 - step % 2, 0, 0, 0)
            ),
            scratch_shapes=[
                pltpu.VMEM((NBLK + 1, BLOCK, BLOCK), jnp.bfloat16),
                pltpu.VMEM((RANK, rows), jnp.bfloat16),
            ],
        ),
        name="slot_gradients",
        **params(8 * rows * D * RANK, moved),
    )

    _, leaving, _, _, _ = forward(swap, where, first_tokens, weights)
    arrived = lax.ppermute(leaving, "section", UP)
    first = jnp.where(upper, arrived, first_tokens)
    second, _, pre, act, scale = forward(swap, where, first, weights)
    _, leaving, _ = backward(swap, where, first, second, last_grads, pre, scale, weights)
    arrived = lax.ppermute(leaving, "section", DOWN)
    grads = jnp.where(upper, last_grads, arrived)
    middle, _, dpre = backward(swap, where, first, second, grads, pre, scale, weights)
    partial = gradient(swap, places, first, second, grads, middle, dpre, act, scale)
    summed = lax.psum_scatter(partial, "dp", scatter_dimension=0, tiled=False)
    own_sum, other_sum = summed[0], summed[1]
    result = own_sum.astype(jnp.float32) + lax.ppermute(other_sum, "section", PAIR).astype(jnp.float32)
    result = result.astype(jnp.bfloat16)
    return (result[0][None], result[1][None])


def solution(mesh):
    in_specs = (
        P("dp", None),
        P("section", "dp", None, None),
        P("section", "dp", None, None),
        P("section", "dp"),
        P("section", "dp"),
        P("dp", None),
    )
    out_specs = (P("section", "dp", None, None), P("section", "dp", None, None))
    return jax.shard_map(
        per_device, mesh=mesh, in_specs=in_specs, out_specs=out_specs, check_vma=False
    )
```

time: 741 us -> 458 us (0.62); the launches traced: 732 us -> 458 us
  local copies, waits for them, and re-layouts: 182 us -> 8.61 us
  Pallas kernels: 0 us -> 151 us
  waiting for transfers between devices: 378 us -> 243 us
  matrix products: 60.1 us -> 0 us
  other arithmetic: 40.5 us -> 4.67 us
  starting transfers between devices: 36 us -> 11 us
  blocking collectives: 18.3 us -> 25.9 us
    ppermute x8 -> x5, waiting for transfers between devices: 216 us -> 62.2 us  [the longest x1 25.7 us: per_device(): arrived = lax.ppermute(leaving, 'section', DOWN)]
    pallas_call x0 -> x5, Pallas kernels: none -> 151 us  [the longest x1 57.9 us: per_device(): gradient(swap, places, first, second, grads, middle, dpre, act, scale)]
    dot_general x9 -> x0, matrix products: 60.1 us -> none  [the longest x2 21.7 us: forward_layer(): jnp.dot(act, mat_b, preferred_element_type=jnp.float32)]
    scatter x2 -> x0, local copies, waits for them, and re-layouts: 48.7 us -> none  [expand(): flat = flat.at[places].set(blocks, mode='drop')]
    reshape x1, local copies, waits for them, and re-layouts: 39.6 us -> 0.79 us  [per_device(): places = places.reshape(-1)]
    gather x4 -> x0, local copies, waits for them, and re-layouts: 34 us -> none  [the longest x2 17 us: slot_grads(): jnp.take(left.reshape(count, rows_b, BLOCK), row_block, axis=1)]
    select_n x27 -> x2, other arithmetic: 36.2 us -> 2.46 us  [the longest x1 1.25 us: per_device(): grads = jnp.where(upper, last_grads, arrived)]
    all_gather x0 -> x1, blocking collectives: none -> 25.9 us  [per_device(): places = lax.all_gather(both_places, 'dp', axis=0).transpose(1, 2, 0, 3)]
  transfers between devices with their start and end apart: 12 -> 7, of which waited for: 12 -> 7; matrix products, arithmetic and copies ran while one was open for 13% -> 1% of each run, Pallas kernels for 0% -> 0%
where the time goes in v1:
time: 458 us
  waiting for transfers between devices  243 us (53%)
  Pallas kernels  151 us (33%)
  blocking collectives  25.9 us (6%)
  between operations  14.1 us (3%)
  starting transfers between devices  11 us (2%)
  local copies, waits for them, and re-layouts  8.61 us (2%)
  other arithmetic  4.67 us (1%)
    reduce_scatter x1, waiting for transfers between devices, per_device(): summed = lax.psum_scatter(partial, 'dp', scatter_dimension=0, tiled=False)  125 us
    pallas_call x1, Pallas kernels, per_device(): gradient(swap, places, first, second, grads, middle, dpre, act, scale)  57.9 us
    all_gather x1, waiting for transfers between devices, per_device(): weights = lax.all_gather(both, 'dp', axis=0)  54.8 us
    all_gather x1, blocking collectives, per_device(): places = lax.all_gather(both_places, 'dp', axis=0).transpose(1, 2, 0, 3)  25.9 us
    ppermute x1, waiting for transfers between devices, per_device(): arrived = lax.ppermute(leaving, 'section', DOWN)  25.7 us
    pallas_call x1, Pallas kernels, per_device(): _, leaving, _, _, _ = forward(swap, where, first_tokens, weights)  23.6 us
    pallas_call x1, Pallas kernels, per_device(): second, _, pre, act, scale = forward(swap, where, first, weights)  23.6 us
    pallas_call x1, Pallas kernels, per_device(): backward(swap, where, first, second, last_grads, pre, scale, weights)  22.9 us
  transfers between devices with their start and end apart: 7, of which 7 were waited for; matrix products, arithmetic and copies ran while one was open for 1% of the time, Pallas kernels for 0%

profile of v1, /device:TPU:0, one launch (start us, length us, event | category | flops | bytes accessed | tf_op | source)
XLA Modules:
  0.0 457.6 jit_solution(8516730445042907280)
XLA Ops:
  7.2 1.1 constant_dynamic-update-slice_fusion.1
  8.3 0.9 constant_dynamic-update-slice_fusion
  9.3 1.7 collective-permute-start.1
  10.9 7.7 %collective-permute-done.1 = bf16[2,5,128,128]{3,2,1,0:T(8,128)(2,1)S(1)} collective-permute-done((bf16[2,5,128,128]{3,2,1,0:T(8,128)(2,1)S(1)}, bf16[2,5,128,128]{3,2,1,0:T(8,128)(2,1)S(1)}, u32[]{:S(2)}, u32[]{:S(2)}) %collective-permute-start.1) | collective-permute-done | bytes 327712 | tf_op jit(solution)/shard_map/ppermute | solution.py:211
  18.6 0.9 pad_maximum_fusion
  19.7 1.8 collective-permute-start
  21.5 1.0 constant_dynamic-slice_fusion.1.first_ref
  22.5 0.8 collective-permute-done
  23.3 25.9 %all-gather = s32[64,2,5]{2,1,0:T(2,128)S(1)} all-gather(s32[2,2,5]{2,1,0:T(2,128)S(1)} %pad_add_fusion), channel_id=2, replica_groups=mesh['section'=4,'dp'=32] {'dp'}, dimensions={0}, use_global_device_ids=true | all-gather | bytes 2640 | tf_op jit(solution)/shard_map/all_gather | solution.py:215
  49.2 0.1 copy.13
  49.3 0.2 select_reduce_fusion
  49.5 0.6 copy.14
  50.1 54.8 %all-gather.4.cloned.1.call-done = bf16[64,2,5,128,128]{4,3,2,1,0:T(8,128)(2,1)} async-done(((bf16[2,2,5,128,128]{4,3,2,1,0:T(8,128)(2,1)}), bf16[64,2,5,128,128]{4,3,2,1,0:T(8,128)(2,1)}) %all-gather.4.cloned.1.call-update) | async-done | bytes 20971536 | tf_op jit(solution)/shard_map/all_gather | solution.py:212
  105.0 23.6 %forward_layers.2 = (bf16[64,8192]{1,0:T(8,128)(2,1)}, bf16[64,8192]{1,0:T(8,128)(2,1)}, f32[2,64,512]{2,1,0:T(8,128)}, bf16[2,64,512]{2,1,0:T(8,128)(2,1)}, f32[2,64,128]{2,1,0:T(8,128)}) custom-call(s32[1]{0:T(128)} %bitcast.swap_ref, s32[1024]{0:T(1024)} %bitcast.32, bf16[64,8192]{1,0:T(8,128)(2,1)} %constant_dynamic-slice_fusion.1.first_ref, ...), custom_call_target="tpu_custom_call" | custom-call | flops 2147483648 | bytes 20971520 | tf_op jit(solution)/shard_map/forward_layers/pallas_call | solution.py:307
  128.6 4.6 %collective-permute-start.2 = (bf16[64,8192]{1,0:T(8,128)(2,1)}, bf16[64,8192]{1,0:T(8,128)(2,1)S(1)}, u32[]{:S(2)}, u32[]{:S(2)}) collective-permute-start(bf16[64,8192]{1,0:T(8,128)(2,1)} %get-tuple-element.10), channel_id=1, source_target_pairs={{0,96},{32,64},{1,97},{33,65},{2,98},{34,66},{3,99},{35,67},{4,100... | collective-permute-start | bytes 3145736 | tf_op jit(solution)/shard_map/ppermute | solution.py:308
  133.2 2.3 constant_dynamic-slice_fusion.grad_ref
  135.5 20.8 %collective-permute-done.2 = bf16[64,8192]{1,0:T(8,128)(2,1)S(1)} collective-permute-done((bf16[64,8192]{1,0:T(8,128)(2,1)}, bf16[64,8192]{1,0:T(8,128)(2,1)S(1)}, u32[]{:S(2)}, u32[]{:S(2)}) %collective-permute-start.2) | collective-permute-done | bytes 1048608 | tf_op jit(solution)/shard_map/ppermute | solution.py:308
  156.3 1.2 broadcast_select_fusion.1.first_ref
  157.5 23.6 %forward_layers.3 = (bf16[64,8192]{1,0:T(8,128)(2,1)}, bf16[64,8192]{1,0:T(8,128)(2,1)}, f32[2,64,512]{2,1,0:T(8,128)}, bf16[2,64,512]{2,1,0:T(8,128)(2,1)}, f32[2,64,128]{2,1,0:T(8,128)}) custom-call(s32[1]{0:T(128)} %bitcast.swap_ref, s32[1024]{0:T(1024)} %bitcast.33, bf16[64,8192]{1,0:T(8,128)(2,1)} %broadcast_select_fusion.1.first_ref, ...), custom_call_target="tpu_custom_call" | custom-call | flops 2147483648 | bytes 20971520 | tf_op jit(solution)/shard_map/forward_layers/pallas_call | solution.py:310
  181.1 22.9 %backward_layers.2 = (bf16[64,8192]{1,0:T(8,128)(2,1)}, bf16[64,8192]{1,0:T(8,128)(2,1)}, bf16[2,64,512]{2,1,0:T(8,128)(2,1)}) custom-call(s32[1]{0:T(128)} %bitcast.swap_ref, s32[1024]{0:T(1024)} %bitcast.34, bf16[64,8192]{1,0:T(8,128)(2,1)} %broadcast_select_fusion.1.first_ref, bf16[64,8192]{1,0:T(8,128)(2,1)} %get-tuple-element.11.second_ref, ...), custom_call_target="tpu_custom_call" | custom-call | flops 2147483648 | bytes 20971520 | tf_op jit(solution)/shard_map/backward_layers/pallas_call | solution.py:311
  204.0 1.3 collective-permute-start.3
  205.3 0.8 reshape.26.places_ref
  206.1 25.7 %collective-permute-done.3 = bf16[64,8192]{1,0:T(8,128)(2,1)S(1)} collective-permute-done((bf16[64,8192]{1,0:T(8,128)(2,1)}, bf16[64,8192]{1,0:T(8,128)(2,1)S(1)}, u32[]{:S(2)}, u32[]{:S(2)}) %collective-permute-start.3) | collective-permute-done | bytes 1048608 | tf_op jit(solution)/shard_map/ppermute | solution.py:312
  231.9 1.2 broadcast_select_fusion.grad_ref
  233.1 22.7 %backward_layers.3 = (bf16[64,8192]{1,0:T(8,128)(2,1)}, bf16[64,8192]{1,0:T(8,128)(2,1)}, bf16[2,64,512]{2,1,0:T(8,128)(2,1)}) custom-call(s32[1]{0:T(128)} %bitcast.swap_ref, s32[1024]{0:T(1024)} %bitcast.35, bf16[64,8192]{1,0:T(8,128)(2,1)} %broadcast_select_fusion.1.first_ref, bf16[64,8192]{1,0:T(8,128)(2,1)} %get-tuple-element.11.second_ref, ...), custom_call_target="tpu_custom_call" | custom-call | flops 2147483648 | bytes 20971520 | tf_op jit(solution)/shard_map/backward_layers/pallas_call | solution.py:314
  255.8 57.9 %slot_gradients.1 = bf16[32,2,2,5,128,128]{5,4,3,2,1,0:T(8,128)(2,1)} custom-call(s32[1]{0:T(128)} %bitcast.swap_ref, s32[640]{0:T(1024)} %reshape.26.places_ref, bf16[64,8192]{1,0:T(8,128)(2,1)} %broadcast_select_fusion.1.first_ref, bf16[64,8192]{1,0:T(8,128)(2,1)} %get-tuple-element.11.second_ref, bf16[64,8192]{1,0:T(8,128)(2,1)} %broadcast_select_fusion.grad_ref, ...), custom_call_target="tpu_custom_call" | custom-call | flops 2147483648 | bytes 20971520 | tf_op jit(solution)/shard_map/slot_gradients/pallas_call | solution.py:315
  313.7 125.5 %reduce-scatter.2.cloned.1.call-done = bf16[1,2,2,5,128,128]{5,4,3,2,1,0:T(8,128)(2,1)} async-done(((bf16[32,2,2,5,128,128]{5,4,3,2,1,0:T(8,128)(2,1)}), bf16[1,2,2,5,128,128]{5,4,3,2,1,0:T(8,128)(2,1)}) %reduce-scatter.2.cloned.1.call-update) | async-done | bytes 655376 | tf_op jit(solution)/shard_map/reduce_scatter | solution.py:316
  439.2 1.0 slice_bitcast_fusion
  440.2 1.5 collective-permute-start.4
  441.7 7.2 %collective-permute-done.4 = bf16[2,5,128,128]{3,2,1,0:T(8,128)(2,1)S(1)} collective-permute-done((bf16[2,5,128,128]{3,2,1,0:T(8,128)(2,1)S(1)}, bf16[2,5,128,128]{3,2,1,0:T(8,128)(2,1)S(1)}, u32[]{:S(2)}, u32[]{:S(2)}) %collective-permute-start.4) | collective-permute-done | bytes 327712 | tf_op jit(solution)/shard_map/ppermute | solution.py:318
  448.9 1.1 fusion
  450.0 0.7 fusion.2
  (17 shorter events, 0.2 us)
Async XLA Ops:
  7.2 12.5 %copy-start.2 = (s32[1,5]{1,0:T(1,128)S(1)}, s32[1,5]{1,0:T(1,128)}, u32[]{:S(2)}) copy-start(s32[1,5]{1,0:T(1,128)} %param.10) | copy-start | bytes 64
  7.2 12.5 %copy-start.3 = (s32[1,5]{1,0:T(1,128)S(1)}, s32[1,5]{1,0:T(1,128)}, u32[]{:S(2)}) copy-start(s32[1,5]{1,0:T(1,128)} %param.9) | copy-start | bytes 64
  7.2 14.3 %copy-start = (bf16[128,8192]{1,0:T(8,128)(2,1)S(1)}, bf16[128,8192]{1,0:T(8,128)(2,1)}, u32[]{:S(2)}) copy-start(bf16[128,8192]{1,0:T(8,128)(2,1)} %param.6) | copy-start | bytes 6291460
  7.2 97.8 %all-gather.4.cloned.1.call-start = ((), (), s32[]{:S(2)}) async-start(), calls=%async_computation.2 | async-start | bytes 21626880 | tf_op jit(solution)/shard_map/all_gather | solution.py:212
  9.3 9.4 %collective-permute-start.1 = (bf16[2,5,128,128]{3,2,1,0:T(8,128)(2,1)S(1)}, bf16[2,5,128,128]{3,2,1,0:T(8,128)(2,1)S(1)}, u32[]{:S(2)}, u32[]{:S(2)}) collective-permute-start(bf16[2,5,128,128]{3,2,1,0:T(8,128)(2,1)S(1)} %constant_dynamic-update-slice_fusion), channel_id=1, source_target_pairs={{0,32},{32,0},{64,96},{96,64},{1,33},{33,1},{65,97},{97,65},{2,34}... | collective-permute-start | bytes 983048 | tf_op jit(solution)/shard_map/ppermute | solution.py:211
  19.6 419.6 %reduce-scatter.2.cloned.1.call-start = ((), (), s32[]{:S(2)}) async-start(), calls=%async_computation.1 | async-start | bytes 21626880 | tf_op jit(solution)/shard_map/reduce_scatter | solution.py:316
  19.7 3.6 collective-permute-start
  128.6 27.7 %collective-permute-start.2 = (bf16[64,8192]{1,0:T(8,128)(2,1)}, bf16[64,8192]{1,0:T(8,128)(2,1)S(1)}, u32[]{:S(2)}, u32[]{:S(2)}) collective-permute-start(bf16[64,8192]{1,0:T(8,128)(2,1)} %get-tuple-element.10), channel_id=1, source_target_pairs={{0,96},{32,64},{1,97},{33,65},{2,98},{34,66},{3,99},{35,67},{4,100... | collective-permute-start | bytes 3145736 | tf_op jit(solution)/shard_map/ppermute | solution.py:308
  181.1 50.8 %copy-start.1 = (bf16[128,8192]{1,0:T(8,128)(2,1)S(1)}, bf16[128,8192]{1,0:T(8,128)(2,1)}, u32[]{:S(2)}) copy-start(bf16[128,8192]{1,0:T(8,128)(2,1)} %param.11) | copy-start | bytes 6291460
  204.0 27.8 %collective-permute-start.3 = (bf16[64,8192]{1,0:T(8,128)(2,1)}, bf16[64,8192]{1,0:T(8,128)(2,1)S(1)}, u32[]{:S(2)}, u32[]{:S(2)}) collective-permute-start(bf16[64,8192]{1,0:T(8,128)(2,1)} %get-tuple-element.14), channel_id=1, source_target_pairs={{96,0},{64,32},{97,1},{65,33},{98,2},{66,34},{99,3},{67,35},{100,4... | collective-permute-start | bytes 3145736 | tf_op jit(solution)/shard_map/ppermute | solution.py:312
  440.2 8.7 %collective-permute-start.4 = (bf16[2,5,128,128]{3,2,1,0:T(8,128)(2,1)S(1)}, bf16[2,5,128,128]{3,2,1,0:T(8,128)(2,1)S(1)}, u32[]{:S(2)}, u32[]{:S(2)}) collective-permute-start(bf16[2,5,128,128]{3,2,1,0:T(8,128)(2,1)S(1)} %slice_bitcast_fusion), channel_id=1, source_target_pairs={{0,32},{32,0},{64,96},{96,64},{1,33},{33,1},{65,97},{97,65},{2,34}... | collective-permute-start | bytes 983048 | tf_op jit(solution)/shard_map/ppermute | solution.py:318
Sparse Core Ops, SparseCore 0:
  19.7 85.2 all-gather.3
  313.8 125.3 reduce-scatter.1

commit v2 on v1

v2 whole, which is shorter than its diff:
```python
import functools

import jax
import jax.numpy as jnp
from jax import lax
from jax.experimental import pallas as pl
from jax.experimental.pallas import tpu as pltpu
from jax.sharding import PartitionSpec as P

D = 8192
RANK = 512
BLOCK = 128
ROWS_D = D // BLOCK
ROWS_K = RANK // BLOCK
NBLK = ROWS_D * ROWS_K
EPS = 1e-05
CHUNK = 1024
BLOCKS = CHUNK // BLOCK
SPAN = 512
NT = (((1,), (1,)), ((), ()))
NN = (((1,), (0,)), ((), ()))
TN = (((0,), (0,)), ((), ()))
PAIR = [(0, 1), (1, 0), (2, 3), (3, 2)]
UP = [(0, 3), (1, 2)]
DOWN = [(3, 0), (2, 1)]


def dot(left, right, dims):
    return lax.dot_general(left, right, dims, preferred_element_type=jnp.float32)


def fetch(where_ref, weights_ref, number):
    code = where_ref[number]
    safe = jnp.maximum(code, 0)
    block = weights_ref[safe >> 3, 0, 0, safe & 7]
    return lax.select(code >= 0, block, jnp.zeros_like(block))


def rows_in(where_ref, weights_ref, base, row, count):
    return jnp.concatenate(
        [
            jnp.concatenate(
                [fetch(where_ref, weights_ref, base + (row + i) * ROWS_K + col) for col in range(ROWS_K)], axis=1
            )
            for i in range(count)
        ],
        axis=0,
    )


def columns_out(where_ref, weights_ref, base, col, count):
    return jnp.concatenate(
        [
            jnp.concatenate(
                [fetch(where_ref, weights_ref, base + row * ROWS_D + col + i) for i in range(count)], axis=1
            )
            for row in range(ROWS_K)
        ],
        axis=0,
    )


def columns(chunk, width=CHUNK):
    return pl.ds(pl.multiple_of(chunk * width, width), width)


def root(hidden_ref):
    def step(chunk, total):
        wide = hidden_ref[:, columns(chunk)].astype(jnp.float32)
        return total + jnp.sum(wide * wide, axis=-1, keepdims=True)

    total = lax.fori_loop(0, D // CHUNK, step, jnp.zeros((hidden_ref.shape[0], 1), jnp.float32))
    return jnp.sqrt(total / D + EPS)


def forward_kernel(
    swap_ref, where_ref, first_ref, weights_ref, second_ref, last_ref, pre_ref, scale_ref, normed_ref, act_ref
):
    step = pl.program_id(0)

    def down(layer, hidden_ref):
        place = layer ^ swap_ref[0]
        base = place * 2 * NBLK
        scale = root(hidden_ref)
        scale_ref[layer] = jnp.broadcast_to(scale, scale_ref.shape[1:])
        pre_ref[layer] = jnp.zeros(pre_ref.shape[1:], jnp.float32)

        @pl.loop(0, D // CHUNK)
        def _(chunk):
            normed = (hidden_ref[:, columns(chunk)].astype(jnp.float32) / scale).astype(jnp.bfloat16)
            normed_ref[place, :, columns(chunk)] = normed
            dense = rows_in(where_ref, weights_ref, base, chunk * BLOCKS, BLOCKS)
            pre_ref[layer] += dot(normed, dense, NN)

    def up(layer, hidden_ref, next_ref):
        place = layer ^ swap_ref[0]
        base = (place * 2 + 1) * NBLK
        pre = pre_ref[layer]
        act_ref[place] = (pre * jax.nn.sigmoid(pre)).astype(jnp.bfloat16)

        @pl.loop(0, D // CHUNK)
        def _(chunk):
            dense = columns_out(where_ref, weights_ref, base, chunk * BLOCKS, BLOCKS)
            moved = dot(act_ref[place], dense, NN)
            next_ref[:, columns(chunk)] = (hidden_ref[:, columns(chunk)].astype(jnp.float32) + moved).astype(jnp.bfloat16)

    pl.when(step == 0)(lambda: down(0, first_ref))
    pl.when(step == 1)(lambda: up(0, first_ref, second_ref))
    pl.when(step == 2)(lambda: down(1, second_ref))
    pl.when(step == 3)(lambda: up(1, second_ref, last_ref))


def backward_kernel(
    layer, swap_ref, where_ref, hidden_ref, upstream_ref, pre_ref, scale_ref, weights_ref, earlier_ref, dpre_ref, total, inner
):
    step = pl.program_id(0)
    place = layer ^ swap_ref[0]

    @pl.when(step == 0)
    def _():
        base = (place * 2 + 1) * NBLK
        total[...] = jnp.zeros(total.shape, jnp.float32)

        @pl.loop(0, D // CHUNK)
        def _(chunk):
            dense = columns_out(where_ref, weights_ref, base, chunk * BLOCKS, BLOCKS)
            total[...] += dot(upstream_ref[:, columns(chunk)], dense, NT)

        pre = pre_ref[layer]
        sig = jax.nn.sigmoid(pre)
        dpre = (total[...] * sig * (1.0 + pre * (1.0 - sig))).astype(jnp.bfloat16)
        dpre_ref[...] = dpre
        mean = jnp.sum(dpre.astype(jnp.float32) * pre, axis=-1, keepdims=True) / D
        inner[...] = jnp.broadcast_to(mean, inner.shape)

    @pl.when(step == 1)
    def _():
        base = place * 2 * NBLK
        scale = scale_ref[layer][:, :1]
        mean = inner[:, :1]

        @pl.loop(0, D // CHUNK)
        def _(chunk):
            dense = rows_in(where_ref, weights_ref, base, chunk * BLOCKS, BLOCKS)
            dnorm = dot(dpre_ref[...], dense, NT)
            unit = hidden_ref[:, columns(chunk)].astype(jnp.float32) / scale
            earlier_ref[:, columns(chunk)] = (
                upstream_ref[:, columns(chunk)].astype(jnp.float32) + (dnorm - unit * mean) / scale
            ).astype(jnp.bfloat16)


def pick(places_ref, dense, out_ref, base):
    owners, slots = out_ref.shape[0], out_ref.shape[2]

    @pl.loop(0, owners)
    def _(owner):
        for slot in range(slots):
            out_ref[owner, 0, slot] = dense[places_ref[base + owner * slots + slot]]


def gradient_in_kernel(places_ref, own_ref, other_ref, dpre_own_ref, dpre_other_ref, out_ref, dense):
    step = pl.program_id(0)

    @pl.when(step == 0)
    def _():
        dense[NBLK] = jnp.zeros((BLOCK, BLOCK), jnp.bfloat16)

        @pl.loop(0, D // SPAN)
        def _(chunk):
            normed = jnp.concatenate([own_ref[:, columns(chunk, SPAN)], other_ref[:, columns(chunk, SPAN)]], axis=0)
            dpre = jnp.concatenate([dpre_own_ref[...], dpre_other_ref[...]], axis=0)
            part = dot(normed, dpre, TN).astype(jnp.bfloat16)
            for row in range(SPAN // BLOCK):
                for col in range(ROWS_K):
                    dense[(chunk * (SPAN // BLOCK) + row) * ROWS_K + col] = part[
                        row * BLOCK : (row + 1) * BLOCK, col * BLOCK : (col + 1) * BLOCK
                    ]

    pick(places_ref, dense, out_ref, step * out_ref.shape[0] * out_ref.shape[2])


def gradient_out_kernel(places_ref, _, act_own_ref, act_other_ref, own_ref, other_ref, out_ref, dense, turned):
    step = pl.program_id(0)

    @pl.when(step == 0)
    def _():
        dense[NBLK] = jnp.zeros((BLOCK, BLOCK), jnp.bfloat16)
        act = jnp.concatenate([act_own_ref[...], act_other_ref[...]], axis=0)
        turned[...] = act.astype(jnp.float32).T.astype(jnp.bfloat16)

        @pl.loop(0, D // SPAN)
        def _(chunk):
            upstream = jnp.concatenate([own_ref[:, columns(chunk, SPAN)], other_ref[:, columns(chunk, SPAN)]], axis=0)
            part = dot(turned[...], upstream, NN).astype(jnp.bfloat16)
            for row in range(ROWS_K):
                for col in range(SPAN // BLOCK):
                    dense[row * ROWS_D + chunk * (SPAN // BLOCK) + col] = part[
                        row * BLOCK : (row + 1) * BLOCK, col * BLOCK : (col + 1) * BLOCK
                    ]

    pick(places_ref, dense, out_ref, (places_ref.shape[0] // 2) + step * out_ref.shape[0] * out_ref.shape[2])


def whole(*shape):
    return pl.BlockSpec(shape, lambda step, *_: (0,) * len(shape))


def params(flops, moved):
    return dict(
        compiler_params=pltpu.CompilerParams(
            dimension_semantics=("arbitrary",), vmem_limit_bytes=56 * 1024 * 1024
        ),
        cost_estimate=pl.CostEstimate(flops=flops, bytes_accessed=moved, transcendentals=0),
    )


def swapped(array):
    return lax.ppermute(array, "section", PAIR)


def per_device(tokens, blocks_in, blocks_out, pos_in, pos_out, cotangent):
    here = lax.axis_index("section")
    owners = lax.axis_size("dp")
    slots = blocks_in.shape[1]
    rows = tokens.shape[0] // 2
    odd = here % 2
    swap = odd.astype(jnp.int32).reshape(1)
    upper = here >= 2
    half = jnp.where((here == 1) | (here == 2), rows, 0)

    own = jnp.stack([blocks_in[0], blocks_out[0]])
    weights = lax.all_gather(jnp.stack([own, swapped(own)]), "dp", axis=0)
    own_places = jnp.stack([pos_in[0], pos_out[0]])
    places = lax.all_gather(jnp.stack([own_places, swapped(own_places)]), "dp", axis=0).transpose(1, 2, 0, 3)
    codes = jnp.arange(owners, dtype=jnp.int32)[:, None] * 8 + jnp.arange(slots, dtype=jnp.int32)
    named = places[..., None] == jnp.arange(NBLK, dtype=jnp.int32)
    where = jnp.max(jnp.where(named, codes[..., None], -1), axis=(2, 3)).reshape(-1)
    places = places[0].reshape(-1)

    first_tokens = lax.dynamic_slice_in_dim(tokens, half, rows, 0)
    last_grads = lax.dynamic_slice_in_dim(cotangent, half, rows, 0)

    def shape(*dims, dtype=jnp.bfloat16):
        return jax.ShapeDtypeStruct(dims, dtype)

    piece = (owners, 1, 1, slots, BLOCK, BLOCK)
    moved = weights.size * 2
    work = 2 * rows * D * RANK

    forward = pl.pallas_call(
        forward_kernel,
        out_shape=(
            shape(rows, D),
            shape(rows, D),
            shape(2, rows, RANK, dtype=jnp.float32),
            shape(2, rows, BLOCK, dtype=jnp.float32),
            shape(2, rows, D),
            shape(2, rows, RANK),
        ),
        grid_spec=pltpu.PrefetchScalarGridSpec(
            num_scalar_prefetch=2,
            grid=(4,),
            in_specs=[
                whole(rows, D),
                pl.BlockSpec(piece, lambda step, swap, _: (0, (step // 2) ^ swap[0], step % 2, 0, 0, 0)),
            ],
            out_specs=[
                whole(rows, D),
                whole(rows, D),
                whole(2, rows, RANK),
                whole(2, rows, BLOCK),
                whole(2, rows, D),
                whole(2, rows, RANK),
            ],
        ),
        name="forward_layers",
        **params(4 * work, moved),
    )

    def backward(layer):
        return pl.pallas_call(
            functools.partial(backward_kernel, layer),
            out_shape=(shape(rows, D), shape(rows, RANK)),
            grid_spec=pltpu.PrefetchScalarGridSpec(
                num_scalar_prefetch=2,
                grid=(2,),
                in_specs=[
                    whole(rows, D),
                    whole(rows, D),
                    whole(2, rows, RANK),
                    whole(2, rows, BLOCK),
                    pl.BlockSpec(piece, lambda step, swap, _: (0, layer ^ swap[0], 1 - step, 0, 0, 0)),
                ],
                out_specs=[whole(rows, D), whole(rows, RANK)],
                scratch_shapes=[pltpu.VMEM((rows, RANK), jnp.float32), pltpu.VMEM((rows, BLOCK), jnp.float32)],
            ),
            name=f"backward_layer_{layer}",
            **params(2 * work, moved // 2),
        )

    steps = 4
    part = (owners // steps, 1, slots, BLOCK, BLOCK)
    partial_shape = shape(owners, 2, slots, BLOCK, BLOCK)
    dense = pltpu.VMEM((NBLK + 1, BLOCK, BLOCK), jnp.bfloat16)
    gradient_in = pl.pallas_call(
        gradient_in_kernel,
        out_shape=partial_shape,
        grid_spec=pltpu.PrefetchScalarGridSpec(
            num_scalar_prefetch=1,
            grid=(steps,),
            in_specs=[whole(rows, D), whole(rows, D), whole(rows, RANK), whole(rows, RANK)],
            out_specs=pl.BlockSpec(part, lambda step, _: (step, 0, 0, 0, 0)),
            scratch_shapes=[dense],
        ),
        name="gradient_in",
        **params(2 * work, moved // 4),
    )
    gradient_out = pl.pallas_call(
        gradient_out_kernel,
        out_shape=partial_shape,
        grid_spec=pltpu.PrefetchScalarGridSpec(
            num_scalar_prefetch=1,
            grid=(steps,),
            in_specs=[
                pl.BlockSpec(memory_space=pl.ANY),
                whole(rows, RANK),
                whole(rows, RANK),
                whole(rows, D),
                whole(rows, D),
            ],
            out_specs=pl.BlockSpec(part, lambda step, _: (step, 1, 0, 0, 0)),
            scratch_shapes=[dense, pltpu.VMEM((RANK, 2 * rows), jnp.bfloat16)],
        ),
        input_output_aliases={1: 0},
        name="gradient_out",
        **params(2 * work, moved // 4),
    )

    _, leaving, _, _, _, _ = forward(swap, where, first_tokens, weights)
    arrived = lax.ppermute(leaving, "section", UP)
    first = jnp.where(upper, arrived, first_tokens)
    second, _, pre, scale, normed, act = forward(swap, where, first, weights)
    normed_other = swapped(normed[1])
    act_other = swapped(act[1])

    middle, _ = backward(1)(swap, where, second, last_grads, pre, scale, weights)
    leaving, _ = backward(0)(swap, where, first, middle, pre, scale, weights)
    arrived = lax.ppermute(leaving, "section", DOWN)
    grads = jnp.where(upper, last_grads, arrived)
    middle, dpre_high = backward(1)(swap, where, second, grads, pre, scale, weights)
    grads_other = swapped(jnp.where(odd == 0, grads, middle))
    grads_own = jnp.where(odd == 0, middle, grads)
    _, dpre_low = backward(0)(swap, where, first, middle, pre, scale, weights)
    dpre_other = swapped(jnp.where(odd == 0, dpre_high, dpre_low))
    dpre_own = jnp.where(odd == 0, dpre_low, dpre_high)

    partial = gradient_in(places, normed[0], normed_other, dpre_own, dpre_other)
    partial = gradient_out(places, partial, act[0], act_other, grads_own, grads_other)
    summed = lax.psum_scatter(partial, "dp", scatter_dimension=0, tiled=False)
    return (summed[0][None], summed[1][None])


def solution(mesh):
    in_specs = (
        P("dp", None),
        P("section", "dp", None, None),
        P("section", "dp", None, None),
        P("section", "dp"),
        P("section", "dp"),
        P("dp", None),
    )
    out_specs = (P("section", "dp", None, None), P("section", "dp", None, None))
    return jax.shard_map(
        per_device, mesh=mesh, in_specs=in_specs, out_specs=out_specs, check_vma=False
    )
```

time: 458 us -> 398 us (0.87)
  Pallas kernels: 151 us -> 113 us
  waiting for transfers between devices: 243 us -> 214 us
    pallas_call x5 -> x8, Pallas kernels: 151 us -> 113 us  [the longest x1 21.4 us: per_device(): _, leaving, _, _, _, _ = forward(swap, where, first_tokens, weights)]
    reduce_scatter x1, waiting for transfers between devices: 125 us -> 95.2 us  [per_device(): summed = lax.psum_scatter(partial, 'dp', scatter_dimension=0, tiled=False)]
    ppermute x3 -> x6, waiting for transfers between devices: 15.7 us -> 16 us  [swapped(): return lax.ppermute(array, 'section', PAIR)]
  transfers between devices with their start and end apart: 7 -> 10, of which waited for: 7 -> 6; matrix products, arithmetic and copies ran while one was open for 1% -> 3% of each run, Pallas kernels for 0% -> 9%
where the time goes in v2:
time: 398 us; the launch traced here: 397 us
  waiting for transfers between devices  214 us (54%)
  Pallas kernels  113 us (28%)
  blocking collectives  25.7 us (6%)
  between operations  14.2 us (4%)
  starting transfers between devices  11.5 us (3%)
  local copies, waits for them, and re-layouts  11.3 us (3%)
  other arithmetic  7.31 us (2%)
    reduce_scatter x1, waiting for transfers between devices, per_device(): summed = lax.psum_scatter(partial, 'dp', scatter_dimension=0, tiled=False)  95.2 us
    all_gather x1, waiting for transfers between devices, per_device(): weights = lax.all_gather(jnp.stack([own, swapped(own)]), 'dp', axis=0)  54.2 us
    all_gather x1, blocking collectives, per_device(): lax.all_gather(jnp.stack([own_places, swapped(own_places)]), 'dp', axis=0)  25.7 us
    ppermute x1, waiting for transfers between devices, per_device(): arrived = lax.ppermute(leaving, 'section', DOWN)  25.2 us
    ppermute x1, waiting for transfers between devices, per_device(): arrived = lax.ppermute(leaving, 'section', UP)  23.1 us
    pallas_call x1, Pallas kernels, per_device(): _, leaving, _, _, _, _ = forward(swap, where, first_tokens, weights)  21.4 us
    pallas_call x1, Pallas kernels, per_device(): second, _, pre, scale, normed, act = forward(swap, where, first, weights)  19.8 us
    ppermute x6, waiting for transfers between devices, swapped(): return lax.ppermute(array, 'section', PAIR)  16 us
  transfers between devices with their start and end apart: 10, of which 6 were waited for; matrix products, arithmetic and copies ran while one was open for 3% of the time, Pallas kernels for 9%

profile of v2, /device:TPU:0, one launch (start us, length us, event | category | flops | bytes accessed | tf_op | source)
XLA Modules:
  0.0 397.0 jit_solution(5855510670673960346)
XLA Ops:
  7.2 1.1 constant_dynamic-update-slice_fusion.1
  8.3 0.9 constant_dynamic-update-slice_fusion
  9.3 1.7 collective-permute-start.1
  10.9 7.7 %collective-permute-done.1 = bf16[2,5,128,128]{3,2,1,0:T(8,128)(2,1)S(1)} collective-permute-done((bf16[2,5,128,128]{3,2,1,0:T(8,128)(2,1)S(1)}, bf16[2,5,128,128]{3,2,1,0:T(8,128)(2,1)S(1)}, u32[]{:S(2)}, u32[]{:S(2)}) %collective-permute-start.1) | collective-permute-done | bytes 327712 | tf_op jit(solution)/shard_map/ppermute | solution.py:218
  18.6 0.9 pad_maximum_fusion
  19.6 1.8 collective-permute-start
  21.5 2.7 constant_dynamic-slice_fusion
  24.1 25.7 %all-gather = s32[64,2,5]{2,1,0:T(2,128)S(1)} all-gather(s32[2,2,5]{2,1,0:T(2,128)S(1)} %pad_add_fusion), channel_id=2, replica_groups=mesh['section'=4,'dp'=32] {'dp'}, dimensions={0}, use_global_device_ids=true | all-gather | bytes 2640 | tf_op jit(solution)/shard_map/all_gather | solution.py:234
  50.7 54.2 %all-gather.4.cloned.1.call-done = bf16[64,2,5,128,128]{4,3,2,1,0:T(8,128)(2,1)} async-done(((bf16[2,2,5,128,128]{4,3,2,1,0:T(8,128)(2,1)}), bf16[64,2,5,128,128]{4,3,2,1,0:T(8,128)(2,1)}) %all-gather.4.cloned.1.call-update) | async-done | bytes 20971536 | tf_op jit(solution)/shard_map/all_gather | solution.py:232
  104.9 21.4 %forward_layers.2 = (bf16[64,8192]{1,0:T(8,128)(2,1)}, bf16[64,8192]{1,0:T(8,128)(2,1)}, f32[2,64,512]{2,1,0:T(8,128)}, f32[2,64,128]{2,1,0:T(8,128)}, bf16[2,64...) custom-call(s32[1]{0:T(128)} %bitcast.4.swap_ref, s32[1024]{0:T(1024)} %bitcast.38, ...), custom_call_target="tpu_custom_call" | custom-call | flops 2147483648 | bytes 20971520 | tf_op jit(solution)/shard_map/forward_layers/pallas_call | solution.py:339
  126.3 4.5 %collective-permute-start.2 = (bf16[64,8192]{1,0:T(8,128)(2,1)}, bf16[64,8192]{1,0:T(8,128)(2,1)S(1)}, u32[]{:S(2)}, u32[]{:S(2)}) collective-permute-start(bf16[64,8192]{1,0:T(8,128)(2,1)} %get-tuple-element.13), channel_id=1, source_target_pairs={{0,96},{32,64},{1,97},{33,65},{2,98},{34,66},{3,99},{35,67},{4,100... | collective-permute-start | bytes 3145736 | tf_op jit(solution)/shard_map/ppermute | solution.py:340
  130.8 23.1 %collective-permute-done.2 = bf16[64,8192]{1,0:T(8,128)(2,1)S(1)} collective-permute-done((bf16[64,8192]{1,0:T(8,128)(2,1)}, bf16[64,8192]{1,0:T(8,128)(2,1)S(1)}, u32[]{:S(2)}, u32[]{:S(2)}) %collective-permute-start.2) | collective-permute-done | bytes 1048608 | tf_op jit(solution)/shard_map/ppermute | solution.py:340
  153.9 1.1 broadcast_select_fusion.3.first_ref.hidden_ref
  155.0 19.8 %forward_layers.3 = (bf16[64,8192]{1,0:T(8,128)(2,1)}, bf16[64,8192]{1,0:T(8,128)(2,1)}, f32[2,64,512]{2,1,0:T(8,128)}, f32[2,64,128]{2,1,0:T(8,128)}, bf16[2,64...) custom-call(s32[1]{0:T(128)} %bitcast.4.swap_ref, s32[1024]{0:T(1024)} %bitcast.39, ...), custom_call_target="tpu_custom_call" | custom-call | flops 2147483648 | bytes 20971520 | tf_op jit(solution)/shard_map/forward_layers/pallas_call | solution.py:342
  174.8 12.5 %backward_layer_1.2 = (bf16[64,8192]{1,0:T(8,128)(2,1)}, bf16[64,512]{1,0:T(8,128)(2,1)}) custom-call(s32[1]{0:T(128)} %bitcast.4.swap_ref, s32[1024]{0:T(1024)} %bitcast.40, bf16[64,8192]{1,0:T(8,128)(2,1)} %get-tuple-element.15.hidden_ref, bf16[64,8192]{1,0:T(8,128)(2,1)} %get-tuple-element.36.upstream_ref, f32[2,64,512]{2,1,0:T(8,128)} %get-tuple-element.16.pre_ref, ...), custom_call_target="tpu_custom_call" | custom-call | flops 1073741824 | bytes 10485760 | tf_op jit(solution)/shard_map/backward_layer_1/pallas_call | solution.py:346
  187.2 12.7 %backward_layer_0.2 = (bf16[64,8192]{1,0:T(8,128)(2,1)}, bf16[64,512]{1,0:T(8,128)(2,1)}) custom-call(s32[1]{0:T(128)} %bitcast.4.swap_ref, s32[1024]{0:T(1024)} %bitcast.41, bf16[64,8192]{1,0:T(8,128)(2,1)} %broadcast_select_fusion.3.first_ref.hidden_ref, bf16[64,8192]{1,0:T(8,128)(2,1)} %get-tuple-element.18.upstream_ref, ...), custom_call_target="tpu_custom_call" | custom-call | flops 1073741824 | bytes 10485760 | tf_op jit(solution)/shard_map/backward_layer_0/pallas_call | solution.py:347
  199.9 1.3 collective-permute-start.4
  201.2 1.2 slice_bitcast_fusion
  202.5 25.2 %collective-permute-done.4 = bf16[64,8192]{1,0:T(8,128)(2,1)S(1)} collective-permute-done((bf16[64,8192]{1,0:T(8,128)(2,1)}, bf16[64,8192]{1,0:T(8,128)(2,1)S(1)}, u32[]{:S(2)}, u32[]{:S(2)}) %collective-permute-start.4) | collective-permute-done | bytes 1048608 | tf_op jit(solution)/shard_map/ppermute | solution.py:348
  227.7 1.2 broadcast_select_fusion.2.upstream_ref
  228.9 14.1 %backward_layer_1.3 = (bf16[64,8192]{1,0:T(8,128)(2,1)}, bf16[64,512]{1,0:T(8,128)(2,1)}) custom-call(s32[1]{0:T(128)} %bitcast.4.swap_ref, s32[1024]{0:T(1024)} %bitcast.42, bf16[64,8192]{1,0:T(8,128)(2,1)} %get-tuple-element.15.hidden_ref, bf16[64,8192]{1,0:T(8,128)(2,1)} %broadcast_select_fusion.2.upstream_ref, f32[2,64,512]{2,1,0:T(8,128)} %get-tuple-element.16.pre_ref, ...), custom_call_target="tpu_custom_call" | custom-call | flops 1073741824 | bytes 10485760 | tf_op jit(solution)/shard_map/backward_layer_1/pallas_call | solution.py:350
  243.0 2.4 broadcast_select_fusion
  245.5 0.7 reshape_squeeze.3.places_ref
  246.2 12.6 %backward_layer_0.3 = (bf16[64,8192]{1,0:T(8,128)(2,1)}, bf16[64,512]{1,0:T(8,128)(2,1)}) custom-call(s32[1]{0:T(128)} %bitcast.4.swap_ref, s32[1024]{0:T(1024)} %bitcast.43, bf16[64,8192]{1,0:T(8,128)(2,1)} %broadcast_select_fusion.3.first_ref.hidden_ref, bf16[64,8192]{1,0:T(8,128)(2,1)} %get-tuple-element.20.upstream_ref, ...), custom_call_target="tpu_custom_call" | custom-call | flops 1073741824 | bytes 10485760 | tf_op jit(solution)/shard_map/backward_layer_0/pallas_call | solution.py:353
  258.8 1.5 broadcast_select_fusion.4
  260.2 2.0 collective-permute-start.5
  262.2 0.6 slice_bitcast_fusion.4
  262.9 8.3 %collective-permute-done.5.dpre_other_ref = bf16[64,512]{1,0:T(8,128)(2,1)S(1)} collective-permute-done((bf16[64,512]{1,0:T(8,128)(2,1)S(1)}, bf16[64,512]{1,0:T(8,128)(2,1)S(1)}, u32[]{:S(2)}, u32[]{:S(2)}) %collective-permute-start.5) | collective-permute-done | bytes 65568 | tf_op jit(solution)/shard_map/ppermute | solution.py:218
  271.8 10.3 %gradient_in.1._ = bf16[32,2,5,128,128]{4,3,2,1,0:T(8,128)(2,1)} custom-call(s32[320]{0:T(512)} %reshape_squeeze.3.places_ref, bf16[64,8192]{1,0:T(8,128)(2,1)} %get-tuple-element.27.own_ref, bf16[64,8192]{1,0:T(8,128)(2,1)} %collective-permute-done.3.other_ref, bf16[64,512]{1,0:T(8,128)(2,1)} %get-tuple-element.33.dpre_own_ref, bf16[64,512]{1,0:T(8,128)(2,1)} %copy-done.8), custom_call_target="tpu_custom_call" | custom-call | flops 1073741824 | bytes 5242880 | tf_op jit(solution)/shard_map/gradient_in/pallas_call | solution.py:357
  283.1 10.0 %gradient_out.1 = bf16[32,2,5,128,128]{4,3,2,1,0:T(8,128)(2,1)} custom-call(s32[320]{0:T(512)} %reshape_squeeze.3.places_ref, bf16[32,2,5,128,128]{4,3,2,1,0:T(8,128)(2,1)} %gradient_in.1._, bf16[64,512]{1,0:T(8,128)(2,1)} %get-tuple-element.31.act_own_ref, bf16[64,512]{1,0:T(8,128)(2,1)} %copy-done.7, ...), custom_call_target="tpu_custom_call", output_to_operand_aliasing={{}: (1, {})} | custom-call | flops 1073741824 | bytes 5242880 | tf_op jit(solution)/shard_map/gradient_out/pallas_call | solution.py:358
  293.1 95.2 %reduce-scatter.2.cloned.1.call-done = bf16[1,2,5,128,128]{4,3,2,1,0:T(8,128)(2,1)} async-done(((bf16[32,2,5,128,128]{4,3,2,1,0:T(8,128)(2,1)}), bf16[1,2,5,128,128]{4,3,2,1,0:T(8,128)(2,1)}) %reduce-scatter.2.cloned.1.call-update) | async-done | bytes 327696 | tf_op jit(solution)/shard_map/reduce_scatter | solution.py:359
  388.4 1.7 slice_bitcast_fusion.2
  (44 shorter events, 2.8 us)
Async XLA Ops:
  7.2 12.4 %copy-start.10 = (s32[1,5]{1,0:T(1,128)S(1)}, s32[1,5]{1,0:T(1,128)}, u32[]{:S(2)}) copy-start(s32[1,5]{1,0:T(1,128)} %param.10) | copy-start | bytes 64
  7.2 12.4 %copy-start.11 = (s32[1,5]{1,0:T(1,128)S(1)}, s32[1,5]{1,0:T(1,128)}, u32[]{:S(2)}) copy-start(s32[1,5]{1,0:T(1,128)} %param.9) | copy-start | bytes 64
  7.2 14.3 %copy-start.5 = (bf16[128,8192]{1,0:T(8,128)(2,1)S(1)}, bf16[128,8192]{1,0:T(8,128)(2,1)}, u32[]{:S(2)}) copy-start(bf16[128,8192]{1,0:T(8,128)(2,1)} %param.11) | copy-start | bytes 6291460
  7.2 97.7 %all-gather.4.cloned.1.call-start = ((), (), s32[]{:S(2)}) async-start(), calls=%async_computation.2 | async-start | bytes 21626880 | tf_op jit(solution)/shard_map/all_gather | solution.py:232
  9.3 9.4 %collective-permute-start.1 = (bf16[2,5,128,128]{3,2,1,0:T(8,128)(2,1)S(1)}, bf16[2,5,128,128]{3,2,1,0:T(8,128)(2,1)S(1)}, u32[]{:S(2)}, u32[]{:S(2)}) collective-permute-start(bf16[2,5,128,128]{3,2,1,0:T(8,128)(2,1)S(1)} %constant_dynamic-update-slice_fusion), channel_id=1, source_target_pairs={{0,32},{32,0},{64,96},{96,64},{1,33},{33,1},{65,97},{97,65},{2,34}... | collective-permute-start | bytes 983048 | tf_op jit(solution)/shard_map/ppermute | solution.py:218
  19.6 368.8 %reduce-scatter.2.cloned.1.call-start = ((), (), s32[]{:S(2)}) async-start(), calls=%async_computation.1 | async-start | bytes 10813440 | tf_op jit(solution)/shard_map/reduce_scatter | solution.py:359
  19.6 4.5 %collective-permute-start = (s32[2,5]{1,0:T(2,128)S(1)}, s32[2,5]{1,0:T(2,128)S(1)}, u32[]{:S(2)}, u32[]{:S(2)}) collective-permute-start(s32[2,5]{1,0:T(2,128)S(1)} %get-tuple-element.35), channel_id=1, source_target_pairs={{0,32},{32,0},{64,96},{96,64},{1,33},{33,1},{65,97},{97,65},{2,34}... | collective-permute-start | bytes 128 | tf_op jit(solution)/shard_map/ppermute | solution.py:218
  104.9 49.0 %copy-start.2 = (bf16[64,8192]{1,0:T(8,128)(2,1)S(1)}, bf16[64,8192]{1,0:T(8,128)(2,1)}, u32[]{:S(2)}) copy-start(bf16[64,8192]{1,0:T(8,128)(2,1)} %get-tuple-element.37.first_ref) | copy-start | bytes 3145732
  126.3 27.6 %collective-permute-start.2 = (bf16[64,8192]{1,0:T(8,128)(2,1)}, bf16[64,8192]{1,0:T(8,128)(2,1)S(1)}, u32[]{:S(2)}, u32[]{:S(2)}) collective-permute-start(bf16[64,8192]{1,0:T(8,128)(2,1)} %get-tuple-element.13), channel_id=1, source_target_pairs={{0,96},{32,64},{1,97},{33,65},{2,98},{34,66},{3,99},{35,67},{4,100... | collective-permute-start | bytes 3145736 | tf_op jit(solution)/shard_map/ppermute | solution.py:340
  187.2 13.9 %copy-start.3 = (bf16[2,64,8192]{2,1,0:T(8,128)(2,1)S(1)}, bf16[2,64,8192]{2,1,0:T(8,128)(2,1)}, u32[]{:S(2)}) copy-start(bf16[2,64,8192]{2,1,0:T(8,128)(2,1)} %get-tuple-element.14) | copy-start | bytes 6291460
  199.9 27.8 %collective-permute-start.4 = (bf16[64,8192]{1,0:T(8,128)(2,1)}, bf16[64,8192]{1,0:T(8,128)(2,1)S(1)}, u32[]{:S(2)}, u32[]{:S(2)}) collective-permute-start(bf16[64,8192]{1,0:T(8,128)(2,1)} %get-tuple-element.19), channel_id=1, source_target_pairs={{96,0},{64,32},{97,1},{65,33},{98,2},{66,34},{99,3},{67,35},{100,4... | collective-permute-start | bytes 3145736 | tf_op jit(solution)/shard_map/ppermute | solution.py:348
  201.2 26.5 %copy-start = (bf16[64,8192]{1,0:T(8,128)(2,1)S(1)}, bf16[64,8192]{1,0:T(8,128)(2,1)}, u32[]{:S(2)}) copy-start(bf16[64,8192]{1,0:T(8,128)(2,1)} %get-tuple-element.36.upstream_ref) | copy-start | bytes 3145732
  202.4 60.5 %collective-permute-start.3 = (bf16[64,8192]{1,0:T(8,128)(2,1)S(1)}, bf16[64,8192]{1,0:T(8,128)(2,1)}, u32[]{:S(2)}, u32[]{:S(2)}) collective-permute-start(bf16[64,8192]{1,0:T(8,128)(2,1)S(1)} %get-tuple-element.26), channel_id=1, source_target_pairs={{0,32},{32,0},{64,96},{96,64},{1,33},{33,1},{65,97},{97,65},{2,34}... | collective-permute-start | bytes 3145736 | tf_op jit(solution)/shard_map/ppermute | solution.py:218
  228.9 14.1 %copy-start.1 = (bf16[64,8192]{1,0:T(8,128)(2,1)S(1)}, bf16[64,8192]{1,0:T(8,128)(2,1)}, u32[]{:S(2)}) copy-start(bf16[64,8192]{1,0:T(8,128)(2,1)} %broadcast_select_fusion.2.upstream_ref) | copy-start | bytes 3145732
  245.5 36.7 %collective-permute-start.7 = (bf16[64,8192]{1,0:T(8,128)(2,1)S(1)}, bf16[64,8192]{1,0:T(8,128)(2,1)S(1)}, u32[]{:S(2)}, u32[]{:S(2)}) collective-permute-start(bf16[64,8192]{1,0:T(8,128)(2,1)S(1)} %get-tuple-element.24), channel_id=1, source_target_pairs={{0,32},{32,0},{64,96},{96,64},{1,33},{33,1},{65,97},{97,65},{2,34}... | collective-permute-start | bytes 3145736 | tf_op jit(solution)/shard_map/ppermute | solution.py:218
  246.2 12.6 %copy-start.9 = (bf16[64,512]{1,0:T(8,128)(2,1)S(1)}, bf16[64,512]{1,0:T(8,128)(2,1)}, u32[]{:S(2)}) copy-start(bf16[64,512]{1,0:T(8,128)(2,1)} %get-tuple-element.22) | copy-start | bytes 196612
  246.2 16.1 %copy-start.6 = (bf16[2,64,512]{2,1,0:T(8,128)(2,1)S(1)}, bf16[2,64,512]{2,1,0:T(8,128)(2,1)}, u32[]{:S(2)}) copy-start(bf16[2,64,512]{2,1,0:T(8,128)(2,1)} %get-tuple-element.23) | copy-start | bytes 393220
  260.2 10.9 %collective-permute-start.5 = (bf16[64,512]{1,0:T(8,128)(2,1)S(1)}, bf16[64,512]{1,0:T(8,128)(2,1)S(1)}, u32[]{:S(2)}, u32[]{:S(2)}) collective-permute-start(bf16[64,512]{1,0:T(8,128)(2,1)S(1)} %get-tuple-element.32), channel_id=1, source_target_pairs={{0,32},{32,0},{64,96},{96,64},{1,33},{33,1},{65,97},{97,65},{2,34}... | collective-permute-start | bytes 196616 | tf_op jit(solution)/shard_map/ppermute | solution.py:218
  262.9 19.3 %collective-permute-start.6 = (bf16[64,512]{1,0:T(8,128)(2,1)S(1)}, bf16[64,512]{1,0:T(8,128)(2,1)S(1)}, u32[]{:S(2)}, u32[]{:S(2)}) collective-permute-start(bf16[64,512]{1,0:T(8,128)(2,1)S(1)} %get-tuple-element.30), channel_id=1, source_target_pairs={{0,32},{32,0},{64,96},{96,64},{1,33},{33,1},{65,97},{97,65},{2,34}... | collective-permute-start | bytes 196616 | tf_op jit(solution)/shard_map/ppermute | solution.py:218
  271.2 0.6 copy-start.8
  282.1 0.6 copy-start.7
  282.1 1.0 copy-start.4
Sparse Core Ops, SparseCore 0:
  19.7 85.1 all-gather.3
  293.3 95.0 reduce-scatter.1

commit v3 on v2

v3 whole, which is shorter than its diff:
```python
import functools

import jax
import jax.numpy as jnp
from jax import lax
from jax.experimental import pallas as pl
from jax.experimental.pallas import tpu as pltpu
from jax.sharding import PartitionSpec as P

D = 8192
RANK = 512
BLOCK = 128
ROWS_D = D // BLOCK
ROWS_K = RANK // BLOCK
NBLK = ROWS_D * ROWS_K
EPS = 1e-05
CHUNK = 1024
BLOCKS = CHUNK // BLOCK
SPAN = 1024
NT = (((1,), (1,)), ((), ()))
NN = (((1,), (0,)), ((), ()))
TN = (((0,), (0,)), ((), ()))
PAIR = [(0, 1), (1, 0), (2, 3), (3, 2)]
UP = [(0, 3), (1, 2)]
DOWN = [(3, 0), (2, 1)]


def dot(left, right, dims):
    return lax.dot_general(left, right, dims, preferred_element_type=jnp.float32)


class Weights:
    def __init__(self, swap_ref, where_ref, source, held, sems, wanted):
        self.where_ref = where_ref
        self.swap = swap_ref[0]
        self.held = held
        self.order = wanted
        owners = source.shape[0]
        self.copies = {}
        for i, (layer, matrix) in enumerate(wanted):
            copy = pltpu.make_async_copy(source.at[:, layer ^ self.swap, matrix], held.at[i, pl.ds(0, owners)], sems.at[i])
            copy.start()
            self.copies[layer, matrix] = copy
        for i in range(len(wanted)):
            held[i, owners, 0] = jnp.zeros(held.shape[3:], held.dtype)

    def wait(self, layer, matrix):
        self.copies[layer, matrix].wait()

    def block(self, layer, matrix, number):
        code = self.where_ref[((layer ^ self.swap) * 2 + matrix) * NBLK + number]
        return self.held[self.order.index((layer, matrix)), code >> 3, code & 7]

    def rows_in(self, layer, chunk):
        rows = range(chunk * BLOCKS, (chunk + 1) * BLOCKS)
        return jnp.concatenate(
            [
                jnp.concatenate([self.block(layer, 0, row * ROWS_K + col) for col in range(ROWS_K)], axis=1)
                for row in rows
            ],
            axis=0,
        )

    def columns_out(self, layer, chunk):
        cols = range(chunk * BLOCKS, (chunk + 1) * BLOCKS)
        return jnp.concatenate(
            [
                jnp.concatenate([self.block(layer, 1, row * ROWS_D + col) for col in cols], axis=1)
                for row in range(ROWS_K)
            ],
            axis=0,
        )


def chunks():
    return [(chunk, slice(chunk * CHUNK, (chunk + 1) * CHUNK)) for chunk in range(D // CHUNK)]


def forward_down(weights, layer, hidden_ref, normed_ref):
    total = 0.0
    for _, cols in chunks():
        wide = hidden_ref[:, cols].astype(jnp.float32)
        total = total + jnp.sum(wide * wide, axis=-1, keepdims=True)
    inverse = 1.0 / jnp.sqrt(total / D + EPS)
    for _, cols in chunks():
        normed_ref[:, cols] = (hidden_ref[:, cols].astype(jnp.float32) * inverse).astype(jnp.bfloat16)
    weights.wait(layer, 0)
    pre = 0.0
    for chunk, cols in chunks():
        pre = pre + dot(normed_ref[:, cols], weights.rows_in(layer, chunk), NN)
    return pre, inverse


def forward_up(weights, layer, hidden_ref, act, next_ref):
    weights.wait(layer, 1)
    for chunk, cols in chunks():
        moved = dot(act, weights.columns_out(layer, chunk), NN)
        next_ref[:, cols] = (hidden_ref[:, cols].astype(jnp.float32) + moved).astype(jnp.bfloat16)


def backward(weights, layer, hidden_ref, upstream_ref, pre, inverse, earlier_ref):
    dact = 0.0
    for chunk, cols in chunks():
        dact = dact + dot(upstream_ref[:, cols], weights.columns_out(layer, chunk), NT)
    sig = jax.nn.sigmoid(pre)
    dpre = (dact * sig * (1.0 + pre * (1.0 - sig))).astype(jnp.bfloat16)
    if earlier_ref is not None:
        mean = jnp.sum(dpre.astype(jnp.float32) * pre, axis=-1, keepdims=True) / D
        pull = mean * inverse * inverse
        for chunk, cols in chunks():
            dnorm = dot(dpre, weights.rows_in(layer, chunk), NT)
            hidden = hidden_ref[:, cols].astype(jnp.float32)
            earlier_ref[:, cols] = (
                upstream_ref[:, cols].astype(jnp.float32) + dnorm * inverse - hidden * pull
            ).astype(jnp.bfloat16)
    return dpre


def silu(pre):
    return (pre * jax.nn.sigmoid(pre)).astype(jnp.bfloat16)


def forward_kernel(swap_ref, where_ref, first_ref, source, last_ref, second_ref, normed_ref, held, sems):
    weights = Weights(swap_ref, where_ref, source, held, sems, [(0, 0), (0, 1), (1, 0), (1, 1)])
    pre, _ = forward_down(weights, 0, first_ref, normed_ref)
    forward_up(weights, 0, first_ref, silu(pre), second_ref)
    pre, _ = forward_down(weights, 1, second_ref, normed_ref)
    forward_up(weights, 1, second_ref, silu(pre), last_ref)


def turn_kernel(
    swap_ref, where_ref, first_ref, grad_ref, source, second_ref, pre_ref, inverse_ref, normed_ref, act_ref, earlier_ref, middle_ref, held, sems
):
    weights = Weights(swap_ref, where_ref, source, held, sems, [(0, 0), (0, 1), (1, 0), (1, 1)])
    pres, inverses = [], []
    for layer, hidden_ref in enumerate((first_ref, second_ref)):
        place = layer ^ swap_ref[0]
        pre, inverse = forward_down(weights, layer, hidden_ref, normed_ref.at[place])
        act = silu(pre)
        pre_ref[layer] = pre
        inverse_ref[layer] = jnp.broadcast_to(inverse, inverse_ref.shape[1:])
        act_ref[place] = act
        if layer == 0:
            forward_up(weights, 0, first_ref, act, second_ref)
    weights.wait(1, 1)
    backward(weights, 1, second_ref, grad_ref, pre_ref[1], inverse_ref[1][:, :1], middle_ref)
    backward(weights, 0, first_ref, middle_ref, pre_ref[0], inverse_ref[0][:, :1], earlier_ref)


def backward_kernel(
    layer, last, swap_ref, where_ref, hidden_ref, upstream_ref, pre_ref, inverse_ref, source, *outs
):
    held, sems = outs[-2:]
    weights = Weights(swap_ref, where_ref, source, held, sems, [(layer, 1)] if last else [(layer, 1), (layer, 0)])
    for matrix in [1] if last else [1, 0]:
        weights.wait(layer, matrix)
    outs[0][...] = backward(
        weights, layer, hidden_ref, upstream_ref, pre_ref[layer], inverse_ref[layer][:, :1], None if last else outs[1]
    )


def pick(places_ref, dense, out_ref, base):
    owners, slots = out_ref.shape[0], out_ref.shape[2]

    for owner in range(owners):
        for slot in range(slots):
            out_ref[owner, 0, slot] = dense[places_ref[base + owner * slots + slot]]


def gradient_in_kernel(places_ref, own_ref, other_ref, dpre_own_ref, dpre_other_ref, out_ref, dense):
    step = pl.program_id(0)

    @pl.when(step == 0)
    def _():
        dense[NBLK] = jnp.zeros((BLOCK, BLOCK), jnp.bfloat16)

        dpre = jnp.concatenate([dpre_own_ref[...], dpre_other_ref[...]], axis=0)
        for chunk in range(D // SPAN):
            cols = slice(chunk * SPAN, (chunk + 1) * SPAN)
            normed = jnp.concatenate([own_ref[:, cols], other_ref[:, cols]], axis=0)
            part = dot(normed, dpre, TN).astype(jnp.bfloat16)
            for row in range(SPAN // BLOCK):
                for col in range(ROWS_K):
                    dense[(chunk * (SPAN // BLOCK) + row) * ROWS_K + col] = part[
                        row * BLOCK : (row + 1) * BLOCK, col * BLOCK : (col + 1) * BLOCK
                    ]

    pick(places_ref, dense, out_ref, step * out_ref.shape[0] * out_ref.shape[2])


def gradient_out_kernel(places_ref, _, act_own_ref, act_other_ref, own_ref, other_ref, out_ref, dense, turned):
    step = pl.program_id(0)

    @pl.when(step == 0)
    def _():
        dense[NBLK] = jnp.zeros((BLOCK, BLOCK), jnp.bfloat16)
        act = jnp.concatenate([act_own_ref[...], act_other_ref[...]], axis=0)
        turned[...] = act.astype(jnp.float32).T.astype(jnp.bfloat16)

        for chunk in range(D // SPAN):
            cols = slice(chunk * SPAN, (chunk + 1) * SPAN)
            upstream = jnp.concatenate([own_ref[:, cols], other_ref[:, cols]], axis=0)
            part = dot(turned[...], upstream, NN).astype(jnp.bfloat16)
            for row in range(ROWS_K):
                for col in range(SPAN // BLOCK):
                    dense[row * ROWS_D + chunk * (SPAN // BLOCK) + col] = part[
                        row * BLOCK : (row + 1) * BLOCK, col * BLOCK : (col + 1) * BLOCK
                    ]

    pick(places_ref, dense, out_ref, (places_ref.shape[0] // 2) + step * out_ref.shape[0] * out_ref.shape[2])


def whole(*shape):
    return pl.BlockSpec(shape, lambda step, *_: (0,) * len(shape))


def params(flops, moved):
    return dict(
        compiler_params=pltpu.CompilerParams(
            dimension_semantics=("arbitrary",), vmem_limit_bytes=56 * 1024 * 1024
        ),
        cost_estimate=pl.CostEstimate(flops=flops, bytes_accessed=moved, transcendentals=0),
    )


def swapped(array):
    return lax.ppermute(array, "section", PAIR)


def per_device(tokens, blocks_in, blocks_out, pos_in, pos_out, cotangent):
    here = lax.axis_index("section")
    owners = lax.axis_size("dp")
    slots = blocks_in.shape[1]
    rows = tokens.shape[0] // 2
    odd = here % 2
    swap = odd.astype(jnp.int32).reshape(1)
    upper = here >= 2
    half = jnp.where((here == 1) | (here == 2), rows, 0)

    own = jnp.stack([blocks_in[0], blocks_out[0]])
    weights = lax.all_gather(jnp.stack([own, swapped(own)]), "dp", axis=0)
    own_places = jnp.stack([pos_in[0], pos_out[0]])
    places = lax.all_gather(jnp.stack([own_places, swapped(own_places)]), "dp", axis=0).transpose(1, 2, 0, 3)
    codes = jnp.arange(owners, dtype=jnp.int32)[:, None] * 8 + jnp.arange(slots, dtype=jnp.int32)
    named = places[..., None] == jnp.arange(NBLK, dtype=jnp.int32)
    where = jnp.max(jnp.where(named, codes[..., None], -1), axis=(2, 3)).reshape(-1)
    where = jnp.where(where < 0, owners * 8, where)
    places = places[0].reshape(-1)

    first_tokens = lax.dynamic_slice_in_dim(tokens, half, rows, 0)
    last_grads = lax.dynamic_slice_in_dim(cotangent, half, rows, 0)

    def shape(*dims, dtype=jnp.bfloat16):
        return jax.ShapeDtypeStruct(dims, dtype)

    moved = weights.size * 2
    work = 2 * rows * D * RANK
    anywhere = pl.BlockSpec(memory_space=pl.ANY)

    def held(count):
        return [
            pltpu.VMEM((count, owners + 1, slots, BLOCK, BLOCK), jnp.bfloat16),
            pltpu.SemaphoreType.DMA((count,)),
        ]

    forward = pl.pallas_call(
        forward_kernel,
        out_shape=shape(rows, D),
        grid_spec=pltpu.PrefetchScalarGridSpec(
            num_scalar_prefetch=2,
            grid=(1,),
            in_specs=[whole(rows, D), anywhere],
            out_specs=whole(rows, D),
            scratch_shapes=[pltpu.VMEM((rows, D), jnp.bfloat16), pltpu.VMEM((rows, D), jnp.bfloat16)] + held(4),
        ),
        name="forward_layers",
        **params(4 * work, moved),
    )
    turn = pl.pallas_call(
        turn_kernel,
        out_shape=(
            shape(rows, D),
            shape(2, rows, RANK, dtype=jnp.float32),
            shape(2, rows, BLOCK, dtype=jnp.float32),
            shape(2, rows, D),
            shape(2, rows, RANK),
            shape(rows, D),
        ),
        grid_spec=pltpu.PrefetchScalarGridSpec(
            num_scalar_prefetch=2,
            grid=(1,),
            in_specs=[whole(rows, D), whole(rows, D), anywhere],
            out_specs=[
                whole(rows, D),
                whole(2, rows, RANK),
                whole(2, rows, BLOCK),
                whole(2, rows, D),
                whole(2, rows, RANK),
                whole(rows, D),
            ],
            scratch_shapes=[pltpu.VMEM((rows, D), jnp.bfloat16)] + held(4),
        ),
        name="turn_layers",
        **params(7 * work, moved),
    )

    def backward_layer(layer, last):
        return pl.pallas_call(
            functools.partial(backward_kernel, layer, last),
            out_shape=(shape(rows, RANK),) + (() if last else (shape(rows, D),)),
            grid_spec=pltpu.PrefetchScalarGridSpec(
                num_scalar_prefetch=2,
                grid=(1,),
                in_specs=[
                    whole(rows, D),
                    whole(rows, D),
                    whole(2, rows, RANK),
                    whole(2, rows, BLOCK),
                    anywhere,
                ],
                out_specs=[whole(rows, RANK)] + ([] if last else [whole(rows, D)]),
                scratch_shapes=held(1 if last else 2),
            ),
            name=f"backward_layer_{layer}",
            **params((1 if last else 2) * work, moved // 4 * (1 if last else 2)),
        )

    steps = 4
    part = (owners // steps, 1, slots, BLOCK, BLOCK)
    partial_shape = shape(owners, 2, slots, BLOCK, BLOCK)
    dense = pltpu.VMEM((NBLK + 1, BLOCK, BLOCK), jnp.bfloat16)
    gradient_in = pl.pallas_call(
        gradient_in_kernel,
        out_shape=partial_shape,
        grid_spec=pltpu.PrefetchScalarGridSpec(
            num_scalar_prefetch=1,
            grid=(steps,),
            in_specs=[whole(rows, D), whole(rows, D), whole(rows, RANK), whole(rows, RANK)],
            out_specs=pl.BlockSpec(part, lambda step, _: (step, 0, 0, 0, 0)),
            scratch_shapes=[dense],
        ),
        name="gradient_in",
        **params(2 * work, moved // 4),
    )
    gradient_out = pl.pallas_call(
        gradient_out_kernel,
        out_shape=partial_shape,
        grid_spec=pltpu.PrefetchScalarGridSpec(
            num_scalar_prefetch=1,
            grid=(steps,),
            in_specs=[
                pl.BlockSpec(memory_space=pl.ANY),
                whole(rows, RANK),
                whole(rows, RANK),
                whole(rows, D),
                whole(rows, D),
            ],
            out_specs=pl.BlockSpec(part, lambda step, _: (step, 1, 0, 0, 0)),
            scratch_shapes=[dense, pltpu.VMEM((RANK, 2 * rows), jnp.bfloat16)],
        ),
        input_output_aliases={1: 0},
        name="gradient_out",
        **params(2 * work, moved // 4),
    )

    arrived = lax.ppermute(forward(swap, where, first_tokens, weights), "section", UP)
    first = jnp.where(upper, arrived, first_tokens)
    second, pre, inverse, normed, act, leaving = turn(swap, where, first, last_grads, weights)
    arrived = lax.ppermute(leaving, "section", DOWN)
    normed_other = swapped(normed[1])
    act_other = swapped(act[1])

    grads = jnp.where(upper, last_grads, arrived)
    dpre_high, middle = backward_layer(1, False)(swap, where, second, grads, pre, inverse, weights)
    grads_other = swapped(jnp.where(odd == 0, grads, middle))
    grads_own = jnp.where(odd == 0, middle, grads)
    (dpre_low,) = backward_layer(0, True)(swap, where, first, middle, pre, inverse, weights)
    dpre_other = swapped(jnp.where(odd == 0, dpre_high, dpre_low))
    dpre_own = jnp.where(odd == 0, dpre_low, dpre_high)

    partial = gradient_in(places, normed[0], normed_other, dpre_own, dpre_other)
    partial = gradient_out(places, partial, act[0], act_other, grads_own, grads_other)
    summed = lax.psum_scatter(partial, "dp", scatter_dimension=0, tiled=False)
    return (summed[0][None], summed[1][None])


def solution(mesh):
    in_specs = (
        P("dp", None),
        P("section", "dp", None, None),
        P("section", "dp", None, None),
        P("section", "dp"),
        P("section", "dp"),
        P("dp", None),
    )
    out_specs = (P("section", "dp", None, None), P("section", "dp", None, None))
    return jax.shard_map(
        per_device, mesh=mesh, in_specs=in_specs, out_specs=out_specs, check_vma=False
    )
```

time: 398 us -> 359 us (0.902)
  Pallas kernels: 113 us -> 70.2 us
    pallas_call x6 -> x4, Pallas kernels: 92.9 us -> 55.2 us  [the longest x1 22.1 us: per_device(): turn(swap, where, first, last_grads, weights)]
    ppermute x6, waiting for transfers between devices: 16 us -> 21 us  [swapped(): return lax.ppermute(array, 'section', PAIR)]
  transfers between devices with their start and end apart: 10 -> 10, of which waited for: 6 -> 7; matrix products, arithmetic and copies ran while one was open for 3% -> 4% of each run, Pallas kernels for 9% -> 8%
where the time goes in v3:
time: 359 us
  waiting for transfers between devices  215 us (60%)
  Pallas kernels  70.2 us (20%)
  blocking collectives  25.9 us (7%)
  between operations  14.2 us (4%)
  local copies, waits for them, and re-layouts  13 us (4%)
  starting transfers between devices  12 us (3%)
  other arithmetic  8.09 us (2%)
    reduce_scatter x1, waiting for transfers between devices, per_device(): summed = lax.psum_scatter(partial, 'dp', scatter_dimension=0, tiled=False)  95.3 us
    all_gather x1, waiting for transfers between devices, per_device(): weights = lax.all_gather(jnp.stack([own, swapped(own)]), 'dp', axis=0)  54.8 us
    all_gather x1, blocking collectives, per_device(): lax.all_gather(jnp.stack([own_places, swapped(own_places)]), 'dp', axis=0)  25.9 us
    ppermute x1, waiting for transfers between devices, per_device(): arrived = lax.ppermute(leaving, 'section', DOWN)  23.5 us
    pallas_call x1, Pallas kernels, per_device(): turn(swap, where, first, last_grads, weights)  22.1 us
    ppermute x6, waiting for transfers between devices, swapped(): return lax.ppermute(array, 'section', PAIR)  21 us
    ppermute x1, waiting for transfers between devices, per_device(): lax.ppermute(forward(swap, where, first_tokens, weights), 'section', UP)  20.6 us
    pallas_call x1, Pallas kernels, per_device(): backward_layer(1, False)(swap, where, second, grads, pre, inverse, weights)  12.8 us
  transfers between devices with their start and end apart: 10, of which 7 were waited for; matrix products, arithmetic and copies ran while one was open for 4% of the time, Pallas kernels for 8%

profile of v3, /device:TPU:0, one launch (start us, length us, event | category | flops | bytes accessed | tf_op | source)
XLA Modules:
  0.0 358.7 jit_solution(13882460584367519456)
XLA Ops:
  7.2 1.1 constant_dynamic-update-slice_fusion.1
  8.3 0.9 constant_dynamic-update-slice_fusion
  9.3 1.7 collective-permute-start.1
  10.9 7.7 %collective-permute-done.1 = bf16[2,5,128,128]{3,2,1,0:T(8,128)(2,1)S(1)} collective-permute-done((bf16[2,5,128,128]{3,2,1,0:T(8,128)(2,1)S(1)}, bf16[2,5,128,128]{3,2,1,0:T(8,128)(2,1)S(1)}, u32[]{:S(2)}, u32[]{:S(2)}) %collective-permute-start.1) | collective-permute-done | bytes 327712 | tf_op jit(solution)/shard_map/ppermute | solution.py:227
  18.6 0.9 pad_maximum_fusion
  19.6 1.8 collective-permute-start
  21.5 1.1 constant_dynamic-slice_fusion.1.first_ref
  22.5 0.7 collective-permute-done
  23.3 25.9 %all-gather = s32[64,2,5]{2,1,0:T(2,128)S(1)} all-gather(s32[2,2,5]{2,1,0:T(2,128)S(1)} %pad_add_fusion), channel_id=2, replica_groups=mesh['section'=4,'dp'=32] {'dp'}, dimensions={0}, use_global_device_ids=true | all-gather | bytes 2640 | tf_op jit(solution)/shard_map/all_gather | solution.py:243
  50.1 54.8 %all-gather.4.cloned.1.call-done = bf16[64,2,5,128,128]{4,3,2,1,0:T(8,128)(2,1)} async-done(((bf16[2,2,5,128,128]{4,3,2,1,0:T(8,128)(2,1)}), bf16[64,2,5,128,128]{4,3,2,1,0:T(8,128)(2,1)}) %all-gather.4.cloned.1.call-update) | async-done | bytes 20971536 | tf_op jit(solution)/shard_map/all_gather | solution.py:241
  104.9 12.0 %forward_layers.1 = bf16[64,8192]{1,0:T(8,128)(2,1)} custom-call(s32[1]{0:T(128)} %bitcast.4.swap_ref, s32[1024]{0:T(1024)} %compare_select_fusion.where_ref, bf16[64,8192]{1,0:T(8,128)(2,1)} %constant_dynamic-slice_fusion.1.first_ref, bf16[32,2,2,5,128,128]{5,4,3,2,1,0:T(8,128)(2,1)} %bitcast.28), custom_call_target="tpu_custom_call" | custom-call | flops 2147483648 | bytes 20971520 | tf_op jit(solution)/shard_map/forward_layers/pallas_call | solution.py:366
  117.0 4.8 %collective-permute-start.2 = (bf16[64,8192]{1,0:T(8,128)(2,1)}, bf16[64,8192]{1,0:T(8,128)(2,1)S(1)}, u32[]{:S(2)}, u32[]{:S(2)}) collective-permute-start(bf16[64,8192]{1,0:T(8,128)(2,1)} %forward_layers.1), channel_id=1, source_target_pairs={{0,96},{32,64},{1,97},{33,65},{2,98},{34,66},{3,99},{35,67},{4,100... | collective-permute-start | bytes 3145736 | tf_op jit(solution)/shard_map/ppermute | solution.py:366
  121.8 2.3 constant_dynamic-slice_fusion.grad_ref
  124.1 20.6 %collective-permute-done.2 = bf16[64,8192]{1,0:T(8,128)(2,1)S(1)} collective-permute-done((bf16[64,8192]{1,0:T(8,128)(2,1)}, bf16[64,8192]{1,0:T(8,128)(2,1)S(1)}, u32[]{:S(2)}, u32[]{:S(2)}) %collective-permute-start.2) | collective-permute-done | bytes 1048608 | tf_op jit(solution)/shard_map/ppermute | solution.py:366
  144.7 1.3 broadcast_select_fusion.3.first_ref.hidden_ref
  146.0 22.1 %turn_layers.1 = (bf16[64,8192]{1,0:T(8,128)(2,1)}, f32[2,64,512]{2,1,0:T(8,128)}, f32[2,64,128]{2,1,0:T(8,128)}, bf16[2,64,8192]{2,1,0:T(8,128)(2,1)}, bf16[2,6...) custom-call(s32[1]{0:T(128)} %bitcast.4.swap_ref, s32[1024]{0:T(1024)} %compare_select_fusion.where_ref, ...), custom_call_target="tpu_custom_call" | custom-call | flops 3758096384 | bytes 20971520 | tf_op jit(solution)/shard_map/turn_layers/pallas_call | solution.py:368
  168.2 1.3 collective-permute-start.4
  169.5 2.8 slice_bitcast_fusion
  172.6 23.5 %collective-permute-done.4 = bf16[64,8192]{1,0:T(8,128)(2,1)S(1)} collective-permute-done((bf16[64,8192]{1,0:T(8,128)(2,1)}, bf16[64,8192]{1,0:T(8,128)(2,1)S(1)}, u32[]{:S(2)}, u32[]{:S(2)}) %collective-permute-start.4) | collective-permute-done | bytes 1048608 | tf_op jit(solution)/shard_map/ppermute | solution.py:369
  196.0 1.2 broadcast_select_fusion.2.upstream_ref
  197.2 12.8 %backward_layer_1.1 = (bf16[64,512]{1,0:T(8,128)(2,1)}, bf16[64,8192]{1,0:T(8,128)(2,1)}) custom-call(s32[1]{0:T(128)} %bitcast.4.swap_ref, s32[1024]{0:T(1024)} %compare_select_fusion.where_ref, bf16[64,8192]{1,0:T(8,128)(2,1)} %get-tuple-element.11.hidden_ref, bf16[64,8192]{1,0:T(8,128)(2,1)} %broadcast_select_fusion.2.upstream_ref, ...), custom_call_target="tpu_custom_call" | custom-call | flops 1073741824 | bytes 10485760 | tf_op jit(solution)/shard_map/backward_layer_1/pallas_call | solution.py:374
  210.1 2.3 broadcast_select_fusion
  212.4 0.7 reshape_squeeze.3.places_ref
  213.2 8.2 %backward_layer_0.1 = bf16[64,512]{1,0:T(8,128)(2,1)} custom-call(s32[1]{0:T(128)} %bitcast.4.swap_ref, s32[1024]{0:T(1024)} %compare_select_fusion.where_ref, bf16[64,8192]{1,0:T(8,128)(2,1)} %broadcast_select_fusion.3.first_ref.hidden_ref, bf16[64,8192]{1,0:T(8,128)(2,1)} %get-tuple-element.15.upstream_ref, f32[2,64,512]{2,1,0:T(8,128)} %get-tuple-element.13.pre_ref, ...), custom_call_target="tpu_custom_call" | custom-call | flops 536870912 | bytes 5242880 | tf_op jit(solution)/shard_map/backward_layer_0/pallas_call | solution.py:377
  221.4 1.5 broadcast_select_fusion.4
  222.9 2.0 collective-permute-start.5
  225.5 12.6 %collective-permute-done.5.dpre_other_ref = bf16[64,512]{1,0:T(8,128)(2,1)S(1)} collective-permute-done((bf16[64,512]{1,0:T(8,128)(2,1)S(1)}, bf16[64,512]{1,0:T(8,128)(2,1)S(1)}, u32[]{:S(2)}, u32[]{:S(2)}) %collective-permute-start.5) | collective-permute-done | bytes 65568 | tf_op jit(solution)/shard_map/ppermute | solution.py:227
  238.1 0.6 copy-done.6
  238.7 7.4 %gradient_in.1._ = bf16[32,2,5,128,128]{4,3,2,1,0:T(8,128)(2,1)} custom-call(s32[320]{0:T(512)} %reshape_squeeze.3.places_ref, bf16[64,8192]{1,0:T(8,128)(2,1)} %get-tuple-element.21.own_ref, bf16[64,8192]{1,0:T(8,128)(2,1)} %collective-permute-done.3.other_ref, bf16[64,512]{1,0:T(8,128)(2,1)} %get-tuple-element.27.dpre_own_ref, bf16[64,512]{1,0:T(8,128)(2,1)} %copy-done.6), custom_call_target="tpu_custom_call" | custom-call | flops 1073741824 | bytes 5242880 | tf_op jit(solution)/shard_map/gradient_in/pallas_call | solution.py:381
  247.2 7.6 %gradient_out.1 = bf16[32,2,5,128,128]{4,3,2,1,0:T(8,128)(2,1)} custom-call(s32[320]{0:T(512)} %reshape_squeeze.3.places_ref, bf16[32,2,5,128,128]{4,3,2,1,0:T(8,128)(2,1)} %gradient_in.1._, bf16[64,512]{1,0:T(8,128)(2,1)} %get-tuple-element.25.act_own_ref, bf16[64,512]{1,0:T(8,128)(2,1)} %copy-done.5, ...), custom_call_target="tpu_custom_call", output_to_operand_aliasing={{}: (1, {})} | custom-call | flops 1073741824 | bytes 5242880 | tf_op jit(solution)/shard_map/gradient_out/pallas_call | solution.py:382
  254.8 95.3 %reduce-scatter.2.cloned.1.call-done = bf16[1,2,5,128,128]{4,3,2,1,0:T(8,128)(2,1)} async-done(((bf16[32,2,5,128,128]{4,3,2,1,0:T(8,128)(2,1)}), bf16[1,2,5,128,128]{4,3,2,1,0:T(8,128)(2,1)}) %reduce-scatter.2.cloned.1.call-update) | async-done | bytes 327696 | tf_op jit(solution)/shard_map/reduce_scatter | solution.py:383
  350.1 1.7 slice_bitcast_fusion.2
  (40 shorter events, 3.0 us)
Async XLA Ops:
  7.2 12.4 %copy-start.8 = (s32[1,5]{1,0:T(1,128)S(1)}, s32[1,5]{1,0:T(1,128)}, u32[]{:S(2)}) copy-start(s32[1,5]{1,0:T(1,128)} %param.10) | copy-start | bytes 64
  7.2 12.4 %copy-start.9 = (s32[1,5]{1,0:T(1,128)S(1)}, s32[1,5]{1,0:T(1,128)}, u32[]{:S(2)}) copy-start(s32[1,5]{1,0:T(1,128)} %param.9) | copy-start | bytes 64
  7.2 14.3 %copy-start.1 = (bf16[128,8192]{1,0:T(8,128)(2,1)S(1)}, bf16[128,8192]{1,0:T(8,128)(2,1)}, u32[]{:S(2)}) copy-start(bf16[128,8192]{1,0:T(8,128)(2,1)} %param.6) | copy-start | bytes 6291460
  7.2 97.7 %all-gather.4.cloned.1.call-start = ((), (), s32[]{:S(2)}) async-start(), calls=%async_computation.2 | async-start | bytes 21626880 | tf_op jit(solution)/shard_map/all_gather | solution.py:241
  9.3 9.4 %collective-permute-start.1 = (bf16[2,5,128,128]{3,2,1,0:T(8,128)(2,1)S(1)}, bf16[2,5,128,128]{3,2,1,0:T(8,128)(2,1)S(1)}, u32[]{:S(2)}, u32[]{:S(2)}) collective-permute-start(bf16[2,5,128,128]{3,2,1,0:T(8,128)(2,1)S(1)} %constant_dynamic-update-slice_fusion), channel_id=1, source_target_pairs={{0,32},{32,0},{64,96},{96,64},{1,33},{33,1},{65,97},{97,65},{2,34}... | collective-permute-start | bytes 983048 | tf_op jit(solution)/shard_map/ppermute | solution.py:227
  19.5 330.6 %reduce-scatter.2.cloned.1.call-start = ((), (), s32[]{:S(2)}) async-start(), calls=%async_computation.1 | async-start | bytes 10813440 | tf_op jit(solution)/shard_map/reduce_scatter | solution.py:383
  19.6 3.6 %collective-permute-start = (s32[2,5]{1,0:T(2,128)S(1)}, s32[2,5]{1,0:T(2,128)S(1)}, u32[]{:S(2)}, u32[]{:S(2)}) collective-permute-start(s32[2,5]{1,0:T(2,128)S(1)} %get-tuple-element.29), channel_id=1, source_target_pairs={{0,32},{32,0},{64,96},{96,64},{1,33},{33,1},{65,97},{97,65},{2,34}... | collective-permute-start | bytes 128 | tf_op jit(solution)/shard_map/ppermute | solution.py:227
  117.0 27.7 %collective-permute-start.2 = (bf16[64,8192]{1,0:T(8,128)(2,1)}, bf16[64,8192]{1,0:T(8,128)(2,1)S(1)}, u32[]{:S(2)}, u32[]{:S(2)}) collective-permute-start(bf16[64,8192]{1,0:T(8,128)(2,1)} %forward_layers.1), channel_id=1, source_target_pairs={{0,96},{32,64},{1,97},{33,65},{2,98},{34,66},{3,99},{35,67},{4,100... | collective-permute-start | bytes 3145736 | tf_op jit(solution)/shard_map/ppermute | solution.py:366
  168.2 27.8 %collective-permute-start.4 = (bf16[64,8192]{1,0:T(8,128)(2,1)}, bf16[64,8192]{1,0:T(8,128)(2,1)S(1)}, u32[]{:S(2)}, u32[]{:S(2)}) collective-permute-start(bf16[64,8192]{1,0:T(8,128)(2,1)} %get-tuple-element.12), channel_id=1, source_target_pairs={{96,0},{64,32},{97,1},{65,33},{98,2},{66,34},{99,3},{67,35},{100,4... | collective-permute-start | bytes 3145736 | tf_op jit(solution)/shard_map/ppermute | solution.py:369
  169.5 26.5 %copy-start.2 = (bf16[128,8192]{1,0:T(8,128)(2,1)S(1)}, bf16[128,8192]{1,0:T(8,128)(2,1)}, u32[]{:S(2)}) copy-start(bf16[128,8192]{1,0:T(8,128)(2,1)} %param.11) | copy-start | bytes 6291460
  172.3 53.2 %collective-permute-start.3 = (bf16[64,8192]{1,0:T(8,128)(2,1)S(1)}, bf16[64,8192]{1,0:T(8,128)(2,1)}, u32[]{:S(2)}, u32[]{:S(2)}) collective-permute-start(bf16[64,8192]{1,0:T(8,128)(2,1)S(1)} %get-tuple-element.20), channel_id=1, source_target_pairs={{0,32},{32,0},{64,96},{96,64},{1,33},{33,1},{65,97},{97,65},{2,34}... | collective-permute-start | bytes 3145736 | tf_op jit(solution)/shard_map/ppermute | solution.py:227
  197.2 12.8 %copy-start = (bf16[64,8192]{1,0:T(8,128)(2,1)S(1)}, bf16[64,8192]{1,0:T(8,128)(2,1)}, u32[]{:S(2)}) copy-start(bf16[64,8192]{1,0:T(8,128)(2,1)} %broadcast_select_fusion.2.upstream_ref) | copy-start | bytes 3145732
  212.4 33.8 %collective-permute-start.7 = (bf16[64,8192]{1,0:T(8,128)(2,1)S(1)}, bf16[64,8192]{1,0:T(8,128)(2,1)S(1)}, u32[]{:S(2)}, u32[]{:S(2)}) collective-permute-start(bf16[64,8192]{1,0:T(8,128)(2,1)S(1)} %get-tuple-element.18), channel_id=1, source_target_pairs={{0,32},{32,0},{64,96},{96,64},{1,33},{33,1},{65,97},{97,65},{2,34}... | collective-permute-start | bytes 3145736 | tf_op jit(solution)/shard_map/ppermute | solution.py:227
  213.2 8.2 %copy-start.7 = (bf16[64,512]{1,0:T(8,128)(2,1)S(1)}, bf16[64,512]{1,0:T(8,128)(2,1)}, u32[]{:S(2)}) copy-start(bf16[64,512]{1,0:T(8,128)(2,1)} %get-tuple-element.16) | copy-start | bytes 196612
  213.2 11.7 %copy-start.4 = (bf16[2,64,512]{2,1,0:T(8,128)(2,1)S(1)}, bf16[2,64,512]{2,1,0:T(8,128)(2,1)}, u32[]{:S(2)}) copy-start(bf16[2,64,512]{2,1,0:T(8,128)(2,1)} %get-tuple-element.17) | copy-start | bytes 393220
  222.9 15.2 %collective-permute-start.5 = (bf16[64,512]{1,0:T(8,128)(2,1)S(1)}, bf16[64,512]{1,0:T(8,128)(2,1)S(1)}, u32[]{:S(2)}, u32[]{:S(2)}) collective-permute-start(bf16[64,512]{1,0:T(8,128)(2,1)S(1)} %get-tuple-element.26), channel_id=1, source_target_pairs={{0,32},{32,0},{64,96},{96,64},{1,33},{33,1},{65,97},{97,65},{2,34}... | collective-permute-start | bytes 196616 | tf_op jit(solution)/shard_map/ppermute | solution.py:227
  225.5 20.7 %collective-permute-start.6 = (bf16[64,512]{1,0:T(8,128)(2,1)S(1)}, bf16[64,512]{1,0:T(8,128)(2,1)S(1)}, u32[]{:S(2)}, u32[]{:S(2)}) collective-permute-start(bf16[64,512]{1,0:T(8,128)(2,1)S(1)} %get-tuple-element.24), channel_id=1, source_target_pairs={{0,32},{32,0},{64,96},{96,64},{1,33},{33,1},{65,97},{97,65},{2,34}... | collective-permute-start | bytes 196616 | tf_op jit(solution)/shard_map/ppermute | solution.py:227
  238.1 0.6 copy-start.6
  246.2 0.6 copy-start.5
  246.2 1.0 copy-start.3
Sparse Core Ops, SparseCore 0:
  19.7 85.2 all-gather.3
  254.9 95.1 reduce-scatter.1

commit v4 on v3

--- a/solution.py
+++ b/solution.py
@@ -16,13 +16,16 @@
 EPS = 1e-05
 CHUNK = 1024
 BLOCKS = CHUNK // BLOCK
-SPAN = 1024
 NT = (((1,), (1,)), ((), ()))
 NN = (((1,), (0,)), ((), ()))
 TN = (((0,), (0,)), ((), ()))
 PAIR = [(0, 1), (1, 0), (2, 3), (3, 2)]
 UP = [(0, 3), (1, 2)]
 DOWN = [(3, 0), (2, 1)]
+RING = 4
+Y = 2
+Z = 8
+CORES = [(i, i ^ 1) for i in range(Z * RING)]
 
 
 def dot(left, right, dims):
@@ -159,55 +162,65 @@
     )
 
 
-def pick(places_ref, dense, out_ref, base):
-    owners, slots = out_ref.shape[0], out_ref.shape[2]
-
-    for owner in range(owners):
-        for slot in range(slots):
-            out_ref[owner, 0, slot] = dense[places_ref[base + owner * slots + slot]]
-
-
-def gradient_in_kernel(places_ref, own_ref, other_ref, dpre_own_ref, dpre_other_ref, out_ref, dense):
+def pick(places_ref, dense, keep_ref, send_ref):
     step = pl.program_id(0)
-
-    @pl.when(step == 0)
+    pieces, slots = keep_ref.shape[1], keep_ref.shape[2]
+    count = places_ref.shape[0] // 2
+    for half, out_ref in enumerate((keep_ref, send_ref)):
+        for piece in range(pieces):
+            for slot in range(slots):
+                index = half * count + step * pieces * slots + piece * slots + slot
+                out_ref[0, piece, slot] = dense[places_ref[index]]
+
+
+def gradient_in_kernel(places_ref, own_ref, other_ref, dpre_own_ref, dpre_other_ref, keep_ref, send_ref, dense):
+    @pl.when(pl.program_id(0) == 0)
     def _():
         dense[NBLK] = jnp.zeros((BLOCK, BLOCK), jnp.bfloat16)
-
         dpre = jnp.concatenate([dpre_own_ref[...], dpre_other_ref[...]], axis=0)
-        for chunk in range(D // SPAN):
-            cols = slice(chunk * SPAN, (chunk + 1) * SPAN)
+        for chunk, cols in chunks():
             normed = jnp.concatenate([own_ref[:, cols], other_ref[:, cols]], axis=0)
             part = dot(normed, dpre, TN).astype(jnp.bfloat16)
-            for row in range(SPAN // BLOCK):
+            for row in range(BLOCKS):
                 for col in range(ROWS_K):
-                    dense[(chunk * (SPAN // BLOCK) + row) * ROWS_K + col] = part[
+                    dense[(chunk * BLOCKS + row) * ROWS_K + col] = part[
                         row * BLOCK : (row + 1) * BLOCK, col * BLOCK : (col + 1) * BLOCK
                     ]
 
-    pick(places_ref, dense, out_ref, step * out_ref.shape[0] * out_ref.shape[2])
-
-
-def gradient_out_kernel(places_ref, _, act_own_ref, act_other_ref, own_ref, other_ref, out_ref, dense, turned):
-    step = pl.program_id(0)
-
-    @pl.when(step == 0)
+    pick(places_ref, dense, keep_ref, send_ref)
+
+
+def gradient_out_kernel(places_ref, act_own_ref, act_other_ref, own_ref, other_ref, keep_ref, send_ref, dense, turned):
+    @pl.when(pl.program_id(0) == 0)
     def _():
         dense[NBLK] = jnp.zeros((BLOCK, BLOCK), jnp.bfloat16)
         act = jnp.concatenate([act_own_ref[...], act_other_ref[...]], axis=0)
         turned[...] = act.astype(jnp.float32).T.astype(jnp.bfloat16)
-
-        for chunk in range(D // SPAN):
-            cols = slice(chunk * SPAN, (chunk + 1) * SPAN)
+        for chunk, cols in chunks():
             upstream = jnp.concatenate([own_ref[:, cols], other_ref[:, cols]], axis=0)
             part = dot(turned[...], upstream, NN).astype(jnp.bfloat16)
             for row in range(ROWS_K):
-                for col in range(SPAN // BLOCK):
-                    dense[row * ROWS_D + chunk * (SPAN // BLOCK) + col] = part[
+                for col in range(BLOCKS):
+                    dense[row * ROWS_D + chunk * BLOCKS + col] = part[
                         row * BLOCK : (row + 1) * BLOCK, col * BLOCK : (col + 1) * BLOCK
                     ]
 
-    pick(places_ref, dense, out_ref, (places_ref.shape[0] // 2) + step * out_ref.shape[0] * out_ref.shape[2])
+    pick(places_ref, dense, keep_ref, send_ref)
+
+
+def pair_sum_kernel(keep_ref, arrived_ref, *outs):
+    for piece, out_ref in enumerate(outs):
+        total = keep_ref[piece, 0].astype(jnp.float32) + arrived_ref[piece, 0].astype(jnp.float32)
+        out_ref[0] = total.astype(jnp.bfloat16)
+
+
+def ring_sum_kernel(*refs):
+    terms, outs = refs[:RING], refs[RING:]
+    for piece, out_ref in enumerate(outs):
+        total = terms[0][piece].astype(jnp.float32)
+        for term in terms[1:]:
+            total = total + term[piece].astype(jnp.float32)
+        out_ref[...] = total.astype(jnp.bfloat16)
 
 
 def whole(*shape):
@@ -221,6 +234,21 @@
         ),
         cost_estimate=pl.CostEstimate(flops=flops, bytes_accessed=moved, transcendentals=0),
     )
+
+
+def turn_axis(array, axis, start):
+    size = array.shape[axis]
+    return lax.dynamic_slice_in_dim(jnp.concatenate([array, array], axis), start, size, axis)
+
+
+def around(array, stride, distance):
+    if distance == 0:
+        return array
+    route = []
+    for i in range(lax.axis_size("dp")):
+        place = i // stride % RING
+        route.append((i, i + ((place + distance) % RING - place) * stride))
+    return lax.ppermute(array, "dp", route)
 
 
 def swapped(array):
@@ -245,7 +273,13 @@
     named = places[..., None] == jnp.arange(NBLK, dtype=jnp.int32)
     where = jnp.max(jnp.where(named, codes[..., None], -1), axis=(2, 3)).reshape(-1)
     where = jnp.where(where < 0, owners * 8, where)
-    places = places[0].reshape(-1)
+    me = lax.axis_index("dp")
+    mine = places[0].reshape(2, RING, RING, 2, slots)
+    mine = turn_axis(mine, 1, me // Z)
+    mine = turn_axis(mine, 2, (me // Y) % RING)
+    mine = turn_axis(mine, 3, me % Y)
+    places_in = mine[0].transpose(2, 1, 0, 3).reshape(-1)
+    places_out = mine[1].transpose(2, 0, 1, 3).reshape(-1)
 
     first_tokens = lax.dynamic_slice_in_dim(tokens, half, rows, 0)
     last_grads = lax.dynamic_slice_in_dim(cotangent, half, rows, 0)
@@ -325,43 +359,60 @@
             **params((1 if last else 2) * work, moved // 4 * (1 if last else 2)),
         )
 
-    steps = 4
-    part = (owners // steps, 1, slots, BLOCK, BLOCK)
-    partial_shape = shape(owners, 2, slots, BLOCK, BLOCK)
+    halves = shape(RING, RING, slots, BLOCK, BLOCK)
+    half_spec = pl.BlockSpec((1, RING, slots, BLOCK, BLOCK), lambda step, _: (step, 0, 0, 0, 0))
     dense = pltpu.VMEM((NBLK + 1, BLOCK, BLOCK), jnp.bfloat16)
-    gradient_in = pl.pallas_call(
-        gradient_in_kernel,
-        out_shape=partial_shape,
-        grid_spec=pltpu.PrefetchScalarGridSpec(
-            num_scalar_prefetch=1,
-            grid=(steps,),
-            in_specs=[whole(rows, D), whole(rows, D), whole(rows, RANK), whole(rows, RANK)],
-            out_specs=pl.BlockSpec(part, lambda step, _: (step, 0, 0, 0, 0)),
-            scratch_shapes=[dense],
-        ),
-        name="gradient_in",
-        **params(2 * work, moved // 4),
-    )
-    gradient_out = pl.pallas_call(
+
+    def gradient(kernel, name, in_specs, scratch):
+        return pl.pallas_call(
+            kernel,
+            out_shape=(halves, halves),
+            grid_spec=pltpu.PrefetchScalarGridSpec(
+                num_scalar_prefetch=1,
+                grid=(RING,),
+                in_specs=in_specs,
+                out_specs=(half_spec, half_spec),
+                scratch_shapes=[dense] + scratch,
+            ),
+            name=name,
+            **params(2 * work, moved // 4),
+        )
+
+    gradient_in = gradient(
+        gradient_in_kernel, "gradient_in", [whole(rows, D)] * 2 + [whole(rows, RANK)] * 2, []
+    )
+    gradient_out = gradient(
         gradient_out_kernel,
-        out_shape=partial_shape,
-        grid_spec=pltpu.PrefetchScalarGridSpec(
-            num_scalar_prefetch=1,
-            grid=(steps,),
-            in_specs=[
-                pl.BlockSpec(memory_space=pl.ANY),
-                whole(rows, RANK),
-                whole(rows, RANK),
-                whole(rows, D),
-                whole(rows, D),
-            ],
-            out_specs=pl.BlockSpec(part, lambda step, _: (step, 1, 0, 0, 0)),
-            scratch_shapes=[dense, pltpu.VMEM((RANK, 2 * rows), jnp.bfloat16)],
-        ),
-        input_output_aliases={1: 0},
-        name="gradient_out",
-        **params(2 * work, moved // 4),
-    )
+        "gradient_out",
+        [whole(rows, RANK)] * 2 + [whole(rows, D)] * 2,
+        [pltpu.VMEM((RANK, 2 * rows), jnp.bfloat16)],
+    )
+    column_spec = pl.BlockSpec((RING, 1, slots, BLOCK, BLOCK), lambda step: (0, step, 0, 0, 0))
+    pair_sum = pl.pallas_call(
+        pair_sum_kernel,
+        out_shape=(shape(RING, slots, BLOCK, BLOCK),) * RING,
+        grid=(RING,),
+        in_specs=[column_spec] * 2,
+        out_specs=(pl.BlockSpec((1, slots, BLOCK, BLOCK), lambda step: (step, 0, 0, 0)),) * RING,
+        name="pair_sum",
+        **params(0, moved // 5),
+    )
+    ring_sum = pl.pallas_call(
+        ring_sum_kernel,
+        out_shape=(shape(slots, BLOCK, BLOCK),) * RING,
+        grid=(1,),
+        in_specs=[whole(RING, slots, BLOCK, BLOCK)] * RING,
+        out_specs=(whole(slots, BLOCK, BLOCK),) * RING,
+        name="ring_sum",
+        **params(0, moved // 8),
+    )
+
+    def scattered(gradient_halves, near, far):
+        keep, send = gradient_halves
+        pieces = pair_sum(keep, lax.ppermute(send, "dp", CORES))
+        pieces = ring_sum(*[around(piece, near, distance) for distance, piece in enumerate(pieces)])
+        terms = [around(piece, far, distance).astype(jnp.float32) for distance, piece in enumerate(pieces)]
+        return sum(terms).astype(jnp.bfloat16)[None]
 
     arrived = lax.ppermute(forward(swap, where, first_tokens, weights), "section", UP)
     first = jnp.where(upper, arrived, first_tokens)
@@ -378,10 +429,9 @@
     dpre_other = swapped(jnp.where(odd == 0, dpre_high, dpre_low))
     dpre_own = jnp.where(odd == 0, dpre_low, dpre_high)
 
-    partial = gradient_in(places, normed[0], normed_other, dpre_own, dpre_other)
-    partial = gradient_out(places, partial, act[0], act_other, grads_own, grads_other)
-    summed = lax.psum_scatter(partial, "dp", scatter_dimension=0, tiled=False)
-    return (summed[0][None], summed[1][None])
+    sums_in = scattered(gradient_in(places_in, normed[0], normed_other, dpre_own, dpre_other), Y, Z)
+    sums_out = scattered(gradient_out(places_out, act[0], act_other, grads_own, grads_other), Z, Y)
+    return (sums_in, sums_out)
 
 
 def solution(mesh):

time: 359 us -> 348 us (0.969); the launches traced: 359 us -> 341 us
  waiting for transfers between devices: 215 us -> 148 us
  starting transfers between devices: 12 us -> 42.3 us
  Pallas kernels: 70.2 us -> 84.6 us
    reduce_scatter x1 -> x0, waiting for transfers between devices: 95.3 us -> none  [per_device(): summed = lax.psum_scatter(partial, 'dp', scatter_dimension=0, tiled=False)]
    ppermute x0 -> x14, starting transfers between devices: none -> 29.9 us  [the longest x12 29.6 us: around(): return lax.ppermute(array, 'dp', route)]
    ppermute x0 -> x14, waiting for transfers between devices: none -> 23 us  [the longest x12 23 us: around(): return lax.ppermute(array, 'dp', route)]
    pallas_call x2 -> x6, Pallas kernels: 15 us -> 29.5 us  [the longest x2 9.16 us: scattered(): pieces = pair_sum(keep, lax.ppermute(send, 'dp', CORES))]
    unnamed x22 -> x40, local copies, waits for them, and re-layouts: 2.73 us -> 7.24 us
    ppermute x6, waiting for transfers between devices: 21 us -> 24.7 us  [swapped(): return lax.ppermute(array, 'section', PAIR)]
  transfers between devices with their start and end apart: 10 -> 23, of which waited for: 7 -> 13; matrix products, arithmetic and copies ran while one was open for 4% -> 4% of each run, Pallas kernels for 8% -> 15%
where the time goes in v4:
time: 348 us; the launch traced here: 341 us
  waiting for transfers between devices  148 us (43%)
  Pallas kernels  84.6 us (24%)
  starting transfers between devices  42.3 us (12%)
  blocking collectives  25.9 us (7%)
  local copies, waits for them, and re-layouts  15.1 us (4%)
  between operations  14.7 us (4%)
  other arithmetic  11 us (3%)
    all_gather x1, waiting for transfers between devices, per_device(): weights = lax.all_gather(jnp.stack([own, swapped(own)]), 'dp', axis=0)  54.8 us
    ppermute x12, starting transfers between devices, around(): return lax.ppermute(array, 'dp', route)  29.6 us
    all_gather x1, blocking collectives, per_device(): lax.all_gather(jnp.stack([own_places, swapped(own_places)]), 'dp', axis=0)  25.9 us
    ppermute x6, waiting for transfers between devices, swapped(): return lax.ppermute(array, 'section', PAIR)  24.7 us
    ppermute x1, waiting for transfers between devices, per_device(): arrived = lax.ppermute(leaving, 'section', DOWN)  23.4 us
    ppermute x12, waiting for transfers between devices, around(): return lax.ppermute(array, 'dp', route)  23 us
    pallas_call x1, Pallas kernels, per_device(): turn(swap, where, first, last_grads, weights)  22 us
    ppermute x1, waiting for transfers between devices, per_device(): lax.ppermute(forward(swap, where, first_tokens, weights), 'section', UP)  21.7 us
  transfers between devices with their start and end apart: 23, of which 13 were waited for; matrix products, arithmetic and copies ran while one was open for 4% of the time, Pallas kernels for 15%

profile of v4, /device:TPU:0, one launch (start us, length us, event | category | flops | bytes accessed | tf_op | source)
XLA Modules:
  0.0 341.4 jit_solution(11378949171770392593)
XLA Ops:
  10.9 7.7 %collective-permute-done.1 = bf16[2,5,128,128]{3,2,1,0:T(8,128)(2,1)S(1)} collective-permute-done((bf16[2,5,128,128]{3,2,1,0:T(8,128)(2,1)S(1)}, bf16[2,5,128,128]{3,2,1,0:T(8,128)(2,1)S(1)}, u32[]{:S(2)}, u32[]{:S(2)}) %collective-permute-start.1) | collective-permute-done | bytes 327712 | tf_op jit(solution)/shard_map/ppermute | solution.py:255
  19.6 1.8 collective-permute-start
  23.3 25.9 %all-gather = s32[64,2,5]{2,1,0:T(2,128)S(1)} all-gather(s32[2,2,5]{2,1,0:T(2,128)S(1)} %pad_add_fusion), channel_id=2, replica_groups=mesh['section'=4,'dp'=32] {'dp'}, dimensions={0}, use_global_device_ids=true | all-gather | bytes 2640 | tf_op jit(solution)/shard_map/all_gather | solution.py:271
  50.1 54.8 %all-gather.4.cloned.1.call-done = bf16[64,2,5,128,128]{4,3,2,1,0:T(8,128)(2,1)} async-done(((bf16[2,2,5,128,128]{4,3,2,1,0:T(8,128)(2,1)}), bf16[64,2,5,128,128]{4,3,2,1,0:T(8,128)(2,1)}) %all-gather.4.cloned.1.call-update) | async-done | bytes 20971536 | tf_op jit(solution)/shard_map/all_gather | solution.py:269
  104.9 12.2 %forward_layers.1 = bf16[64,8192]{1,0:T(8,128)(2,1)} custom-call(s32[1]{0:T(128)} %bitcast.7.swap_ref, s32[1024]{0:T(1024)} %compare_select_fusion.where_ref, bf16[64,8192]{1,0:T(8,128)(2,1)} %constant_dynamic-slice_fusion.1.first_ref, bf16[32,2,2,5,128,128]{5,4,3,2,1,0:T(8,128)(2,1)} %bitcast.33), custom_call_target="tpu_custom_call" | custom-call | flops 2147483648 | bytes 20971520 | tf_op jit(solution)/shard_map/forward_layers/pallas_call | solution.py:417
  117.1 4.8 %collective-permute-start.2 = (bf16[64,8192]{1,0:T(8,128)(2,1)}, bf16[64,8192]{1,0:T(8,128)(2,1)S(1)}, u32[]{:S(2)}, u32[]{:S(2)}) collective-permute-start(bf16[64,8192]{1,0:T(8,128)(2,1)} %forward_layers.1), channel_id=1, source_target_pairs={{0,96},{32,64},{1,97},{33,65},{2,98},{34,66},{3,99},{35,67},{4,100... | collective-permute-start | bytes 3145736 | tf_op jit(solution)/shard_map/ppermute | solution.py:417
  123.1 21.7 %collective-permute-done.2 = bf16[64,8192]{1,0:T(8,128)(2,1)S(1)} collective-permute-done((bf16[64,8192]{1,0:T(8,128)(2,1)}, bf16[64,8192]{1,0:T(8,128)(2,1)S(1)}, u32[]{:S(2)}, u32[]{:S(2)}) %collective-permute-start.2) | collective-permute-done | bytes 1048608 | tf_op jit(solution)/shard_map/ppermute | solution.py:417
  146.0 22.0 %turn_layers.1 = (bf16[64,8192]{1,0:T(8,128)(2,1)}, f32[2,64,512]{2,1,0:T(8,128)}, f32[2,64,128]{2,1,0:T(8,128)}, bf16[2,64,8192]{2,1,0:T(8,128)(2,1)}, bf16[2,6...) custom-call(s32[1]{0:T(128)} %bitcast.7.swap_ref, s32[1024]{0:T(1024)} %compare_select_fusion.where_ref, ...), custom_call_target="tpu_custom_call" | custom-call | flops 3758096384 | bytes 20971520 | tf_op jit(solution)/shard_map/turn_layers/pallas_call | solution.py:419
  169.4 2.7 slice_bitcast_fusion
  172.5 23.4 %collective-permute-done.4 = bf16[64,8192]{1,0:T(8,128)(2,1)S(1)} collective-permute-done((bf16[64,8192]{1,0:T(8,128)(2,1)}, bf16[64,8192]{1,0:T(8,128)(2,1)S(1)}, u32[]{:S(2)}, u32[]{:S(2)}) %collective-permute-start.4) | collective-permute-done | bytes 1048608 | tf_op jit(solution)/shard_map/ppermute | solution.py:420
  197.1 12.7 %backward_layer_1.1 = (bf16[64,512]{1,0:T(8,128)(2,1)}, bf16[64,8192]{1,0:T(8,128)(2,1)}) custom-call(s32[1]{0:T(128)} %bitcast.7.swap_ref, s32[1024]{0:T(1024)} %compare_select_fusion.where_ref, bf16[64,8192]{1,0:T(8,128)(2,1)} %get-tuple-element.31.hidden_ref, bf16[64,8192]{1,0:T(8,128)(2,1)} %broadcast_select_fusion.2.upstream_ref, ...), custom_call_target="tpu_custom_call" | custom-call | flops 1073741824 | bytes 10485760 | tf_op jit(solution)/shard_map/backward_layer_1/pallas_call | solution.py:425
  209.8 2.8 broadcast_select_fusion
  212.7 8.2 %backward_layer_0.1 = bf16[64,512]{1,0:T(8,128)(2,1)} custom-call(s32[1]{0:T(128)} %bitcast.7.swap_ref, s32[1024]{0:T(1024)} %compare_select_fusion.where_ref, bf16[64,8192]{1,0:T(8,128)(2,1)} %broadcast_select_fusion.3.first_ref.hidden_ref, bf16[64,8192]{1,0:T(8,128)(2,1)} %get-tuple-element.35.upstream_ref, f32[2,64,512]{2,1,0:T(8,128)} %get-tuple-element.33.pre_ref, ...), custom_call_target="tpu_custom_call" | custom-call | flops 536870912 | bytes 5242880 | tf_op jit(solution)/shard_map/backward_layer_0/pallas_call | solution.py:428
  222.4 2.0 collective-permute-start.5
  225.1 12.7 %collective-permute-done.5.dpre_other_ref = bf16[64,512]{1,0:T(8,128)(2,1)S(1)} collective-permute-done((bf16[64,512]{1,0:T(8,128)(2,1)S(1)}, bf16[64,512]{1,0:T(8,128)(2,1)S(1)}, u32[]{:S(2)}, u32[]{:S(2)}) %collective-permute-start.5) | collective-permute-done | bytes 65568 | tf_op jit(solution)/shard_map/ppermute | solution.py:255
  238.5 7.5 %gradient_in.1 = (bf16[4,4,5,128,128]{4,3,2,1,0:T(8,128)(2,1)}, bf16[4,4,5,128,128]{4,3,2,1,0:T(8,128)(2,1)}) custom-call(s32[160]{0:T(256)} %reshape.22.places_ref, bf16[64,8192]{1,0:T(8,128)(2,1)} %get-tuple-element.61.own_ref, bf16[64,8192]{1,0:T(8,128)(2,1)} %copy-done.16, bf16[64,512]{1,0:T(8,128)(2,1)} %get-tuple-element.65.dpre_own_ref, ...), custom_call_target="tpu_custom_call" | custom-call | flops 1073741824 | bytes 5242880 | tf_op jit(solution)/shard_map/gradient_in/pallas_call | solution.py:432
  247.6 3.5 %collective-permute-done.13.act_other_ref = bf16[64,512]{1,0:T(8,128)(2,1)S(1)} collective-permute-done((bf16[64,512]{1,0:T(8,128)(2,1)S(1)}, bf16[64,512]{1,0:T(8,128)(2,1)S(1)}, u32[]{:S(2)}, u32[]{:S(2)}) %collective-permute-start.13) | collective-permute-done | bytes 65568 | tf_op jit(solution)/shard_map/ppermute | solution.py:255
  251.7 7.6 %gradient_out.1 = (bf16[4,4,5,128,128]{4,3,2,1,0:T(8,128)(2,1)}, bf16[4,4,5,128,128]{4,3,2,1,0:T(8,128)(2,1)}) custom-call(s32[160]{0:T(256)} %reshape.25.places_ref, bf16[64,512]{1,0:T(8,128)(2,1)} %get-tuple-element.63.act_own_ref, bf16[64,512]{1,0:T(8,128)(2,1)} %copy-done.18, bf16[64,8192]{1,0:T(8,128)(2,1)} %get-tuple-element.59.own_ref, ...), custom_call_target="tpu_custom_call" | custom-call | flops 1073741824 | bytes 5242880 | tf_op jit(solution)/shard_map/gradient_out/pallas_call | solution.py:433
  261.1 4.6 %pair_sum.2 = (bf16[4,5,128,128]{3,2,1,0:T(8,128)(2,1)}, bf16[4,5,128,128]{3,2,1,0:T(8,128)(2,1)}, bf16[4,5,128,128]{3,2,1,0:T(8,128)(2,1)}, bf16[4,5,128,128]{3,2,1,0:T(8,128)(2,1)}) custom-call(bf16[4,4,5,128,128]{4,3,2,1,0:T(8,128)(2,1)} %get-tuple-element.37.keep_ref, bf16[4,4,5,128,128]{4,3,2,1,0:T(8,128)(2,1)} %copy-done.1), custom_call_target="tpu_custom_call" | custom-call | bytes 4194304 | tf_op jit(solution)/shard_map/pair_sum/pallas_call | solution.py:412
  267.1 2.7 collective-permute-start.8
  272.7 4.6 %pair_sum.3 = (bf16[4,5,128,128]{3,2,1,0:T(8,128)(2,1)}, bf16[4,5,128,128]{3,2,1,0:T(8,128)(2,1)}, bf16[4,5,128,128]{3,2,1,0:T(8,128)(2,1)}, bf16[4,5,128,128]{3,2,1,0:T(8,128)(2,1)}) custom-call(bf16[4,4,5,128,128]{4,3,2,1,0:T(8,128)(2,1)} %get-tuple-element.48.keep_ref, bf16[4,4,5,128,128]{4,3,2,1,0:T(8,128)(2,1)} %copy-done.2), custom_call_target="tpu_custom_call" | custom-call | bytes 4194304 | tf_op jit(solution)/shard_map/pair_sum/pallas_call | solution.py:412
  277.3 2.3 collective-permute-start.17
  279.6 4.6 %collective-permute-done.7.refs_1_ = bf16[4,5,128,128]{3,2,1,0:T(8,128)(2,1)S(1)} collective-permute-done((bf16[4,5,128,128]{3,2,1,0:T(8,128)(2,1)}, bf16[4,5,128,128]{3,2,1,0:T(8,128)(2,1)S(1)}, u32[]{:S(2)}, u32[]{:S(2)}) %collective-permute-start.7) | collective-permute-done | bytes 655392 | tf_op jit(solution)/shard_map/ppermute | solution.py:251
  284.2 16.3 %collective-permute-start.18 = (bf16[4,5,128,128]{3,2,1,0:T(8,128)(2,1)}, bf16[4,5,128,128]{3,2,1,0:T(8,128)(2,1)S(1)}, u32[]{:S(2)}, u32[]{:S(2)}) collective-permute-start(bf16[4,5,128,128]{3,2,1,0:T(8,128)(2,1)} %get-tuple-element.53), channel_id=1, source_target_pairs={{0,24},{1,25},{2,26},{3,27},{4,28},{5,29},{6,30},{7,31},{8,0},{9,1... | collective-permute-start | bytes 1966088 | tf_op jit(solution)/shard_map/ppermute | solution.py:251
  301.6 2.7 ring_sum.2
  304.3 2.2 collective-permute-start.11
  306.5 3.0 collective-permute-done.16.refs_1_
  309.5 10.0 %collective-permute-done.18.refs_3_ = bf16[4,5,128,128]{3,2,1,0:T(8,128)(2,1)S(1)} collective-permute-done((bf16[4,5,128,128]{3,2,1,0:T(8,128)(2,1)}, bf16[4,5,128,128]{3,2,1,0:T(8,128)(2,1)S(1)}, u32[]{:S(2)}, u32[]{:S(2)}) %collective-permute-start.18) | collective-permute-done | bytes 655392 | tf_op jit(solution)/shard_map/ppermute | solution.py:251
  320.4 2.7 ring_sum.3
  323.1 3.2 collective-permute-start.21
  327.1 4.6 %collective-permute-done.19 = bf16[5,128,128]{2,1,0:T(8,128)(2,1)S(1)} collective-permute-done((bf16[5,128,128]{2,1,0:T(8,128)(2,1)}, bf16[5,128,128]{2,1,0:T(8,128)(2,1)S(1)}, u32[]{:S(2)}, u32[]{:S(2)}) %collective-permute-start.19) | collective-permute-done | bytes 163872 | tf_op jit(solution)/shard_map/ppermute | solution.py:251
  332.4 1.7 fusion.1
  (95 shorter events, 27.6 us)
Async XLA Ops:
  7.2 12.4 %copy-start.14 = (s32[1,5]{1,0:T(1,128)S(1)}, s32[1,5]{1,0:T(1,128)}, u32[]{:S(2)}) copy-start(s32[1,5]{1,0:T(1,128)} %param.10) | copy-start | bytes 64
  7.2 12.4 %copy-start.15 = (s32[1,5]{1,0:T(1,128)S(1)}, s32[1,5]{1,0:T(1,128)}, u32[]{:S(2)}) copy-start(s32[1,5]{1,0:T(1,128)} %param.9) | copy-start | bytes 64
  7.2 14.3 %copy-start.3 = (bf16[128,8192]{1,0:T(8,128)(2,1)S(1)}, bf16[128,8192]{1,0:T(8,128)(2,1)}, u32[]{:S(2)}) copy-start(bf16[128,8192]{1,0:T(8,128)(2,1)} %param.6) | copy-start | bytes 6291460
  7.2 97.7 %all-gather.4.cloned.1.call-start = ((), (), s32[]{:S(2)}) async-start(), calls=%async_computation | async-start | bytes 21626880 | tf_op jit(solution)/shard_map/all_gather | solution.py:269
  9.3 9.4 %collective-permute-start.1 = (bf16[2,5,128,128]{3,2,1,0:T(8,128)(2,1)S(1)}, bf16[2,5,128,128]{3,2,1,0:T(8,128)(2,1)S(1)}, u32[]{:S(2)}, u32[]{:S(2)}) collective-permute-start(bf16[2,5,128,128]{3,2,1,0:T(8,128)(2,1)S(1)} %constant_dynamic-update-slice_fusion), channel_id=1, source_target_pairs={{0,32},{32,0},{64,96},{96,64},{1,33},{33,1},{65,97},{97,65},{2,34}... | collective-permute-start | bytes 983048 | tf_op jit(solution)/shard_map/ppermute | solution.py:255
  19.6 3.6 %collective-permute-start = (s32[2,5]{1,0:T(2,128)S(1)}, s32[2,5]{1,0:T(2,128)S(1)}, u32[]{:S(2)}, u32[]{:S(2)}) collective-permute-start(s32[2,5]{1,0:T(2,128)S(1)} %get-tuple-element.69), channel_id=1, source_target_pairs={{0,32},{32,0},{64,96},{96,64},{1,33},{33,1},{65,97},{97,65},{2,34}... | collective-permute-start | bytes 128 | tf_op jit(solution)/shard_map/ppermute | solution.py:255
  104.9 17.0 %copy-start.4 = (bf16[128,8192]{1,0:T(8,128)(2,1)S(1)}, bf16[128,8192]{1,0:T(8,128)(2,1)}, u32[]{:S(2)}) copy-start(bf16[128,8192]{1,0:T(8,128)(2,1)} %param.11) | copy-start | bytes 6291460
  117.1 27.7 %collective-permute-start.2 = (bf16[64,8192]{1,0:T(8,128)(2,1)}, bf16[64,8192]{1,0:T(8,128)(2,1)S(1)}, u32[]{:S(2)}, u32[]{:S(2)}) collective-permute-start(bf16[64,8192]{1,0:T(8,128)(2,1)} %forward_layers.1), channel_id=1, source_target_pairs={{0,96},{32,64},{1,97},{33,65},{2,98},{34,66},{3,99},{35,67},{4,100... | collective-permute-start | bytes 3145736 | tf_op jit(solution)/shard_map/ppermute | solution.py:417
  168.1 27.9 %collective-permute-start.4 = (bf16[64,8192]{1,0:T(8,128)(2,1)}, bf16[64,8192]{1,0:T(8,128)(2,1)S(1)}, u32[]{:S(2)}, u32[]{:S(2)}) collective-permute-start(bf16[64,8192]{1,0:T(8,128)(2,1)} %get-tuple-element.32), channel_id=1, source_target_pairs={{96,0},{64,32},{97,1},{65,33},{98,2},{66,34},{99,3},{67,35},{100,4... | collective-permute-start | bytes 3145736 | tf_op jit(solution)/shard_map/ppermute | solution.py:420
  172.0 53.1 %collective-permute-start.3 = (bf16[64,8192]{1,0:T(8,128)(2,1)S(1)}, bf16[64,8192]{1,0:T(8,128)(2,1)S(1)}, u32[]{:S(2)}, u32[]{:S(2)}) collective-permute-start(bf16[64,8192]{1,0:T(8,128)(2,1)S(1)} %get-tuple-element.60), channel_id=1, source_target_pairs={{0,32},{32,0},{64,96},{96,64},{1,33},{33,1},{65,97},{97,65},{2,34}... | collective-permute-start | bytes 3145736 | tf_op jit(solution)/shard_map/ppermute | solution.py:255
  197.1 12.7 %copy-start = (bf16[64,8192]{1,0:T(8,128)(2,1)S(1)}, bf16[64,8192]{1,0:T(8,128)(2,1)}, u32[]{:S(2)}) copy-start(bf16[64,8192]{1,0:T(8,128)(2,1)} %broadcast_select_fusion.2.upstream_ref) | copy-start | bytes 3145732
  212.6 38.5 %collective-permute-start.14 = (bf16[64,8192]{1,0:T(8,128)(2,1)}, bf16[64,8192]{1,0:T(8,128)(2,1)}, u32[]{:S(2)}, u32[]{:S(2)}) collective-permute-start(bf16[64,8192]{1,0:T(8,128)(2,1)} %get-tuple-element.58), channel_id=1, source_target_pairs={{0,32},{32,0},{64,96},{96,64},{1,33},{33,1},{65,97},{97,65},{2,34}... | collective-permute-start | bytes 3145736 | tf_op jit(solution)/shard_map/ppermute | solution.py:255
  222.4 23.5 %copy-start.12 = (bf16[2,64,512]{2,1,0:T(8,128)(2,1)S(1)}, bf16[2,64,512]{2,1,0:T(8,128)(2,1)}, u32[]{:S(2)}) copy-start(bf16[2,64,512]{2,1,0:T(8,128)(2,1)} %get-tuple-element.47) | copy-start | bytes 393220
  222.4 15.4 %collective-permute-start.5 = (bf16[64,512]{1,0:T(8,128)(2,1)S(1)}, bf16[64,512]{1,0:T(8,128)(2,1)S(1)}, u32[]{:S(2)}, u32[]{:S(2)}) collective-permute-start(bf16[64,512]{1,0:T(8,128)(2,1)S(1)} %get-tuple-element.64), channel_id=1, source_target_pairs={{0,32},{32,0},{64,96},{96,64},{1,33},{33,1},{65,97},{97,65},{2,34}... | collective-permute-start | bytes 196616 | tf_op jit(solution)/shard_map/ppermute | solution.py:255
  225.1 12.7 %copy-start.16 = (bf16[64,8192]{1,0:T(8,128)(2,1)}, bf16[64,8192]{1,0:T(8,128)(2,1)S(1)}, u32[]{:S(2)}) copy-start(bf16[64,8192]{1,0:T(8,128)(2,1)S(1)} %collective-permute-done.3.other_ref) | copy-start | bytes 3145732
  245.9 13.6 %collective-permute-start.6 = (bf16[4,4,5,128,128]{4,3,2,1,0:T(8,128)(2,1)}, bf16[4,4,5,128,128]{4,3,2,1,0:T(8,128)(2,1)S(1)}, u32[]{:S(2)}, u32[]{:S(2)}) collective-permute-start(bf16[4,4,5,128,128]{4,3,2,1,0:T(8,128)(2,1)} %get-tuple-element.38), channel_id=1, source_target_pairs={{0,1},{1,0},{2,3},{3,2},{4,5},{5,4},{6,7},{7,6},{8,9},{9,8},{10,11... | collective-permute-start | bytes 7864328 | tf_op jit(solution)/shard_map/ppermute | solution.py:412
  246.6 4.5 %collective-permute-start.13 = (bf16[64,512]{1,0:T(8,128)(2,1)S(1)}, bf16[64,512]{1,0:T(8,128)(2,1)S(1)}, u32[]{:S(2)}, u32[]{:S(2)}) collective-permute-start(bf16[64,512]{1,0:T(8,128)(2,1)S(1)} %get-tuple-element.62), channel_id=1, source_target_pairs={{0,32},{32,0},{64,96},{96,64},{1,33},{33,1},{65,97},{97,65},{2,34}... | collective-permute-start | bytes 196616 | tf_op jit(solution)/shard_map/ppermute | solution.py:255
  259.3 12.0 %collective-permute-start.15 = (bf16[4,4,5,128,128]{4,3,2,1,0:T(8,128)(2,1)}, bf16[4,4,5,128,128]{4,3,2,1,0:T(8,128)(2,1)S(1)}, u32[]{:S(2)}, u32[]{:S(2)}) collective-permute-start(bf16[4,4,5,128,128]{4,3,2,1,0:T(8,128)(2,1)} %get-tuple-element.49), channel_id=1, source_target_pairs={{0,1},{1,0},{2,3},{3,2},{4,5},{5,4},{6,7},{7,6},{8,9},{9,8},{10,11... | collective-permute-start | bytes 7864328 | tf_op jit(solution)/shard_map/ppermute | solution.py:412
  265.7 18.5 %collective-permute-start.7 = (bf16[4,5,128,128]{3,2,1,0:T(8,128)(2,1)}, bf16[4,5,128,128]{3,2,1,0:T(8,128)(2,1)S(1)}, u32[]{:S(2)}, u32[]{:S(2)}) collective-permute-start(bf16[4,5,128,128]{3,2,1,0:T(8,128)(2,1)} %get-tuple-element.40), channel_id=1, source_target_pairs={{0,2},{1,3},{2,4},{3,5},{4,6},{5,7},{6,0},{7,1},{8,10},{9,11},{10,... | collective-permute-start | bytes 1966088 | tf_op jit(solution)/shard_map/ppermute | solution.py:251
  267.1 33.4 %collective-permute-start.8 = (bf16[4,5,128,128]{3,2,1,0:T(8,128)(2,1)}, bf16[4,5,128,128]{3,2,1,0:T(8,128)(2,1)S(1)}, u32[]{:S(2)}, u32[]{:S(2)}) collective-permute-start(bf16[4,5,128,128]{3,2,1,0:T(8,128)(2,1)} %get-tuple-element.41), channel_id=1, source_target_pairs={{0,4},{1,5},{2,6},{3,7},{4,0},{5,1},{6,2},{7,3},{8,12},{9,13},{10,... | collective-permute-start | bytes 1966088 | tf_op jit(solution)/shard_map/ppermute | solution.py:251
  269.9 30.7 %collective-permute-start.9 = (bf16[4,5,128,128]{3,2,1,0:T(8,128)(2,1)}, bf16[4,5,128,128]{3,2,1,0:T(8,128)(2,1)S(1)}, u32[]{:S(2)}, u32[]{:S(2)}) collective-permute-start(bf16[4,5,128,128]{3,2,1,0:T(8,128)(2,1)} %get-tuple-element.42), channel_id=1, source_target_pairs={{0,6},{1,7},{2,0},{3,1},{4,2},{5,3},{6,4},{7,5},{8,14},{9,15},{10,... | collective-permute-start | bytes 1966088 | tf_op jit(solution)/shard_map/ppermute | solution.py:251
  277.3 32.1 %collective-permute-start.16 = (bf16[4,5,128,128]{3,2,1,0:T(8,128)(2,1)}, bf16[4,5,128,128]{3,2,1,0:T(8,128)(2,1)S(1)}, u32[]{:S(2)}, u32[]{:S(2)}) collective-permute-start(bf16[4,5,128,128]{3,2,1,0:T(8,128)(2,1)} %get-tuple-element.51), channel_id=1, source_target_pairs={{0,8},{1,9},{2,10},{3,11},{4,12},{5,13},{6,14},{7,15},{8,16},{9,17... | collective-permute-start | bytes 1966088 | tf_op jit(solution)/shard_map/ppermute | solution.py:251
  277.3 32.2 %collective-permute-start.17 = (bf16[4,5,128,128]{3,2,1,0:T(8,128)(2,1)}, bf16[4,5,128,128]{3,2,1,0:T(8,128)(2,1)S(1)}, u32[]{:S(2)}, u32[]{:S(2)}) collective-permute-start(bf16[4,5,128,128]{3,2,1,0:T(8,128)(2,1)} %get-tuple-element.52), channel_id=1, source_target_pairs={{0,16},{1,17},{2,18},{3,19},{4,20},{5,21},{6,22},{7,23},{8,24},{9,... | collective-permute-start | bytes 1966088 | tf_op jit(solution)/shard_map/ppermute | solution.py:251
  284.2 16.4 %copy-start.7 = (bf16[4,5,128,128]{3,2,1,0:T(8,128)(2,1)}, bf16[4,5,128,128]{3,2,1,0:T(8,128)(2,1)S(1)}, u32[]{:S(2)}) copy-start(bf16[4,5,128,128]{3,2,1,0:T(8,128)(2,1)S(1)} %collective-permute-done.7.refs_1_) | copy-start | bytes 1966084
  284.2 35.3 %collective-permute-start.18 = (bf16[4,5,128,128]{3,2,1,0:T(8,128)(2,1)}, bf16[4,5,128,128]{3,2,1,0:T(8,128)(2,1)S(1)}, u32[]{:S(2)}, u32[]{:S(2)}) collective-permute-start(bf16[4,5,128,128]{3,2,1,0:T(8,128)(2,1)} %get-tuple-element.53), channel_id=1, source_target_pairs={{0,24},{1,25},{2,26},{3,27},{4,28},{5,29},{6,30},{7,31},{8,0},{9,1... | collective-permute-start | bytes 1966088 | tf_op jit(solution)/shard_map/ppermute | solution.py:251
  304.3 22.0 %copy-start.11 = (bf16[5,128,128]{2,1,0:T(8,128)(2,1)S(1)}, bf16[5,128,128]{2,1,0:T(8,128)(2,1)}, u32[]{:S(2)}) copy-start(bf16[5,128,128]{2,1,0:T(8,128)(2,1)} %get-tuple-element.43) | copy-start | bytes 491524
  304.3 18.8 %collective-permute-start.10 = (bf16[5,128,128]{2,1,0:T(8,128)(2,1)}, bf16[5,128,128]{2,1,0:T(8,128)(2,1)S(1)}, u32[]{:S(2)}, u32[]{:S(2)}) collective-permute-start(bf16[5,128,128]{2,1,0:T(8,128)(2,1)} %get-tuple-element.44), channel_id=1, source_target_pairs={{0,8},{1,9},{2,10},{3,11},{4,12},{5,13},{6,14},{7,15},{8,16},{9,17... | collective-permute-start | bytes 491528 | tf_op jit(solution)/shard_map/ppermute | solution.py:251
  304.3 22.0 %collective-permute-start.11 = (bf16[5,128,128]{2,1,0:T(8,128)(2,1)}, bf16[5,128,128]{2,1,0:T(8,128)(2,1)S(1)}, u32[]{:S(2)}, u32[]{:S(2)}) collective-permute-start(bf16[5,128,128]{2,1,0:T(8,128)(2,1)} %get-tuple-element.45), channel_id=1, source_target_pairs={{0,16},{1,17},{2,18},{3,19},{4,20},{5,21},{6,22},{7,23},{8,24},{9,... | collective-permute-start | bytes 491528 | tf_op jit(solution)/shard_map/ppermute | solution.py:251
  309.5 16.8 %collective-permute-start.12 = (bf16[5,128,128]{2,1,0:T(8,128)(2,1)}, bf16[5,128,128]{2,1,0:T(8,128)(2,1)S(1)}, u32[]{:S(2)}, u32[]{:S(2)}) collective-permute-start(bf16[5,128,128]{2,1,0:T(8,128)(2,1)} %get-tuple-element.46), channel_id=1, source_target_pairs={{0,24},{1,25},{2,26},{3,27},{4,28},{5,29},{6,30},{7,31},{8,0},{9,1... | collective-permute-start | bytes 491528 | tf_op jit(solution)/shard_map/ppermute | solution.py:251
  323.0 8.6 %collective-permute-start.19 = (bf16[5,128,128]{2,1,0:T(8,128)(2,1)}, bf16[5,128,128]{2,1,0:T(8,128)(2,1)S(1)}, u32[]{:S(2)}, u32[]{:S(2)}) collective-permute-start(bf16[5,128,128]{2,1,0:T(8,128)(2,1)} %get-tuple-element.55), channel_id=1, source_target_pairs={{0,2},{1,3},{2,4},{3,5},{4,6},{5,7},{6,0},{7,1},{8,10},{9,11},{10,... | collective-permute-start | bytes 491528 | tf_op jit(solution)/shard_map/ppermute | solution.py:251
  323.0 8.6 %collective-permute-start.20 = (bf16[5,128,128]{2,1,0:T(8,128)(2,1)}, bf16[5,128,128]{2,1,0:T(8,128)(2,1)S(1)}, u32[]{:S(2)}, u32[]{:S(2)}) collective-permute-start(bf16[5,128,128]{2,1,0:T(8,128)(2,1)} %get-tuple-element.56), channel_id=1, source_target_pairs={{0,4},{1,5},{2,6},{3,7},{4,0},{5,1},{6,2},{7,3},{8,12},{9,13},{10,... | collective-permute-start | bytes 491528 | tf_op jit(solution)/shard_map/ppermute | solution.py:251
  323.1 9.4 %collective-permute-start.21 = (bf16[5,128,128]{2,1,0:T(8,128)(2,1)}, bf16[5,128,128]{2,1,0:T(8,128)(2,1)S(1)}, u32[]{:S(2)}, u32[]{:S(2)}) collective-permute-start(bf16[5,128,128]{2,1,0:T(8,128)(2,1)} %get-tuple-element.57), channel_id=1, source_target_pairs={{0,6},{1,7},{2,0},{3,1},{4,2},{5,3},{6,4},{7,5},{8,14},{9,15},{10,... | collective-permute-start | bytes 491528 | tf_op jit(solution)/shard_map/ppermute | solution.py:251
  (10 other events, 35.3 us)
Sparse Core Ops, SparseCore 0:
  19.7 85.1 all-gather.3

commit v5 on v4

--- a/solution.py
+++ b/solution.py
@@ -132,10 +132,11 @@
 
 
 def turn_kernel(
-    swap_ref, where_ref, first_ref, grad_ref, source, second_ref, pre_ref, inverse_ref, normed_ref, act_ref, earlier_ref, middle_ref, held, sems
+    swap_ref, where_ref, tokens_ref, arrived_ref, grad_ref, source, second_ref, pre_ref, inverse_ref, normed_ref, act_ref, earlier_ref, first_ref, middle_ref, held, sems
 ):
     weights = Weights(swap_ref, where_ref, source, held, sems, [(0, 0), (0, 1), (1, 0), (1, 1)])
-    pres, inverses = [], []
+    for _, cols in chunks():
+        first_ref[:, cols] = lax.select(swap_ref[1] > 0, arrived_ref[:, cols], tokens_ref[:, cols])
     for layer, hidden_ref in enumerate((first_ref, second_ref)):
         place = layer ^ swap_ref[0]
         pre, inverse = forward_down(weights, layer, hidden_ref, normed_ref.at[place])
@@ -150,16 +151,33 @@
     backward(weights, 0, first_ref, middle_ref, pre_ref[0], inverse_ref[0][:, :1], earlier_ref)
 
 
-def backward_kernel(
-    layer, last, swap_ref, where_ref, hidden_ref, upstream_ref, pre_ref, inverse_ref, source, *outs
+def high_kernel(
+    swap_ref, where_ref, hidden_ref, grad_ref, arrived_ref, pre_ref, inverse_ref, source, dpre_ref, middle_ref, own_ref, early_ref, late_ref, upstream_ref, held, sems
 ):
-    held, sems = outs[-2:]
-    weights = Weights(swap_ref, where_ref, source, held, sems, [(layer, 1)] if last else [(layer, 1), (layer, 0)])
-    for matrix in [1] if last else [1, 0]:
-        weights.wait(layer, matrix)
-    outs[0][...] = backward(
-        weights, layer, hidden_ref, upstream_ref, pre_ref[layer], inverse_ref[layer][:, :1], None if last else outs[1]
-    )
+    weights = Weights(swap_ref, where_ref, source, held, sems, [(1, 1), (1, 0)])
+    rows = early_ref.shape[0]
+    even = swap_ref[0] == 0
+    for _, cols in chunks():
+        upstream_ref[:, cols] = lax.select(swap_ref[1] > 0, grad_ref[:, cols], arrived_ref[:, cols])
+    weights.wait(1, 1)
+    weights.wait(1, 0)
+    dpre_ref[...] = backward(weights, 1, hidden_ref, upstream_ref, pre_ref[1], inverse_ref[1][:, :1], middle_ref)
+    for _, cols in chunks():
+        upper, lower = upstream_ref[:, cols], middle_ref[:, cols]
+        own_ref[:, cols] = lax.select(even, lower, upper)
+        sent = lax.select(even, upper, lower)
+        early_ref[:, cols] = sent[:rows]
+        late_ref[:, cols] = sent[rows:]
+
+
+def low_kernel(swap_ref, where_ref, middle_ref, high_ref, pre_ref, source, own_ref, sent_ref, held, sems):
+    weights = Weights(swap_ref, where_ref, source, held, sems, [(0, 1)])
+    even = swap_ref[0] == 0
+    weights.wait(0, 1)
+    low = backward(weights, 0, None, middle_ref, pre_ref[0], None, None)
+    high = high_ref[...]
+    own_ref[...] = lax.select(even, low, high)
+    sent_ref[...] = lax.select(even, high, low)
 
 
 def pick(places_ref, dense, keep_ref, send_ref):
@@ -190,14 +208,16 @@
     pick(places_ref, dense, keep_ref, send_ref)
 
 
-def gradient_out_kernel(places_ref, act_own_ref, act_other_ref, own_ref, other_ref, keep_ref, send_ref, dense, turned):
+def gradient_out_kernel(
+    places_ref, act_own_ref, act_other_ref, own_ref, early_ref, late_ref, keep_ref, send_ref, dense, turned
+):
     @pl.when(pl.program_id(0) == 0)
     def _():
         dense[NBLK] = jnp.zeros((BLOCK, BLOCK), jnp.bfloat16)
         act = jnp.concatenate([act_own_ref[...], act_other_ref[...]], axis=0)
         turned[...] = act.astype(jnp.float32).T.astype(jnp.bfloat16)
         for chunk, cols in chunks():
-            upstream = jnp.concatenate([own_ref[:, cols], other_ref[:, cols]], axis=0)
+            upstream = jnp.concatenate([own_ref[:, cols], early_ref[:, cols], late_ref[:, cols]], axis=0)
             part = dot(turned[...], upstream, NN).astype(jnp.bfloat16)
             for row in range(ROWS_K):
                 for col in range(BLOCKS):
@@ -206,21 +226,6 @@
                     ]
 
     pick(places_ref, dense, keep_ref, send_ref)
-
-
-def pair_sum_kernel(keep_ref, arrived_ref, *outs):
-    for piece, out_ref in enumerate(outs):
-        total = keep_ref[piece, 0].astype(jnp.float32) + arrived_ref[piece, 0].astype(jnp.float32)
-        out_ref[0] = total.astype(jnp.bfloat16)
-
-
-def ring_sum_kernel(*refs):
-    terms, outs = refs[:RING], refs[RING:]
-    for piece, out_ref in enumerate(outs):
-        total = terms[0][piece].astype(jnp.float32)
-        for term in terms[1:]:
-            total = total + term[piece].astype(jnp.float32)
-        out_ref[...] = total.astype(jnp.bfloat16)
 
 
 def whole(*shape):
@@ -251,6 +256,10 @@
     return lax.ppermute(array, "dp", route)
 
 
+def rounded_sum(*terms):
+    return sum(term.astype(jnp.float32) for term in terms).astype(jnp.bfloat16)
+
+
 def swapped(array):
     return lax.ppermute(array, "section", PAIR)
 
@@ -261,8 +270,7 @@
     slots = blocks_in.shape[1]
     rows = tokens.shape[0] // 2
     odd = here % 2
-    swap = odd.astype(jnp.int32).reshape(1)
-    upper = here >= 2
+    swap = jnp.stack([odd, here // 2]).astype(jnp.int32)
     half = jnp.where((here == 1) | (here == 2), rows, 0)
 
     own = jnp.stack([blocks_in[0], blocks_out[0]])
@@ -323,7 +331,7 @@
         grid_spec=pltpu.PrefetchScalarGridSpec(
             num_scalar_prefetch=2,
             grid=(1,),
-            in_specs=[whole(rows, D), whole(rows, D), anywhere],
+            in_specs=[whole(rows, D)] * 3 + [anywhere],
             out_specs=[
                 whole(rows, D),
                 whole(2, rows, RANK),
@@ -332,32 +340,38 @@
                 whole(2, rows, RANK),
                 whole(rows, D),
             ],
-            scratch_shapes=[pltpu.VMEM((rows, D), jnp.bfloat16)] + held(4),
+            scratch_shapes=[pltpu.VMEM((rows, D), jnp.bfloat16)] * 2 + held(4),
         ),
         name="turn_layers",
         **params(7 * work, moved),
     )
 
-    def backward_layer(layer, last):
-        return pl.pallas_call(
-            functools.partial(backward_kernel, layer, last),
-            out_shape=(shape(rows, RANK),) + (() if last else (shape(rows, D),)),
-            grid_spec=pltpu.PrefetchScalarGridSpec(
-                num_scalar_prefetch=2,
-                grid=(1,),
-                in_specs=[
-                    whole(rows, D),
-                    whole(rows, D),
-                    whole(2, rows, RANK),
-                    whole(2, rows, BLOCK),
-                    anywhere,
-                ],
-                out_specs=[whole(rows, RANK)] + ([] if last else [whole(rows, D)]),
-                scratch_shapes=held(1 if last else 2),
-            ),
-            name=f"backward_layer_{layer}",
-            **params((1 if last else 2) * work, moved // 4 * (1 if last else 2)),
-        )
+    high = pl.pallas_call(
+        high_kernel,
+        out_shape=(shape(rows, RANK), shape(rows, D), shape(rows, D), shape(rows // 2, D), shape(rows // 2, D)),
+        grid_spec=pltpu.PrefetchScalarGridSpec(
+            num_scalar_prefetch=2,
+            grid=(1,),
+            in_specs=[whole(rows, D)] * 3 + [whole(2, rows, RANK), whole(2, rows, BLOCK), anywhere],
+            out_specs=[whole(rows, RANK)] + [whole(rows, D)] * 2 + [whole(rows // 2, D)] * 2,
+            scratch_shapes=[pltpu.VMEM((rows, D), jnp.bfloat16)] + held(2),
+        ),
+        name="backward_high",
+        **params(2 * work, moved // 2),
+    )
+    low = pl.pallas_call(
+        low_kernel,
+        out_shape=(shape(rows, RANK), shape(rows, RANK)),
+        grid_spec=pltpu.PrefetchScalarGridSpec(
+            num_scalar_prefetch=2,
+            grid=(1,),
+            in_specs=[whole(rows, D), whole(rows, RANK), whole(2, rows, RANK), anywhere],
+            out_specs=[whole(rows, RANK)] * 2,
+            scratch_shapes=held(1),
+        ),
+        name="backward_low",
+        **params(0, 0),
+    )
 
     halves = shape(RING, RING, slots, BLOCK, BLOCK)
     half_spec = pl.BlockSpec((1, RING, slots, BLOCK, BLOCK), lambda step, _: (step, 0, 0, 0, 0))
@@ -375,7 +389,7 @@
                 scratch_shapes=[dense] + scratch,
             ),
             name=name,
-            **params(2 * work, moved // 4),
+            **params(0, 0),
         )
 
     gradient_in = gradient(
@@ -384,53 +398,35 @@
     gradient_out = gradient(
         gradient_out_kernel,
         "gradient_out",
-        [whole(rows, RANK)] * 2 + [whole(rows, D)] * 2,
+        [whole(rows, RANK)] * 2 + [whole(rows, D)] + [whole(rows // 2, D)] * 2,
         [pltpu.VMEM((RANK, 2 * rows), jnp.bfloat16)],
     )
-    column_spec = pl.BlockSpec((RING, 1, slots, BLOCK, BLOCK), lambda step: (0, step, 0, 0, 0))
-    pair_sum = pl.pallas_call(
-        pair_sum_kernel,
-        out_shape=(shape(RING, slots, BLOCK, BLOCK),) * RING,
-        grid=(RING,),
-        in_specs=[column_spec] * 2,
-        out_specs=(pl.BlockSpec((1, slots, BLOCK, BLOCK), lambda step: (step, 0, 0, 0)),) * RING,
-        name="pair_sum",
-        **params(0, moved // 5),
-    )
-    ring_sum = pl.pallas_call(
-        ring_sum_kernel,
-        out_shape=(shape(slots, BLOCK, BLOCK),) * RING,
-        grid=(1,),
-        in_specs=[whole(RING, slots, BLOCK, BLOCK)] * RING,
-        out_specs=(whole(slots, BLOCK, BLOCK),) * RING,
-        name="ring_sum",
-        **params(0, moved // 8),
-    )
-
-    def scattered(gradient_halves, near, far):
-        keep, send = gradient_halves
-        pieces = pair_sum(keep, lax.ppermute(send, "dp", CORES))
-        pieces = ring_sum(*[around(piece, near, distance) for distance, piece in enumerate(pieces)])
-        terms = [around(piece, far, distance).astype(jnp.float32) for distance, piece in enumerate(pieces)]
-        return sum(terms).astype(jnp.bfloat16)[None]
+    def core_sums(keep, send):
+        arrived = lax.ppermute(send, "dp", CORES)
+        return [rounded_sum(keep[i], arrived[i]) for i in range(RING)]
+
+    def scattered(pieces, near, far):
+        terms = [around(piece, near, distance) for distance, piece in enumerate(pieces)]
+        pieces = [rounded_sum(*[term[i] for term in terms]) for i in range(RING)]
+        return rounded_sum(*[around(piece, far, distance) for distance, piece in enumerate(pieces)])[None]
 
     arrived = lax.ppermute(forward(swap, where, first_tokens, weights), "section", UP)
-    first = jnp.where(upper, arrived, first_tokens)
-    second, pre, inverse, normed, act, leaving = turn(swap, where, first, last_grads, weights)
+    second, pre, inverse, normed, act, leaving = turn(swap, where, first_tokens, arrived, last_grads, weights)
     arrived = lax.ppermute(leaving, "section", DOWN)
-    normed_other = swapped(normed[1])
-    act_other = swapped(act[1])
-
-    grads = jnp.where(upper, last_grads, arrived)
-    dpre_high, middle = backward_layer(1, False)(swap, where, second, grads, pre, inverse, weights)
-    grads_other = swapped(jnp.where(odd == 0, grads, middle))
-    grads_own = jnp.where(odd == 0, middle, grads)
-    (dpre_low,) = backward_layer(0, True)(swap, where, first, middle, pre, inverse, weights)
-    dpre_other = swapped(jnp.where(odd == 0, dpre_high, dpre_low))
-    dpre_own = jnp.where(odd == 0, dpre_low, dpre_high)
-
-    sums_in = scattered(gradient_in(places_in, normed[0], normed_other, dpre_own, dpre_other), Y, Z)
-    sums_out = scattered(gradient_out(places_out, act[0], act_other, grads_own, grads_other), Z, Y)
+    arrived, normed_other, act_other = lax.optimization_barrier((arrived, swapped(normed[1]), swapped(act[1])))
+
+    dpre_high, middle, grads_own, early, late = high(swap, where, second, last_grads, arrived, pre, inverse, weights)
+    early = swapped(early)
+    dpre_own, dpre_sent = low(swap, where, middle, dpre_high, pre, weights)
+    early, late, dpre_sent = lax.optimization_barrier((early, late, dpre_sent))
+    dpre_other = swapped(dpre_sent)
+    late = swapped(late)
+
+    pieces_in = core_sums(*gradient_in(places_in, normed[0], normed_other, dpre_own, dpre_other))
+    late, *pieces_in = lax.optimization_barrier((late, *pieces_in))
+    pieces_out = core_sums(*gradient_out(places_out, act[0], act_other, grads_own, early, late))
+    sums_in = scattered(pieces_in, Y, Z)
+    sums_out = scattered(pieces_out, Z, Y)
     return (sums_in, sums_out)
 
 

time: 348 us -> 336 us (0.966)
  waiting for transfers between devices: 148 us -> 165 us
  Pallas kernels: 84.6 us -> 71 us
  starting transfers between devices: 42.3 us -> 29.4 us
    ppermute x1, waiting for transfers between devices: 23.4 us -> 0.01 us  [per_device(): arrived = lax.ppermute(leaving, 'section', DOWN)]
    ppermute x6 -> x7, waiting for transfers between devices: 24.7 us -> 44.5 us  [swapped(): return lax.ppermute(array, 'section', PAIR)]
    ppermute x12, waiting for transfers between devices: 23 us -> 40.4 us  [around(): return lax.ppermute(array, 'dp', route)]
    pallas_call x8 -> x4, Pallas kernels: 65 us -> 51.3 us  [the longest x1 22.3 us: per_device(): turn(swap, where, first_tokens, arrived, last_grads, weights)]
    ppermute x12, starting transfers between devices: 29.6 us -> 16.2 us  [around(): return lax.ppermute(array, 'dp', route)]
    select_n x4 -> x0, other arithmetic: 6.66 us -> none  [the longest x1 2.76 us: per_device(): grads_other = swapped(jnp.where(odd == 0, grads, middle))]
    convert_element_type x0 -> x2, other arithmetic: none -> 6.58 us  [rounded_sum(): sum((term.astype(jnp.float32) for term in terms)).astype(jnp.bfloat16)]
    ppermute x2, waiting for transfers between devices: 0.01 us -> 3.78 us  [core_sums(): arrived = lax.ppermute(send, 'dp', CORES)]
  transfers between devices with their start and end apart: 23 -> 24, of which waited for: 13 -> 16; matrix products, arithmetic and copies ran while one was open for 4% -> 5% of each run, Pallas kernels for 15% -> 2%
where the time goes in v5:
time: 336 us; the launch traced here: 329 us
  waiting for transfers between devices  165 us (49%)
  Pallas kernels  71 us (21%)
  starting transfers between devices  29.4 us (9%)
  blocking collectives  25.9 us (8%)
  between operations  14.7 us (4%)
  local copies, waits for them, and re-layouts  11.7 us (3%)
  other arithmetic  11.4 us (3%)
    all_gather x1, waiting for transfers between devices, per_device(): weights = lax.all_gather(jnp.stack([own, swapped(own)]), 'dp', axis=0)  54.9 us
    ppermute x7, waiting for transfers between devices, swapped(): return lax.ppermute(array, 'section', PAIR)  44.5 us
    ppermute x12, waiting for transfers between devices, around(): return lax.ppermute(array, 'dp', route)  40.4 us
    all_gather x1, blocking collectives, per_device(): lax.all_gather(jnp.stack([own_places, swapped(own_places)]), 'dp', axis=0)  25.9 us
    pallas_call x1, Pallas kernels, per_device(): turn(swap, where, first_tokens, arrived, last_grads, weights)  22.3 us
    ppermute x1, waiting for transfers between devices, per_device(): lax.ppermute(forward(swap, where, first_tokens, weights), 'section', UP)  21.8 us
    ppermute x12, starting transfers between devices, around(): return lax.ppermute(array, 'dp', route)  16.2 us
    pallas_call x1, Pallas kernels, per_device(): high(swap, where, second, last_grads, arrived, pre, inverse, weights)  13.7 us
  transfers between devices with their start and end apart: 24, of which 16 were waited for; matrix products, arithmetic and copies ran while one was open for 5% of the time, Pallas kernels for 2%

profile of v5, /device:TPU:0, one launch (start us, length us, event | category | flops | bytes accessed | tf_op | source)
XLA Modules:
  0.0 329.5 jit_solution(454588624535808508)
XLA Ops:
  9.3 1.7 collective-permute-start.1
  10.9 7.7 %collective-permute-done.1 = bf16[2,5,128,128]{3,2,1,0:T(8,128)(2,1)S(1)} collective-permute-done((bf16[2,5,128,128]{3,2,1,0:T(8,128)(2,1)S(1)}, bf16[2,5,128,128]{3,2,1,0:T(8,128)(2,1)S(1)}, u32[]{:S(2)}, u32[]{:S(2)}) %collective-permute-start.1) | collective-permute-done | bytes 327712 | tf_op jit(solution)/shard_map/ppermute | solution.py:264
  19.6 1.8 collective-permute-start
  23.3 25.9 %all-gather = s32[64,2,5]{2,1,0:T(2,128)S(1)} all-gather(s32[2,2,5]{2,1,0:T(2,128)S(1)} %pad_add_fusion), channel_id=2, replica_groups=mesh['section'=4,'dp'=32] {'dp'}, dimensions={0}, use_global_device_ids=true | all-gather | bytes 2640 | tf_op jit(solution)/shard_map/all_gather | solution.py:279
  50.1 54.9 %all-gather.4.cloned.1.call-done = bf16[64,2,5,128,128]{4,3,2,1,0:T(8,128)(2,1)} async-done(((bf16[2,2,5,128,128]{4,3,2,1,0:T(8,128)(2,1)}), bf16[64,2,5,128,128]{4,3,2,1,0:T(8,128)(2,1)}) %all-gather.4.cloned.1.call-update) | async-done | bytes 20971536 | tf_op jit(solution)/shard_map/all_gather | solution.py:277
  104.9 12.2 %forward_layers.1 = bf16[64,8192]{1,0:T(8,128)(2,1)} custom-call(s32[2]{0:T(128)} %pad_add_fusion.2.swap_ref, s32[1024]{0:T(1024)} %compare_select_fusion.where_ref, bf16[64,8192]{1,0:T(8,128)(2,1)} %constant_dynamic-slice_fusion.1.first_ref.tokens_ref, bf16[32,2,2,5,128,128]{5,4,3,2,1,0:T(8,128)(2,1)} %bitcast.94), custom_call_target="tpu_custom_call" | custom-call | flops 2147483648 | bytes 20971520 | tf_op jit(solution)/shard_map/forward_layers/pallas_call | solution.py:413
  117.1 4.8 %collective-permute-start.2 = (bf16[64,8192]{1,0:T(8,128)(2,1)}, bf16[64,8192]{1,0:T(8,128)(2,1)S(1)}, u32[]{:S(2)}, u32[]{:S(2)}) collective-permute-start(bf16[64,8192]{1,0:T(8,128)(2,1)} %forward_layers.1), channel_id=1, source_target_pairs={{0,96},{32,64},{1,97},{33,65},{2,98},{34,66},{3,99},{35,67},{4,100... | collective-permute-start | bytes 3145736 | tf_op jit(solution)/shard_map/ppermute | solution.py:413
  123.1 21.8 %collective-permute-done.2.arrived_ref = bf16[64,8192]{1,0:T(8,128)(2,1)S(1)} collective-permute-done((bf16[64,8192]{1,0:T(8,128)(2,1)}, bf16[64,8192]{1,0:T(8,128)(2,1)S(1)}, u32[]{:S(2)}, u32[]{:S(2)}) %collective-permute-start.2) | collective-permute-done | bytes 1048608 | tf_op jit(solution)/shard_map/ppermute | solution.py:413
  145.9 22.3 %turn_layers.1 = (bf16[64,8192]{1,0:T(8,128)(2,1)}, f32[2,64,512]{2,1,0:T(8,128)}, f32[2,64,128]{2,1,0:T(8,128)}, bf16[2,64,8192]{2,1,0:T(8,128)(2,1)}, bf16[2,6...) custom-call(s32[2]{0:T(128)} %pad_add_fusion.2.swap_ref, s32[1024]{0:T(1024)} %compare_select_fusion.where_ref, ...), custom_call_target="tpu_custom_call" | custom-call | flops 3758096384 | bytes 20971520 | tf_op jit(solution)/shard_map/turn_layers/pallas_call | solution.py:414
  169.5 2.7 slice_bitcast_fusion
  173.1 2.0 collective-permute-start.5
  175.1 23.1 %collective-permute-done.5.act_other_ref = bf16[64,512]{1,0:T(8,128)(2,1)S(1)} collective-permute-done((bf16[64,512]{1,0:T(8,128)(2,1)S(1)}, bf16[64,512]{1,0:T(8,128)(2,1)S(1)}, u32[]{:S(2)}, u32[]{:S(2)}) %collective-permute-start.5) | collective-permute-done | bytes 65568 | tf_op jit(solution)/shard_map/ppermute | solution.py:264
  199.2 13.7 %backward_high.1 = (bf16[64,512]{1,0:T(8,128)(2,1)}, bf16[64,8192]{1,0:T(8,128)(2,1)}, bf16[64,8192]{1,0:T(8,128)(2,1)}, bf16[32,8192]{1,0:T(8,128)(2,1)}, bf16[32,8192]{1,0:T(8,128)(2,1)}) custom-call(s32[2]{0:T(128)} %pad_add_fusion.2.swap_ref, s32[1024]{0:T(1024)} %compare_select_fusion.where_ref, bf16[64,8192]{1,0:T(8,128)(2,1)} %get-tuple-element.30.hidden_ref, ...), custom_call_target="tpu_custom_call" | custom-call | flops 1073741824 | bytes 10485760 | tf_op jit(solution)/shard_map/backward_high/pallas_call | solution.py:418
  213.4 7.8 %backward_low.1 = (bf16[64,512]{1,0:T(8,128)(2,1)}, bf16[64,512]{1,0:T(8,128)(2,1)}) custom-call(s32[2]{0:T(128)} %pad_add_fusion.2.swap_ref, s32[1024]{0:T(1024)} %compare_select_fusion.where_ref, bf16[64,8192]{1,0:T(8,128)(2,1)} %get-tuple-element.39.middle_ref, bf16[64,512]{1,0:T(8,128)(2,1)} %get-tuple-element.40.high_ref, ...), custom_call_target="tpu_custom_call" | custom-call | tf_op jit(solution)/shard_map/backward_low/pallas_call | solution.py:420
  221.3 4.2 %collective-permute-done.6.early_ref = bf16[32,8192]{1,0:T(8,128)(2,1)S(1)} collective-permute-done((bf16[32,8192]{1,0:T(8,128)(2,1)}, bf16[32,8192]{1,0:T(8,128)(2,1)S(1)}, u32[]{:S(2)}, u32[]{:S(2)}) %collective-permute-start.6) | collective-permute-done | bytes 524320 | tf_op jit(solution)/shard_map/ppermute | solution.py:264
  226.5 3.4 %collective-permute-done.8.dpre_other_ref = bf16[64,512]{1,0:T(8,128)(2,1)S(1)} collective-permute-done((bf16[64,512]{1,0:T(8,128)(2,1)}, bf16[64,512]{1,0:T(8,128)(2,1)S(1)}, u32[]{:S(2)}, u32[]{:S(2)}) %collective-permute-start.8) | collective-permute-done | bytes 65568 | tf_op jit(solution)/shard_map/ppermute | solution.py:264
  230.6 7.5 %gradient_in.1 = (bf16[4,4,5,128,128]{4,3,2,1,0:T(8,128)(2,1)}, bf16[4,4,5,128,128]{4,3,2,1,0:T(8,128)(2,1)}) custom-call(s32[160]{0:T(256)} %reshape.128.places_ref, bf16[64,8192]{1,0:T(8,128)(2,1)} %get-tuple-element.72.own_ref, bf16[64,8192]{1,0:T(8,128)(2,1)} %copy-done.4, bf16[64,512]{1,0:T(8,128)(2,1)} %get-tuple-element.44.dpre_own_ref, ...), custom_call_target="tpu_custom_call" | custom-call | tf_op jit(solution)/shard_map/gradient_in/pallas_call | solution.py:425
  239.4 3.8 %collective-permute-done.9 = bf16[4,4,5,128,128]{4,3,2,1,0:T(8,128)(2,1)S(1)} collective-permute-done((bf16[4,4,5,128,128]{4,3,2,1,0:T(8,128)(2,1)}, bf16[4,4,5,128,128]{4,3,2,1,0:T(8,128)(2,1)S(1)}, u32[]{:S(2)}, u32[]{:S(2)}) %collective-permute-start.9) | collective-permute-done | bytes 2621472 | tf_op jit(solution)/shard_map/ppermute | solution.py:405
  243.2 3.8 %fusion.3 = (bf16[4,5,128,128]{3,2,1,0:T(8,128)(2,1)S(1)}, bf16[4,5,128,128]{3,2,1,0:T(8,128)(2,1)}, bf16[4,5,128,128]{3,2,1,0:T(8,128)(2,1)}, bf16[4,5,128,128]{3,2,1,0:T(8,128)(2,1)S(1)}) fusion(bf16[4,4,5,128,128]{4,3,2,1,0:T(8,128)(2,1)S(1)} %collective-permute-done.9, bf16[4,4,5,128,128]{4,3,2,1,0:T(8,128)(2,1)} %get-tuple-element.46), kind=kLoop, calls=%fused_computation.13 | loop fusion | flops 5242880 | bytes 7864320 | tf_op jit(solution)/shard_map/convert_element_type | solution.py:260
  247.0 6.0 %collective-permute-done.7.late_ref = bf16[32,8192]{1,0:T(8,128)(2,1)} collective-permute-done((bf16[32,8192]{1,0:T(8,128)(2,1)}, bf16[32,8192]{1,0:T(8,128)(2,1)}, u32[]{:S(2)}, u32[]{:S(2)}) %collective-permute-start.7) | collective-permute-done | bytes 524320 | tf_op jit(solution)/shard_map/ppermute | solution.py:264
  253.0 7.5 %gradient_out.1 = (bf16[4,4,5,128,128]{4,3,2,1,0:T(8,128)(2,1)}, bf16[4,4,5,128,128]{4,3,2,1,0:T(8,128)(2,1)}) custom-call(s32[160]{0:T(256)} %reshape.129.places_ref, bf16[64,512]{1,0:T(8,128)(2,1)} %get-tuple-element.74.act_own_ref, bf16[64,512]{1,0:T(8,128)(2,1)} %copy-done.8, bf16[64,8192]{1,0:T(8,128)(2,1)} %get-tuple-element.53.own_ref, ...), custom_call_target="tpu_custom_call" | custom-call | tf_op jit(solution)/shard_map/gradient_out/pallas_call | solution.py:427
  261.9 2.7 collective-permute-start.11
  266.1 2.8 add_convert_fusion.3
  268.8 1.9 collective-permute-start.19
  271.4 7.6 %collective-permute-done.10 = bf16[4,5,128,128]{3,2,1,0:T(8,128)(2,1)S(1)} collective-permute-done((bf16[4,5,128,128]{3,2,1,0:T(8,128)(2,1)}, bf16[4,5,128,128]{3,2,1,0:T(8,128)(2,1)S(1)}, u32[]{:S(2)}, u32[]{:S(2)}) %collective-permute-start.10) | collective-permute-done | bytes 655392 | tf_op jit(solution)/shard_map/ppermute | solution.py:256
  280.3 13.8 %collective-permute-done.11 = bf16[4,5,128,128]{3,2,1,0:T(8,128)(2,1)S(1)} collective-permute-done((bf16[4,5,128,128]{3,2,1,0:T(8,128)(2,1)}, bf16[4,5,128,128]{3,2,1,0:T(8,128)(2,1)S(1)}, u32[]{:S(2)}, u32[]{:S(2)}) %collective-permute-start.11) | collective-permute-done | bytes 655392 | tf_op jit(solution)/shard_map/ppermute | solution.py:256
  294.4 1.5 collective-permute-start.13
  295.9 1.8 collective-permute-start.15
  299.2 11.7 %collective-permute-done.17 = bf16[4,5,128,128]{3,2,1,0:T(8,128)(2,1)S(1)} collective-permute-done((bf16[4,5,128,128]{3,2,1,0:T(8,128)(2,1)S(1)}, bf16[4,5,128,128]{3,2,1,0:T(8,128)(2,1)S(1)}, u32[]{:S(2)}, u32[]{:S(2)}) %collective-permute-start.17) | collective-permute-done | bytes 655392 | tf_op jit(solution)/shard_map/ppermute | solution.py:256
  311.3 3.2 collective-permute-start.22
  314.6 3.6 %collective-permute-done.14 = bf16[5,128,128]{2,1,0:T(8,128)(2,1)S(1)} collective-permute-done((bf16[5,128,128]{2,1,0:T(8,128)(2,1)S(1)}, bf16[5,128,128]{2,1,0:T(8,128)(2,1)S(1)}, u32[]{:S(2)}, u32[]{:S(2)}) %collective-permute-start.14) | collective-permute-done | bytes 163872 | tf_op jit(solution)/shard_map/ppermute | solution.py:256
  319.6 1.8 collective-permute-done.21
  (80 shorter events, 23.9 us)
Async XLA Ops:
  7.2 14.9 %copy-start = (bf16[128,8192]{1,0:T(8,128)(2,1)S(1)}, bf16[128,8192]{1,0:T(8,128)(2,1)}, u32[]{:S(2)}) copy-start(bf16[128,8192]{1,0:T(8,128)(2,1)} %param.6) | copy-start | bytes 6291460
  7.2 12.4 %copy-start.10 = (s32[1,5]{1,0:T(1,128)S(1)}, s32[1,5]{1,0:T(1,128)}, u32[]{:S(2)}) copy-start(s32[1,5]{1,0:T(1,128)} %param.10) | copy-start | bytes 64
  7.2 12.4 %copy-start.11 = (s32[1,5]{1,0:T(1,128)S(1)}, s32[1,5]{1,0:T(1,128)}, u32[]{:S(2)}) copy-start(s32[1,5]{1,0:T(1,128)} %param.9) | copy-start | bytes 64
  7.2 97.7 %all-gather.4.cloned.1.call-start = ((), (), s32[]{:S(2)}) async-start(), calls=%async_computation | async-start | bytes 21626880 | tf_op jit(solution)/shard_map/all_gather | solution.py:277
  9.3 9.4 %collective-permute-start.1 = (bf16[2,5,128,128]{3,2,1,0:T(8,128)(2,1)S(1)}, bf16[2,5,128,128]{3,2,1,0:T(8,128)(2,1)S(1)}, u32[]{:S(2)}, u32[]{:S(2)}) collective-permute-start(bf16[2,5,128,128]{3,2,1,0:T(8,128)(2,1)S(1)} %constant_dynamic-update-slice_fusion), channel_id=1, source_target_pairs={{0,32},{32,0},{64,96},{96,64},{1,33},{33,1},{65,97},{97,65},{2,34}... | collective-permute-start | bytes 983048 | tf_op jit(solution)/shard_map/ppermute | solution.py:264
  19.6 3.6 %collective-permute-start = (s32[2,5]{1,0:T(2,128)S(1)}, s32[2,5]{1,0:T(2,128)S(1)}, u32[]{:S(2)}, u32[]{:S(2)}) collective-permute-start(s32[2,5]{1,0:T(2,128)S(1)} %get-tuple-element.79), channel_id=1, source_target_pairs={{0,32},{32,0},{64,96},{96,64},{1,33},{33,1},{65,97},{97,65},{2,34}... | collective-permute-start | bytes 128 | tf_op jit(solution)/shard_map/ppermute | solution.py:264
  104.9 17.0 %copy-start.5 = (bf16[128,8192]{1,0:T(8,128)(2,1)S(1)}, bf16[128,8192]{1,0:T(8,128)(2,1)}, u32[]{:S(2)}) copy-start(bf16[128,8192]{1,0:T(8,128)(2,1)} %param.11) | copy-start | bytes 6291460
  117.1 27.7 %collective-permute-start.2 = (bf16[64,8192]{1,0:T(8,128)(2,1)}, bf16[64,8192]{1,0:T(8,128)(2,1)S(1)}, u32[]{:S(2)}, u32[]{:S(2)}) collective-permute-start(bf16[64,8192]{1,0:T(8,128)(2,1)} %forward_layers.1), channel_id=1, source_target_pairs={{0,96},{32,64},{1,97},{33,65},{2,98},{34,66},{3,99},{35,67},{4,100... | collective-permute-start | bytes 3145736 | tf_op jit(solution)/shard_map/ppermute | solution.py:413
  168.2 30.0 %collective-permute-start.3 = (bf16[64,8192]{1,0:T(8,128)(2,1)}, bf16[64,8192]{1,0:T(8,128)(2,1)S(1)}, u32[]{:S(2)}, u32[]{:S(2)}) collective-permute-start(bf16[64,8192]{1,0:T(8,128)(2,1)} %get-tuple-element.31), channel_id=1, source_target_pairs={{96,0},{64,32},{97,1},{65,33},{98,2},{66,34},{99,3},{67,35},{100,4... | collective-permute-start | bytes 3145736 | tf_op jit(solution)/shard_map/ppermute | solution.py:415
  172.2 25.9 %collective-permute-start.4 = (bf16[64,8192]{1,0:T(8,128)(2,1)S(1)}, bf16[64,8192]{1,0:T(8,128)(2,1)S(1)}, u32[]{:S(2)}, u32[]{:S(2)}) collective-permute-start(bf16[64,8192]{1,0:T(8,128)(2,1)S(1)} %get-tuple-element.73), channel_id=1, source_target_pairs={{0,32},{32,0},{64,96},{96,64},{1,33},{33,1},{65,97},{97,65},{2,34}... | collective-permute-start | bytes 3145736 | tf_op jit(solution)/shard_map/ppermute | solution.py:264
  173.1 25.0 %collective-permute-start.5 = (bf16[64,512]{1,0:T(8,128)(2,1)S(1)}, bf16[64,512]{1,0:T(8,128)(2,1)S(1)}, u32[]{:S(2)}, u32[]{:S(2)}) collective-permute-start(bf16[64,512]{1,0:T(8,128)(2,1)S(1)} %get-tuple-element.75), channel_id=1, source_target_pairs={{0,32},{32,0},{64,96},{96,64},{1,33},{33,1},{65,97},{97,65},{2,34}... | collective-permute-start | bytes 196616 | tf_op jit(solution)/shard_map/ppermute | solution.py:264
  198.2 14.7 %copy-start.8 = (bf16[64,512]{1,0:T(8,128)(2,1)}, bf16[64,512]{1,0:T(8,128)(2,1)S(1)}, u32[]{:S(2)}) copy-start(bf16[64,512]{1,0:T(8,128)(2,1)S(1)} %collective-permute-done.5.act_other_ref) | copy-start | bytes 196612
  198.2 14.7 %copy-start.4 = (bf16[64,8192]{1,0:T(8,128)(2,1)}, bf16[64,8192]{1,0:T(8,128)(2,1)S(1)}, u32[]{:S(2)}) copy-start(bf16[64,8192]{1,0:T(8,128)(2,1)S(1)} %collective-permute-done.4.other_ref) | copy-start | bytes 3145732
  212.8 12.6 %collective-permute-start.6 = (bf16[32,8192]{1,0:T(8,128)(2,1)}, bf16[32,8192]{1,0:T(8,128)(2,1)S(1)}, u32[]{:S(2)}, u32[]{:S(2)}) collective-permute-start(bf16[32,8192]{1,0:T(8,128)(2,1)} %get-tuple-element.37), channel_id=1, source_target_pairs={{0,32},{32,0},{64,96},{96,64},{1,33},{33,1},{65,97},{97,65},{2,34}... | collective-permute-start | bytes 1572872 | tf_op jit(solution)/shard_map/ppermute | solution.py:264
  225.5 12.6 %copy-start.6 = (bf16[32,8192]{1,0:T(8,128)(2,1)}, bf16[32,8192]{1,0:T(8,128)(2,1)S(1)}, u32[]{:S(2)}) copy-start(bf16[32,8192]{1,0:T(8,128)(2,1)S(1)} %collective-permute-done.6.early_ref) | copy-start | bytes 1572868
  225.5 4.5 %collective-permute-start.8 = (bf16[64,512]{1,0:T(8,128)(2,1)}, bf16[64,512]{1,0:T(8,128)(2,1)S(1)}, u32[]{:S(2)}, u32[]{:S(2)}) collective-permute-start(bf16[64,512]{1,0:T(8,128)(2,1)} %get-tuple-element.45), channel_id=1, source_target_pairs={{0,32},{32,0},{64,96},{96,64},{1,33},{33,1},{65,97},{97,65},{2,34}... | collective-permute-start | bytes 196616 | tf_op jit(solution)/shard_map/ppermute | solution.py:264
  238.1 5.1 %collective-permute-start.9 = (bf16[4,4,5,128,128]{4,3,2,1,0:T(8,128)(2,1)}, bf16[4,4,5,128,128]{4,3,2,1,0:T(8,128)(2,1)S(1)}, u32[]{:S(2)}, u32[]{:S(2)}) collective-permute-start(bf16[4,4,5,128,128]{4,3,2,1,0:T(8,128)(2,1)} %get-tuple-element.47), channel_id=1, source_target_pairs={{0,1},{1,0},{2,3},{3,2},{4,5},{5,4},{6,7},{7,6},{8,9},{9,8},{10,11... | collective-permute-start | bytes 7864328 | tf_op jit(solution)/shard_map/ppermute | solution.py:405
  238.1 14.9 %collective-permute-start.7 = (bf16[32,8192]{1,0:T(8,128)(2,1)}, bf16[32,8192]{1,0:T(8,128)(2,1)}, u32[]{:S(2)}, u32[]{:S(2)}) collective-permute-start(bf16[32,8192]{1,0:T(8,128)(2,1)} %get-tuple-element.42), channel_id=1, source_target_pairs={{0,32},{32,0},{64,96},{96,64},{1,33},{33,1},{65,97},{97,65},{2,34}... | collective-permute-start | bytes 1572872 | tf_op jit(solution)/shard_map/ppermute | solution.py:264
  260.4 5.6 %collective-permute-start.16 = (bf16[4,4,5,128,128]{4,3,2,1,0:T(8,128)(2,1)}, bf16[4,4,5,128,128]{4,3,2,1,0:T(8,128)(2,1)S(1)}, u32[]{:S(2)}, u32[]{:S(2)}) collective-permute-start(bf16[4,4,5,128,128]{4,3,2,1,0:T(8,128)(2,1)} %get-tuple-element.57), channel_id=1, source_target_pairs={{0,1},{1,0},{2,3},{3,2},{4,5},{5,4},{6,7},{7,6},{8,9},{9,8},{10,11... | collective-permute-start | bytes 7864328 | tf_op jit(solution)/shard_map/ppermute | solution.py:405
  260.4 18.6 %collective-permute-start.10 = (bf16[4,5,128,128]{3,2,1,0:T(8,128)(2,1)}, bf16[4,5,128,128]{3,2,1,0:T(8,128)(2,1)S(1)}, u32[]{:S(2)}, u32[]{:S(2)}) collective-permute-start(bf16[4,5,128,128]{3,2,1,0:T(8,128)(2,1)} %get-tuple-element.49), channel_id=1, source_target_pairs={{0,2},{1,3},{2,4},{3,5},{4,6},{5,7},{6,0},{7,1},{8,10},{9,11},{10,... | collective-permute-start | bytes 1966088 | tf_op jit(solution)/shard_map/ppermute | solution.py:256
  261.9 32.1 %collective-permute-start.11 = (bf16[4,5,128,128]{3,2,1,0:T(8,128)(2,1)}, bf16[4,5,128,128]{3,2,1,0:T(8,128)(2,1)S(1)}, u32[]{:S(2)}, u32[]{:S(2)}) collective-permute-start(bf16[4,5,128,128]{3,2,1,0:T(8,128)(2,1)} %get-tuple-element.50), channel_id=1, source_target_pairs={{0,4},{1,5},{2,6},{3,7},{4,0},{5,1},{6,2},{7,3},{8,12},{9,13},{10,... | collective-permute-start | bytes 1966088 | tf_op jit(solution)/shard_map/ppermute | solution.py:256
  264.7 29.4 %collective-permute-start.12 = (bf16[4,5,128,128]{3,2,1,0:T(8,128)(2,1)S(1)}, bf16[4,5,128,128]{3,2,1,0:T(8,128)(2,1)S(1)}, u32[]{:S(2)}, u32[]{:S(2)}) collective-permute-start(bf16[4,5,128,128]{3,2,1,0:T(8,128)(2,1)S(1)} %get-tuple-element.51), channel_id=1, source_target_pairs={{0,6},{1,7},{2,0},{3,1},{4,2},{5,3},{6,4},{7,5},{8,14},{9,15},{10,... | collective-permute-start | bytes 1966088 | tf_op jit(solution)/shard_map/ppermute | solution.py:256
  268.8 30.2 %collective-permute-start.19 = (bf16[4,5,128,128]{3,2,1,0:T(8,128)(2,1)S(1)}, bf16[4,5,128,128]{3,2,1,0:T(8,128)(2,1)S(1)}, u32[]{:S(2)}, u32[]{:S(2)}) collective-permute-start(bf16[4,5,128,128]{3,2,1,0:T(8,128)(2,1)S(1)} %get-tuple-element.59), channel_id=1, source_target_pairs={{0,24},{1,25},{2,26},{3,27},{4,28},{5,29},{6,30},{7,31},{8,0},{9,1... | collective-permute-start | bytes 1966088 | tf_op jit(solution)/shard_map/ppermute | solution.py:256
  270.7 28.5 %collective-permute-start.18 = (bf16[4,5,128,128]{3,2,1,0:T(8,128)(2,1)S(1)}, bf16[4,5,128,128]{3,2,1,0:T(8,128)(2,1)S(1)}, u32[]{:S(2)}, u32[]{:S(2)}) collective-permute-start(bf16[4,5,128,128]{3,2,1,0:T(8,128)(2,1)S(1)} %get-tuple-element.60), channel_id=1, source_target_pairs={{0,16},{1,17},{2,18},{3,19},{4,20},{5,21},{6,22},{7,23},{8,24},{9,... | collective-permute-start | bytes 1966088 | tf_op jit(solution)/shard_map/ppermute | solution.py:256
  279.0 31.9 %collective-permute-start.17 = (bf16[4,5,128,128]{3,2,1,0:T(8,128)(2,1)S(1)}, bf16[4,5,128,128]{3,2,1,0:T(8,128)(2,1)S(1)}, u32[]{:S(2)}, u32[]{:S(2)}) collective-permute-start(bf16[4,5,128,128]{3,2,1,0:T(8,128)(2,1)S(1)} %get-tuple-element.61), channel_id=1, source_target_pairs={{0,8},{1,9},{2,10},{3,11},{4,12},{5,13},{6,14},{7,15},{8,16},{9,17... | collective-permute-start | bytes 1966088 | tf_op jit(solution)/shard_map/ppermute | solution.py:256
  294.4 20.2 %collective-permute-start.13 = (bf16[5,128,128]{2,1,0:T(8,128)(2,1)S(1)}, bf16[5,128,128]{2,1,0:T(8,128)(2,1)S(1)}, u32[]{:S(2)}, u32[]{:S(2)}) collective-permute-start(bf16[5,128,128]{2,1,0:T(8,128)(2,1)S(1)} %get-tuple-element.69), channel_id=1, source_target_pairs={{0,8},{1,9},{2,10},{3,11},{4,12},{5,13},{6,14},{7,15},{8,16},{9,17... | collective-permute-start | bytes 491528 | tf_op jit(solution)/shard_map/ppermute | solution.py:256
  295.9 18.7 %collective-permute-start.15 = (bf16[5,128,128]{2,1,0:T(8,128)(2,1)S(1)}, bf16[5,128,128]{2,1,0:T(8,128)(2,1)S(1)}, u32[]{:S(2)}, u32[]{:S(2)}) collective-permute-start(bf16[5,128,128]{2,1,0:T(8,128)(2,1)S(1)} %get-tuple-element.70), channel_id=1, source_target_pairs={{0,24},{1,25},{2,26},{3,27},{4,28},{5,29},{6,30},{7,31},{8,0},{9,1... | collective-permute-start | bytes 491528 | tf_op jit(solution)/shard_map/ppermute | solution.py:256
  299.0 19.2 %collective-permute-start.14 = (bf16[5,128,128]{2,1,0:T(8,128)(2,1)S(1)}, bf16[5,128,128]{2,1,0:T(8,128)(2,1)S(1)}, u32[]{:S(2)}, u32[]{:S(2)}) collective-permute-start(bf16[5,128,128]{2,1,0:T(8,128)(2,1)S(1)} %get-tuple-element.71), channel_id=1, source_target_pairs={{0,16},{1,17},{2,18},{3,19},{4,20},{5,21},{6,22},{7,23},{8,24},{9,... | collective-permute-start | bytes 491528 | tf_op jit(solution)/shard_map/ppermute | solution.py:256
  311.2 8.4 %collective-permute-start.20 = (bf16[5,128,128]{2,1,0:T(8,128)(2,1)S(1)}, bf16[5,128,128]{2,1,0:T(8,128)(2,1)S(1)}, u32[]{:S(2)}, u32[]{:S(2)}) collective-permute-start(bf16[5,128,128]{2,1,0:T(8,128)(2,1)S(1)} %get-tuple-element.66), channel_id=1, source_target_pairs={{0,2},{1,3},{2,4},{3,5},{4,6},{5,7},{6,0},{7,1},{8,10},{9,11},{10,... | collective-permute-start | bytes 491528 | tf_op jit(solution)/shard_map/ppermute | solution.py:256
  311.3 8.3 %collective-permute-start.22 = (bf16[5,128,128]{2,1,0:T(8,128)(2,1)S(1)}, bf16[5,128,128]{2,1,0:T(8,128)(2,1)S(1)}, u32[]{:S(2)}, u32[]{:S(2)}) collective-permute-start(bf16[5,128,128]{2,1,0:T(8,128)(2,1)S(1)} %get-tuple-element.67), channel_id=1, source_target_pairs={{0,6},{1,7},{2,0},{3,1},{4,2},{5,3},{6,4},{7,5},{8,14},{9,15},{10,... | collective-permute-start | bytes 491528 | tf_op jit(solution)/shard_map/ppermute | solution.py:256
  314.5 7.7 %copy-start.1 = (bf16[128,8192]{1,0:T(8,128)(2,1)S(1)}, bf16[128,8192]{1,0:T(8,128)(2,1)}, u32[]{:S(2)}) copy-start(bf16[128,8192]{1,0:T(8,128)(2,1)} %param.6) | copy-start | bytes 6291460
  314.6 6.8 %collective-permute-start.21 = (bf16[5,128,128]{2,1,0:T(8,128)(2,1)S(1)}, bf16[5,128,128]{2,1,0:T(8,128)(2,1)S(1)}, u32[]{:S(2)}, u32[]{:S(2)}) collective-permute-start(bf16[5,128,128]{2,1,0:T(8,128)(2,1)S(1)} %get-tuple-element.68), channel_id=1, source_target_pairs={{0,4},{1,5},{2,6},{3,7},{4,0},{5,1},{6,2},{7,3},{8,12},{9,13},{10,... | collective-permute-start | bytes 491528 | tf_op jit(solution)/shard_map/ppermute | solution.py:256
  (4 other events, 5.6 us)
Sparse Core Ops, SparseCore 0:
  19.7 85.1 all-gather.3

commit v6 on v5

--- a/solution.py
+++ b/solution.py
@@ -131,12 +131,23 @@
     forward_up(weights, 1, second_ref, silu(pre), last_ref)
 
 
+def choose(arrived, arrived_ref, here_ref, out_ref, sem):
+    @pl.when(arrived)
+    def _():
+        copy = pltpu.make_async_copy(arrived_ref, out_ref, sem)
+        copy.start()
+        copy.wait()
+
+    @pl.when(jnp.logical_not(arrived))
+    def _():
+        out_ref[...] = here_ref[...]
+
+
 def turn_kernel(
     swap_ref, where_ref, tokens_ref, arrived_ref, grad_ref, source, second_ref, pre_ref, inverse_ref, normed_ref, act_ref, earlier_ref, first_ref, middle_ref, held, sems
 ):
     weights = Weights(swap_ref, where_ref, source, held, sems, [(0, 0), (0, 1), (1, 0), (1, 1)])
-    for _, cols in chunks():
-        first_ref[:, cols] = lax.select(swap_ref[1] > 0, arrived_ref[:, cols], tokens_ref[:, cols])
+    choose(swap_ref[1] > 0, arrived_ref, tokens_ref, first_ref, sems.at[4])
     for layer, hidden_ref in enumerate((first_ref, second_ref)):
         place = layer ^ swap_ref[0]
         pre, inverse = forward_down(weights, layer, hidden_ref, normed_ref.at[place])
@@ -152,22 +163,18 @@
 
 
 def high_kernel(
-    swap_ref, where_ref, hidden_ref, grad_ref, arrived_ref, pre_ref, inverse_ref, source, dpre_ref, middle_ref, own_ref, early_ref, late_ref, upstream_ref, held, sems
+    swap_ref, where_ref, hidden_ref, grad_ref, arrived_ref, pre_ref, inverse_ref, source, dpre_ref, middle_ref, own_ref, sent_ref, upstream_ref, held, sems
 ):
     weights = Weights(swap_ref, where_ref, source, held, sems, [(1, 1), (1, 0)])
-    rows = early_ref.shape[0]
     even = swap_ref[0] == 0
-    for _, cols in chunks():
-        upstream_ref[:, cols] = lax.select(swap_ref[1] > 0, grad_ref[:, cols], arrived_ref[:, cols])
+    choose(swap_ref[1] == 0, arrived_ref, grad_ref, upstream_ref, sems.at[2])
     weights.wait(1, 1)
     weights.wait(1, 0)
     dpre_ref[...] = backward(weights, 1, hidden_ref, upstream_ref, pre_ref[1], inverse_ref[1][:, :1], middle_ref)
     for _, cols in chunks():
         upper, lower = upstream_ref[:, cols], middle_ref[:, cols]
         own_ref[:, cols] = lax.select(even, lower, upper)
-        sent = lax.select(even, upper, lower)
-        early_ref[:, cols] = sent[:rows]
-        late_ref[:, cols] = sent[rows:]
+        sent_ref[:, cols] = lax.select(even, upper, lower)
 
 
 def low_kernel(swap_ref, where_ref, middle_ref, high_ref, pre_ref, source, own_ref, sent_ref, held, sems):
@@ -209,7 +216,7 @@
 
 
 def gradient_out_kernel(
-    places_ref, act_own_ref, act_other_ref, own_ref, early_ref, late_ref, keep_ref, send_ref, dense, turned
+    places_ref, act_own_ref, act_other_ref, own_ref, other_ref, keep_ref, send_ref, dense, turned
 ):
     @pl.when(pl.program_id(0) == 0)
     def _():
@@ -217,7 +224,7 @@
         act = jnp.concatenate([act_own_ref[...], act_other_ref[...]], axis=0)
         turned[...] = act.astype(jnp.float32).T.astype(jnp.bfloat16)
         for chunk, cols in chunks():
-            upstream = jnp.concatenate([own_ref[:, cols], early_ref[:, cols], late_ref[:, cols]], axis=0)
+            upstream = jnp.concatenate([own_ref[:, cols], other_ref[:, cols]], axis=0)
             part = dot(turned[...], upstream, NN).astype(jnp.bfloat16)
             for row in range(ROWS_K):
                 for col in range(BLOCKS):
@@ -273,8 +280,8 @@
     swap = jnp.stack([odd, here // 2]).astype(jnp.int32)
     half = jnp.where((here == 1) | (here == 2), rows, 0)
 
-    own = jnp.stack([blocks_in[0], blocks_out[0]])
-    weights = lax.all_gather(jnp.stack([own, swapped(own)]), "dp", axis=0)
+    both = jnp.stack([blocks_in[0], blocks_out[0], swapped(blocks_in[0]), swapped(blocks_out[0])])
+    weights = lax.all_gather(both, "dp", axis=0).reshape(owners, 2, 2, slots, BLOCK, BLOCK)
     own_places = jnp.stack([pos_in[0], pos_out[0]])
     places = lax.all_gather(jnp.stack([own_places, swapped(own_places)]), "dp", axis=0).transpose(1, 2, 0, 3)
     codes = jnp.arange(owners, dtype=jnp.int32)[:, None] * 8 + jnp.arange(slots, dtype=jnp.int32)
@@ -302,7 +309,7 @@
     def held(count):
         return [
             pltpu.VMEM((count, owners + 1, slots, BLOCK, BLOCK), jnp.bfloat16),
-            pltpu.SemaphoreType.DMA((count,)),
+            pltpu.SemaphoreType.DMA((count + 1,)),
         ]
 
     forward = pl.pallas_call(
@@ -331,7 +338,7 @@
         grid_spec=pltpu.PrefetchScalarGridSpec(
             num_scalar_prefetch=2,
             grid=(1,),
-            in_specs=[whole(rows, D)] * 3 + [anywhere],
+            in_specs=[whole(rows, D), anywhere, whole(rows, D), anywhere],
             out_specs=[
                 whole(rows, D),
                 whole(2, rows, RANK),
@@ -348,12 +355,12 @@
 
     high = pl.pallas_call(
         high_kernel,
-        out_shape=(shape(rows, RANK), shape(rows, D), shape(rows, D), shape(rows // 2, D), shape(rows // 2, D)),
+        out_shape=(shape(rows, RANK),) + (shape(rows, D),) * 3,
         grid_spec=pltpu.PrefetchScalarGridSpec(
             num_scalar_prefetch=2,
             grid=(1,),
-            in_specs=[whole(rows, D)] * 3 + [whole(2, rows, RANK), whole(2, rows, BLOCK), anywhere],
-            out_specs=[whole(rows, RANK)] + [whole(rows, D)] * 2 + [whole(rows // 2, D)] * 2,
+            in_specs=[whole(rows, D)] * 2 + [anywhere, whole(2, rows, RANK), whole(2, rows, BLOCK), anywhere],
+            out_specs=[whole(rows, RANK)] + [whole(rows, D)] * 3,
             scratch_shapes=[pltpu.VMEM((rows, D), jnp.bfloat16)] + held(2),
         ),
         name="backward_high",
@@ -370,7 +377,7 @@
             scratch_shapes=held(1),
         ),
         name="backward_low",
-        **params(0, 0),
+        **params(work, moved),
     )
 
     halves = shape(RING, RING, slots, BLOCK, BLOCK)
@@ -389,7 +396,7 @@
                 scratch_shapes=[dense] + scratch,
             ),
             name=name,
-            **params(0, 0),
+            **params(2 * work, 3 * moved),
         )
 
     gradient_in = gradient(
@@ -398,7 +405,7 @@
     gradient_out = gradient(
         gradient_out_kernel,
         "gradient_out",
-        [whole(rows, RANK)] * 2 + [whole(rows, D)] + [whole(rows // 2, D)] * 2,
+        [whole(rows, RANK)] * 2 + [whole(rows, D)] * 2,
         [pltpu.VMEM((RANK, 2 * rows), jnp.bfloat16)],
     )
     def core_sums(keep, send):
@@ -415,16 +422,14 @@
     arrived = lax.ppermute(leaving, "section", DOWN)
     arrived, normed_other, act_other = lax.optimization_barrier((arrived, swapped(normed[1]), swapped(act[1])))
 
-    dpre_high, middle, grads_own, early, late = high(swap, where, second, last_grads, arrived, pre, inverse, weights)
-    early = swapped(early)
+    dpre_high, middle, grads_own, sent = high(swap, where, second, last_grads, arrived, pre, inverse, weights)
+    grads_other = swapped(sent)
     dpre_own, dpre_sent = low(swap, where, middle, dpre_high, pre, weights)
-    early, late, dpre_sent = lax.optimization_barrier((early, late, dpre_sent))
-    dpre_other = swapped(dpre_sent)
-    late = swapped(late)
-
-    pieces_in = core_sums(*gradient_in(places_in, normed[0], normed_other, dpre_own, dpre_other))
-    late, *pieces_in = lax.optimization_barrier((late, *pieces_in))
-    pieces_out = core_sums(*gradient_out(places_out, act[0], act_other, grads_own, early, late))
+    grads_other, dpre_other = lax.optimization_barrier((grads_other, swapped(dpre_sent)))
+
+    halves_in = gradient_in(places_in, normed[0], normed_other, dpre_own, dpre_other)
+    halves_out = gradient_out(places_out, act[0], act_other, grads_own, grads_other)
+    pieces_in, pieces_out = core_sums(*halves_in), core_sums(*halves_out)
     sums_in = scattered(pieces_in, Y, Z)
     sums_out = scattered(pieces_out, Z, Y)
     return (sums_in, sums_out)

time: 336 us -> 340 us (1.012)
  starting transfers between devices: 29.4 us -> 35.6 us
  waiting for transfers between devices: 165 us -> 169 us
    ppermute x1, waiting for transfers between devices: 0.01 us -> 7.06 us  [per_device(): arrived = lax.ppermute(leaving, 'section', DOWN)]
    ppermute x12, starting transfers between devices: 16.2 us -> 20.6 us  [around(): return lax.ppermute(array, 'dp', route)]
    convert_element_type x2, other arithmetic: 6.58 us -> 2.48 us  [rounded_sum(): sum((term.astype(jnp.float32) for term in terms)).astype(jnp.bfloat16)]
    ppermute x2, waiting for transfers between devices: 3.78 us -> 0.01 us  [core_sums(): arrived = lax.ppermute(send, 'dp', CORES)]
  transfers between devices with their start and end apart: 24 -> 24, of which waited for: 16 -> 13; matrix products, arithmetic and copies ran while one was open for 5% -> 3% of each run, Pallas kernels for 2% -> 5%
where the time goes in v6:
time: 340 us; the launch traced here: 334 us
  waiting for transfers between devices  169 us (50%)
  Pallas kernels  70.8 us (21%)
  starting transfers between devices  35.6 us (10%)
  blocking collectives  25.9 us (8%)
  between operations  14.7 us (4%)
  local copies, waits for them, and re-layouts  9.74 us (3%)
  other arithmetic  8.31 us (2%)
    all_gather x1, waiting for transfers between devices, per_device(): lax.all_gather(both, 'dp', axis=0)  54.8 us
    ppermute x7, waiting for transfers between devices, swapped(): return lax.ppermute(array, 'section', PAIR)  44 us
    ppermute x12, waiting for transfers between devices, around(): return lax.ppermute(array, 'dp', route)  40.8 us
    all_gather x1, blocking collectives, per_device(): lax.all_gather(jnp.stack([own_places, swapped(own_places)]), 'dp', axis=0)  25.9 us
    pallas_call x1, Pallas kernels, per_device(): turn(swap, where, first_tokens, arrived, last_grads, weights)  22 us
    ppermute x1, waiting for transfers between devices, per_device(): lax.ppermute(forward(swap, where, first_tokens, weights), 'section', UP)  22 us
    ppermute x12, starting transfers between devices, around(): return lax.ppermute(array, 'dp', route)  20.6 us
    pallas_call x1, Pallas kernels, per_device(): high(swap, where, second, last_grads, arrived, pre, inverse, weights)  13.6 us
  transfers between devices with their start and end apart: 24, of which 13 were waited for; matrix products, arithmetic and copies ran while one was open for 3% of the time, Pallas kernels for 5%

profile of v6, /device:TPU:0, one launch (start us, length us, event | category | flops | bytes accessed | tf_op | source)
XLA Modules:
  0.0 333.8 jit_solution(1301401168507937540)
XLA Ops:
  7.2 1.7 collective-permute-start.2
  9.4 5.3 %collective-permute-done.2 = bf16[5,128,128]{2,1,0:T(8,128)(2,1)S(1)} collective-permute-done((bf16[5,128,128]{2,1,0:T(8,128)(2,1)}, bf16[5,128,128]{2,1,0:T(8,128)(2,1)S(1)}, u32[]{:S(2)}, u32[]{:S(2)}) %collective-permute-start.2) | collective-permute-done | bytes 163872 | tf_op jit(solution)/shard_map/ppermute | solution.py:271
  14.6 2.2 collective-permute-done.1
  16.8 1.9 pad_maximum_fusion
  18.8 1.8 collective-permute-start
  22.5 25.9 %all-gather = s32[64,2,5]{2,1,0:T(2,128)S(1)} all-gather(s32[2,2,5]{2,1,0:T(2,128)S(1)} %pad_add_fusion), channel_id=2, replica_groups=mesh['section'=4,'dp'=32] {'dp'}, dimensions={0}, use_global_device_ids=true | all-gather | bytes 2640 | tf_op jit(solution)/shard_map/all_gather | solution.py:286
  49.3 54.8 %all-gather.4.cloned.1.call-done = bf16[128,5,128,128]{3,2,1,0:T(8,128)(2,1)} async-done(((bf16[4,5,128,128]{3,2,1,0:T(8,128)(2,1)}), bf16[128,5,128,128]{3,2,1,0:T(8,128)(2,1)}) %all-gather.4.cloned.1.call-update) | async-done | bytes 20971536 | tf_op jit(solution)/shard_map/all_gather | solution.py:284
  104.1 12.2 %forward_layers.1 = bf16[64,8192]{1,0:T(8,128)(2,1)} custom-call(s32[2]{0:T(128)} %pad_add_fusion.2.swap_ref, s32[1024]{0:T(1024)} %compare_select_fusion.where_ref, bf16[64,8192]{1,0:T(8,128)(2,1)} %constant_dynamic-slice_fusion.1.first_ref.tokens_ref, bf16[32,2,2,5,128,128]{5,4,3,2,1,0:T(8,128)(2,1)} %bitcast.114), custom_call_target="tpu_custom_call" | custom-call | flops 2147483648 | bytes 20971520 | tf_op jit(solution)/shard_map/forward_layers/pallas_call | solution.py:420
  116.4 4.7 %collective-permute-start.3 = (bf16[64,8192]{1,0:T(8,128)(2,1)}, bf16[64,8192]{1,0:T(8,128)(2,1)S(1)}, u32[]{:S(2)}, u32[]{:S(2)}) collective-permute-start(bf16[64,8192]{1,0:T(8,128)(2,1)} %forward_layers.1), channel_id=1, source_target_pairs={{0,96},{32,64},{1,97},{33,65},{2,98},{34,66},{3,99},{35,67},{4,100... | collective-permute-start | bytes 3145736 | tf_op jit(solution)/shard_map/ppermute | solution.py:420
  122.1 22.0 %collective-permute-done.3.arrived_ref = bf16[64,8192]{1,0:T(8,128)(2,1)S(1)} collective-permute-done((bf16[64,8192]{1,0:T(8,128)(2,1)}, bf16[64,8192]{1,0:T(8,128)(2,1)S(1)}, u32[]{:S(2)}, u32[]{:S(2)}) %collective-permute-start.3) | collective-permute-done | bytes 1048608 | tf_op jit(solution)/shard_map/ppermute | solution.py:420
  145.1 22.0 %turn_layers.1 = (bf16[64,8192]{1,0:T(8,128)(2,1)}, f32[2,64,512]{2,1,0:T(8,128)}, f32[2,64,128]{2,1,0:T(8,128)}, bf16[2,64,8192]{2,1,0:T(8,128)(2,1)}, bf16[2,6...) custom-call(s32[2]{0:T(128)} %pad_add_fusion.2.swap_ref, s32[1024]{0:T(1024)} %compare_select_fusion.where_ref, ...), custom_call_target="tpu_custom_call" | custom-call | flops 3758096384 | bytes 20971520 | tf_op jit(solution)/shard_map/turn_layers/pallas_call | solution.py:421
  167.1 2.8 slice_bitcast_fusion
  170.1 1.3 collective-permute-start.4
  172.0 2.0 collective-permute-start.6
  174.0 21.8 %collective-permute-done.6.act_other_ref = bf16[64,512]{1,0:T(8,128)(2,1)S(1)} collective-permute-done((bf16[64,512]{1,0:T(8,128)(2,1)S(1)}, bf16[64,512]{1,0:T(8,128)(2,1)S(1)}, u32[]{:S(2)}, u32[]{:S(2)}) %collective-permute-start.6) | collective-permute-done | bytes 65568 | tf_op jit(solution)/shard_map/ppermute | solution.py:271
  195.8 7.1 %collective-permute-done.4.arrived_ref = bf16[64,8192]{1,0:T(8,128)(2,1)S(1)} collective-permute-done((bf16[64,8192]{1,0:T(8,128)(2,1)S(1)}, bf16[64,8192]{1,0:T(8,128)(2,1)S(1)}, u32[]{:S(2)}, u32[]{:S(2)}) %collective-permute-start.4) | collective-permute-done | bytes 1048608 | tf_op jit(solution)/shard_map/ppermute | solution.py:422
  203.9 13.6 %backward_high.1 = (bf16[64,512]{1,0:T(8,128)(2,1)}, bf16[64,8192]{1,0:T(8,128)(2,1)}, bf16[64,8192]{1,0:T(8,128)(2,1)}, bf16[64,8192]{1,0:T(8,128)(2,1)}) custom-call(s32[2]{0:T(128)} %pad_add_fusion.2.swap_ref, s32[1024]{0:T(1024)} %compare_select_fusion.where_ref, bf16[64,8192]{1,0:T(8,128)(2,1)} %get-tuple-element.27.hidden_ref, ...), custom_call_target="tpu_custom_call" | custom-call | flops 1073741824 | bytes 10485760 | tf_op jit(solution)/shard_map/backward_high/pallas_call | solution.py:425
  218.9 7.9 %backward_low.1 = (bf16[64,512]{1,0:T(8,128)(2,1)}, bf16[64,512]{1,0:T(8,128)(2,1)}) custom-call(s32[2]{0:T(128)} %pad_add_fusion.2.swap_ref, s32[1024]{0:T(1024)} %compare_select_fusion.where_ref, bf16[64,8192]{1,0:T(8,128)(2,1)} %get-tuple-element.31.middle_ref, bf16[64,512]{1,0:T(8,128)(2,1)} %get-tuple-element.32.high_ref, ...), custom_call_target="tpu_custom_call" | custom-call | flops 536870912 | bytes 20971520 | tf_op jit(solution)/shard_map/backward_low/pallas_call | solution.py:427
  228.4 14.6 %collective-permute-done.8.dpre_other_ref = bf16[64,512]{1,0:T(8,128)(2,1)S(1)} collective-permute-done((bf16[64,512]{1,0:T(8,128)(2,1)}, bf16[64,512]{1,0:T(8,128)(2,1)S(1)}, u32[]{:S(2)}, u32[]{:S(2)}) %collective-permute-start.8) | collective-permute-done | bytes 65568 | tf_op jit(solution)/shard_map/ppermute | solution.py:271
  243.7 7.5 %gradient_in.1 = (bf16[4,4,5,128,128]{4,3,2,1,0:T(8,128)(2,1)}, bf16[4,4,5,128,128]{4,3,2,1,0:T(8,128)(2,1)}) custom-call(s32[160]{0:T(256)} %reshape.142.places_ref, bf16[64,8192]{1,0:T(8,128)(2,1)} %get-tuple-element.59.own_ref, bf16[64,8192]{1,0:T(8,128)(2,1)} %copy-done.10, bf16[64,512]{1,0:T(8,128)(2,1)} %get-tuple-element.33.dpre_own_ref, ...), custom_call_target="tpu_custom_call" | custom-call | flops 1073741824 | bytes 62914560 | tf_op jit(solution)/shard_map/gradient_in/pallas_call | solution.py:430
  251.9 7.7 %gradient_out.1 = (bf16[4,4,5,128,128]{4,3,2,1,0:T(8,128)(2,1)}, bf16[4,4,5,128,128]{4,3,2,1,0:T(8,128)(2,1)}) custom-call(s32[160]{0:T(256)} %reshape.145.places_ref, bf16[64,512]{1,0:T(8,128)(2,1)} %get-tuple-element.60.act_own_ref, bf16[64,512]{1,0:T(8,128)(2,1)} %copy-done.13, bf16[64,8192]{1,0:T(8,128)(2,1)} %get-tuple-element.40.own_ref, ...), custom_call_target="tpu_custom_call" | custom-call | flops 1073741824 | bytes 62914560 | tf_op jit(solution)/shard_map/gradient_out/pallas_call | solution.py:431
  261.3 2.8 collective-permute-start.12
  265.8 1.4 add_convert_fusion.3
  267.3 1.6 collective-permute-start.19
  269.5 22.9 %collective-permute-done.12 = bf16[4,5,128,128]{3,2,1,0:T(8,128)(2,1)S(1)} collective-permute-done((bf16[4,5,128,128]{3,2,1,0:T(8,128)(2,1)S(1)}, bf16[4,5,128,128]{3,2,1,0:T(8,128)(2,1)S(1)}, u32[]{:S(2)}, u32[]{:S(2)}) %collective-permute-start.12) | collective-permute-done | bytes 655392 | tf_op jit(solution)/shard_map/ppermute | solution.py:263
  292.4 3.7 %collective-permute-done.10 = bf16[4,5,128,128]{3,2,1,0:T(8,128)(2,1)S(1)} collective-permute-done((bf16[4,5,128,128]{3,2,1,0:T(8,128)(2,1)S(1)}, bf16[4,5,128,128]{3,2,1,0:T(8,128)(2,1)S(1)}, u32[]{:S(2)}, u32[]{:S(2)}) %collective-permute-start.10) | collective-permute-done | bytes 655392 | tf_op jit(solution)/shard_map/ppermute | solution.py:263
  296.5 3.2 collective-permute-start.15
  299.8 9.7 %collective-permute-done.17 = bf16[4,5,128,128]{3,2,1,0:T(8,128)(2,1)S(1)} collective-permute-done((bf16[4,5,128,128]{3,2,1,0:T(8,128)(2,1)S(1)}, bf16[4,5,128,128]{3,2,1,0:T(8,128)(2,1)S(1)}, u32[]{:S(2)}, u32[]{:S(2)}) %collective-permute-start.17) | collective-permute-done | bytes 655392 | tf_op jit(solution)/shard_map/ppermute | solution.py:263
  309.9 9.0 %collective-permute-start.22 = (bf16[5,128,128]{2,1,0:T(8,128)(2,1)S(1)}, bf16[5,128,128]{2,1,0:T(8,128)(2,1)S(1)}, u32[]{:S(2)}, u32[]{:S(2)}) collective-permute-start(bf16[5,128,128]{2,1,0:T(8,128)(2,1)S(1)} %get-tuple-element.53), channel_id=1, source_target_pairs={{0,6},{1,7},{2,0},{3,1},{4,2},{5,3},{6,4},{7,5},{8,14},{9,15},{10,... | collective-permute-start | bytes 491528 | tf_op jit(solution)/shard_map/ppermute | solution.py:263
  318.9 1.5 collective-permute-start.21
  321.2 1.5 collective-permute-done.20
  322.7 3.0 collective-permute-done.21
  (84 shorter events, 18.3 us)
Async XLA Ops:
  7.2 14.1 %copy-start = (bf16[128,8192]{1,0:T(8,128)(2,1)S(1)}, bf16[128,8192]{1,0:T(8,128)(2,1)}, u32[]{:S(2)}) copy-start(bf16[128,8192]{1,0:T(8,128)(2,1)} %param.6) | copy-start | bytes 6291460
  7.2 11.6 %copy-start.8 = (s32[1,5]{1,0:T(1,128)S(1)}, s32[1,5]{1,0:T(1,128)}, u32[]{:S(2)}) copy-start(s32[1,5]{1,0:T(1,128)} %param.10) | copy-start | bytes 64
  7.2 11.6 %copy-start.9 = (s32[1,5]{1,0:T(1,128)S(1)}, s32[1,5]{1,0:T(1,128)}, u32[]{:S(2)}) copy-start(s32[1,5]{1,0:T(1,128)} %param.9) | copy-start | bytes 64
  7.2 96.9 %all-gather.4.cloned.1.call-start = ((), (), s32[]{:S(2)}) async-start(), calls=%async_computation | async-start | bytes 21626880 | tf_op jit(solution)/shard_map/all_gather | solution.py:284
  7.2 7.4 %collective-permute-start.2 = (bf16[5,128,128]{2,1,0:T(8,128)(2,1)}, bf16[5,128,128]{2,1,0:T(8,128)(2,1)S(1)}, u32[]{:S(2)}, u32[]{:S(2)}) collective-permute-start(bf16[5,128,128]{2,1,0:T(8,128)(2,1)} %bitcast.120), channel_id=1, source_target_pairs={{0,32},{32,0},{64,96},{96,64},{1,33},{33,1},{65,97},{97,65},{2,34}... | collective-permute-start | bytes 491528 | tf_op jit(solution)/shard_map/ppermute | solution.py:271
  8.9 7.9 %collective-permute-start.1 = (bf16[5,128,128]{2,1,0:T(8,128)(2,1)}, bf16[5,128,128]{2,1,0:T(8,128)(2,1)S(1)}, u32[]{:S(2)}, u32[]{:S(2)}) collective-permute-start(bf16[5,128,128]{2,1,0:T(8,128)(2,1)} %bitcast.121), channel_id=1, source_target_pairs={{0,32},{32,0},{64,96},{96,64},{1,33},{33,1},{65,97},{97,65},{2,34}... | collective-permute-start | bytes 491528 | tf_op jit(solution)/shard_map/ppermute | solution.py:271
  18.8 3.6 %collective-permute-start = (s32[2,5]{1,0:T(2,128)S(1)}, s32[2,5]{1,0:T(2,128)S(1)}, u32[]{:S(2)}, u32[]{:S(2)}) collective-permute-start(s32[2,5]{1,0:T(2,128)S(1)} %get-tuple-element.65), channel_id=1, source_target_pairs={{0,32},{32,0},{64,96},{96,64},{1,33},{33,1},{65,97},{97,65},{2,34}... | collective-permute-start | bytes 128 | tf_op jit(solution)/shard_map/ppermute | solution.py:271
  104.1 16.9 %copy-start.6 = (bf16[128,8192]{1,0:T(8,128)(2,1)S(1)}, bf16[128,8192]{1,0:T(8,128)(2,1)}, u32[]{:S(2)}) copy-start(bf16[128,8192]{1,0:T(8,128)(2,1)} %param.11) | copy-start | bytes 6291460
  116.4 27.7 %collective-permute-start.3 = (bf16[64,8192]{1,0:T(8,128)(2,1)}, bf16[64,8192]{1,0:T(8,128)(2,1)S(1)}, u32[]{:S(2)}, u32[]{:S(2)}) collective-permute-start(bf16[64,8192]{1,0:T(8,128)(2,1)} %forward_layers.1), channel_id=1, source_target_pairs={{0,96},{32,64},{1,97},{33,65},{2,98},{34,66},{3,99},{35,67},{4,100... | collective-permute-start | bytes 3145736 | tf_op jit(solution)/shard_map/ppermute | solution.py:420
  169.9 25.9 %collective-permute-start.5 = (bf16[64,8192]{1,0:T(8,128)(2,1)S(1)}, bf16[64,8192]{1,0:T(8,128)(2,1)S(1)}, u32[]{:S(2)}, u32[]{:S(2)}) collective-permute-start(bf16[64,8192]{1,0:T(8,128)(2,1)S(1)} %get-tuple-element.58), channel_id=1, source_target_pairs={{0,32},{32,0},{64,96},{96,64},{1,33},{33,1},{65,97},{97,65},{2,34}... | collective-permute-start | bytes 3145736 | tf_op jit(solution)/shard_map/ppermute | solution.py:271
  170.1 32.7 %collective-permute-start.4 = (bf16[64,8192]{1,0:T(8,128)(2,1)S(1)}, bf16[64,8192]{1,0:T(8,128)(2,1)S(1)}, u32[]{:S(2)}, u32[]{:S(2)}) collective-permute-start(bf16[64,8192]{1,0:T(8,128)(2,1)S(1)} %copy-done.12), channel_id=1, source_target_pairs={{96,0},{64,32},{97,1},{65,33},{98,2},{66,34},{99,3},{67,35},{100,4... | collective-permute-start | bytes 3145736 | tf_op jit(solution)/shard_map/ppermute | solution.py:422
  172.0 23.7 %collective-permute-start.6 = (bf16[64,512]{1,0:T(8,128)(2,1)S(1)}, bf16[64,512]{1,0:T(8,128)(2,1)S(1)}, u32[]{:S(2)}, u32[]{:S(2)}) collective-permute-start(bf16[64,512]{1,0:T(8,128)(2,1)S(1)} %get-tuple-element.61), channel_id=1, source_target_pairs={{0,32},{32,0},{64,96},{96,64},{1,33},{33,1},{65,97},{97,65},{2,34}... | collective-permute-start | bytes 196616 | tf_op jit(solution)/shard_map/ppermute | solution.py:271
  195.8 21.7 %copy-start.13 = (bf16[64,512]{1,0:T(8,128)(2,1)}, bf16[64,512]{1,0:T(8,128)(2,1)S(1)}, u32[]{:S(2)}) copy-start(bf16[64,512]{1,0:T(8,128)(2,1)S(1)} %collective-permute-done.6.act_other_ref) | copy-start | bytes 196612
  195.8 21.7 %copy-start.10 = (bf16[64,8192]{1,0:T(8,128)(2,1)}, bf16[64,8192]{1,0:T(8,128)(2,1)S(1)}, u32[]{:S(2)}) copy-start(bf16[64,8192]{1,0:T(8,128)(2,1)S(1)} %collective-permute-done.5.other_ref) | copy-start | bytes 3145732
  217.5 25.6 %collective-permute-start.7 = (bf16[64,8192]{1,0:T(8,128)(2,1)}, bf16[64,8192]{1,0:T(8,128)(2,1)S(1)}, u32[]{:S(2)}, u32[]{:S(2)}) collective-permute-start(bf16[64,8192]{1,0:T(8,128)(2,1)} %get-tuple-element.34), channel_id=1, source_target_pairs={{0,32},{32,0},{64,96},{96,64},{1,33},{33,1},{65,97},{97,65},{2,34}... | collective-permute-start | bytes 3145736 | tf_op jit(solution)/shard_map/ppermute | solution.py:271
  226.8 16.3 %collective-permute-start.8 = (bf16[64,512]{1,0:T(8,128)(2,1)}, bf16[64,512]{1,0:T(8,128)(2,1)S(1)}, u32[]{:S(2)}, u32[]{:S(2)}) collective-permute-start(bf16[64,512]{1,0:T(8,128)(2,1)} %get-tuple-element.35), channel_id=1, source_target_pairs={{0,32},{32,0},{64,96},{96,64},{1,33},{33,1},{65,97},{97,65},{2,34}... | collective-permute-start | bytes 196616 | tf_op jit(solution)/shard_map/ppermute | solution.py:271
  243.1 8.1 %copy-start.11 = (bf16[64,8192]{1,0:T(8,128)(2,1)}, bf16[64,8192]{1,0:T(8,128)(2,1)S(1)}, u32[]{:S(2)}) copy-start(bf16[64,8192]{1,0:T(8,128)(2,1)S(1)} %collective-permute-done.7.other_ref) | copy-start | bytes 3145732
  251.2 9.1 %collective-permute-start.9 = (bf16[4,4,5,128,128]{4,3,2,1,0:T(8,128)(2,1)}, bf16[4,4,5,128,128]{4,3,2,1,0:T(8,128)(2,1)S(1)}, u32[]{:S(2)}, u32[]{:S(2)}) collective-permute-start(bf16[4,4,5,128,128]{4,3,2,1,0:T(8,128)(2,1)} %get-tuple-element.38), channel_id=1, source_target_pairs={{0,1},{1,0},{2,3},{3,2},{4,5},{5,4},{6,7},{7,6},{8,9},{9,8},{10,11... | collective-permute-start | bytes 7864328 | tf_op jit(solution)/shard_map/ppermute | solution.py:412
  251.8 8.4 %copy-start.3 = (bf16[4,4,5,128,128]{4,3,2,1,0:T(8,128)(2,1)S(1)}, bf16[4,4,5,128,128]{4,3,2,1,0:T(8,128)(2,1)}, u32[]{:S(2)}) copy-start(bf16[4,4,5,128,128]{4,3,2,1,0:T(8,128)(2,1)} %get-tuple-element.37) | copy-start | bytes 7864324
  259.5 6.3 %collective-permute-start.16 = (bf16[4,4,5,128,128]{4,3,2,1,0:T(8,128)(2,1)}, bf16[4,4,5,128,128]{4,3,2,1,0:T(8,128)(2,1)S(1)}, u32[]{:S(2)}, u32[]{:S(2)}) collective-permute-start(bf16[4,4,5,128,128]{4,3,2,1,0:T(8,128)(2,1)} %get-tuple-element.43), channel_id=1, source_target_pairs={{0,1},{1,0},{2,3},{3,2},{4,5},{5,4},{6,7},{7,6},{8,9},{9,8},{10,11... | collective-permute-start | bytes 7864328 | tf_op jit(solution)/shard_map/ppermute | solution.py:412
  261.3 31.1 %collective-permute-start.12 = (bf16[4,5,128,128]{3,2,1,0:T(8,128)(2,1)S(1)}, bf16[4,5,128,128]{3,2,1,0:T(8,128)(2,1)S(1)}, u32[]{:S(2)}, u32[]{:S(2)}) collective-permute-start(bf16[4,5,128,128]{3,2,1,0:T(8,128)(2,1)S(1)} %get-tuple-element.49), channel_id=1, source_target_pairs={{0,6},{1,7},{2,0},{3,1},{4,2},{5,3},{6,4},{7,5},{8,14},{9,15},{10,... | collective-permute-start | bytes 1966088 | tf_op jit(solution)/shard_map/ppermute | solution.py:263
  264.1 28.3 %collective-permute-start.11 = (bf16[4,5,128,128]{3,2,1,0:T(8,128)(2,1)S(1)}, bf16[4,5,128,128]{3,2,1,0:T(8,128)(2,1)S(1)}, u32[]{:S(2)}, u32[]{:S(2)}) collective-permute-start(bf16[4,5,128,128]{3,2,1,0:T(8,128)(2,1)S(1)} %get-tuple-element.50), channel_id=1, source_target_pairs={{0,4},{1,5},{2,6},{3,7},{4,0},{5,1},{6,2},{7,3},{8,12},{9,13},{10,... | collective-permute-start | bytes 1966088 | tf_op jit(solution)/shard_map/ppermute | solution.py:263
  264.9 31.2 %collective-permute-start.10 = (bf16[4,5,128,128]{3,2,1,0:T(8,128)(2,1)S(1)}, bf16[4,5,128,128]{3,2,1,0:T(8,128)(2,1)S(1)}, u32[]{:S(2)}, u32[]{:S(2)}) collective-permute-start(bf16[4,5,128,128]{3,2,1,0:T(8,128)(2,1)S(1)} %get-tuple-element.51), channel_id=1, source_target_pairs={{0,2},{1,3},{2,4},{3,5},{4,6},{5,7},{6,0},{7,1},{8,10},{9,11},{10,... | collective-permute-start | bytes 1966088 | tf_op jit(solution)/shard_map/ppermute | solution.py:263
  267.3 32.5 %collective-permute-start.19 = (bf16[4,5,128,128]{3,2,1,0:T(8,128)(2,1)S(1)}, bf16[4,5,128,128]{3,2,1,0:T(8,128)(2,1)S(1)}, u32[]{:S(2)}, u32[]{:S(2)}) collective-permute-start(bf16[4,5,128,128]{3,2,1,0:T(8,128)(2,1)S(1)} %get-tuple-element.45), channel_id=1, source_target_pairs={{0,24},{1,25},{2,26},{3,27},{4,28},{5,29},{6,30},{7,31},{8,0},{9,1... | collective-permute-start | bytes 1966088 | tf_op jit(solution)/shard_map/ppermute | solution.py:263
  268.8 30.9 %collective-permute-start.18 = (bf16[4,5,128,128]{3,2,1,0:T(8,128)(2,1)S(1)}, bf16[4,5,128,128]{3,2,1,0:T(8,128)(2,1)S(1)}, u32[]{:S(2)}, u32[]{:S(2)}) collective-permute-start(bf16[4,5,128,128]{3,2,1,0:T(8,128)(2,1)S(1)} %get-tuple-element.46), channel_id=1, source_target_pairs={{0,16},{1,17},{2,18},{3,19},{4,20},{5,21},{6,22},{7,23},{8,24},{9,... | collective-permute-start | bytes 1966088 | tf_op jit(solution)/shard_map/ppermute | solution.py:263
  292.4 17.1 %collective-permute-start.17 = (bf16[4,5,128,128]{3,2,1,0:T(8,128)(2,1)S(1)}, bf16[4,5,128,128]{3,2,1,0:T(8,128)(2,1)S(1)}, u32[]{:S(2)}, u32[]{:S(2)}) collective-permute-start(bf16[4,5,128,128]{3,2,1,0:T(8,128)(2,1)S(1)} %get-tuple-element.47), channel_id=1, source_target_pairs={{0,8},{1,9},{2,10},{3,11},{4,12},{5,13},{6,14},{7,15},{8,16},{9,17... | collective-permute-start | bytes 1966088 | tf_op jit(solution)/shard_map/ppermute | solution.py:263
  296.4 22.4 %collective-permute-start.13 = (bf16[5,128,128]{2,1,0:T(8,128)(2,1)S(1)}, bf16[5,128,128]{2,1,0:T(8,128)(2,1)S(1)}, u32[]{:S(2)}, u32[]{:S(2)}) collective-permute-start(bf16[5,128,128]{2,1,0:T(8,128)(2,1)S(1)} %get-tuple-element.55), channel_id=1, source_target_pairs={{0,8},{1,9},{2,10},{3,11},{4,12},{5,13},{6,14},{7,15},{8,16},{9,17... | collective-permute-start | bytes 491528 | tf_op jit(solution)/shard_map/ppermute | solution.py:263
  296.5 23.8 %collective-permute-start.15 = (bf16[5,128,128]{2,1,0:T(8,128)(2,1)S(1)}, bf16[5,128,128]{2,1,0:T(8,128)(2,1)S(1)}, u32[]{:S(2)}, u32[]{:S(2)}) collective-permute-start(bf16[5,128,128]{2,1,0:T(8,128)(2,1)S(1)} %get-tuple-element.56), channel_id=1, source_target_pairs={{0,24},{1,25},{2,26},{3,27},{4,28},{5,29},{6,30},{7,31},{8,0},{9,1... | collective-permute-start | bytes 491528 | tf_op jit(solution)/shard_map/ppermute | solution.py:263
  299.7 20.6 %collective-permute-start.14 = (bf16[5,128,128]{2,1,0:T(8,128)(2,1)S(1)}, bf16[5,128,128]{2,1,0:T(8,128)(2,1)S(1)}, u32[]{:S(2)}, u32[]{:S(2)}) collective-permute-start(bf16[5,128,128]{2,1,0:T(8,128)(2,1)S(1)} %get-tuple-element.57), channel_id=1, source_target_pairs={{0,16},{1,17},{2,18},{3,19},{4,20},{5,21},{6,22},{7,23},{8,24},{9,... | collective-permute-start | bytes 491528 | tf_op jit(solution)/shard_map/ppermute | solution.py:263
  309.8 12.9 %collective-permute-start.20 = (bf16[5,128,128]{2,1,0:T(8,128)(2,1)S(1)}, bf16[5,128,128]{2,1,0:T(8,128)(2,1)S(1)}, u32[]{:S(2)}, u32[]{:S(2)}) collective-permute-start(bf16[5,128,128]{2,1,0:T(8,128)(2,1)S(1)} %get-tuple-element.52), channel_id=1, source_target_pairs={{0,2},{1,3},{2,4},{3,5},{4,6},{5,7},{6,0},{7,1},{8,10},{9,11},{10,... | collective-permute-start | bytes 491528 | tf_op jit(solution)/shard_map/ppermute | solution.py:263
  309.9 12.8 %collective-permute-start.22 = (bf16[5,128,128]{2,1,0:T(8,128)(2,1)S(1)}, bf16[5,128,128]{2,1,0:T(8,128)(2,1)S(1)}, u32[]{:S(2)}, u32[]{:S(2)}) collective-permute-start(bf16[5,128,128]{2,1,0:T(8,128)(2,1)S(1)} %get-tuple-element.53), channel_id=1, source_target_pairs={{0,6},{1,7},{2,0},{3,1},{4,2},{5,3},{6,4},{7,5},{8,14},{9,15},{10,... | collective-permute-start | bytes 491528 | tf_op jit(solution)/shard_map/ppermute | solution.py:263
  318.9 6.8 %collective-permute-start.21 = (bf16[5,128,128]{2,1,0:T(8,128)(2,1)S(1)}, bf16[5,128,128]{2,1,0:T(8,128)(2,1)S(1)}, u32[]{:S(2)}, u32[]{:S(2)}) collective-permute-start(bf16[5,128,128]{2,1,0:T(8,128)(2,1)S(1)} %get-tuple-element.54), channel_id=1, source_target_pairs={{0,4},{1,5},{2,6},{3,7},{4,0},{5,1},{6,2},{7,3},{8,12},{9,13},{10,... | collective-permute-start | bytes 491528 | tf_op jit(solution)/shard_map/ppermute | solution.py:263
  (7 other events, 23.1 us)
Sparse Core Ops, SparseCore 0:
  18.9 85.1 all-gather.3

commit v7 on v6

--- a/solution.py
+++ b/solution.py
@@ -25,6 +25,8 @@
 RING = 4
 Y = 2
 Z = 8
+NEAR = ((0, 3, 1, 2), (0, 1, 3, 2))
+FAR = ((0, 3), (1, 2))
 CORES = [(i, i ^ 1) for i in range(Z * RING)]
 
 
@@ -144,7 +146,7 @@
 
 
 def turn_kernel(
-    swap_ref, where_ref, tokens_ref, arrived_ref, grad_ref, source, second_ref, pre_ref, inverse_ref, normed_ref, act_ref, earlier_ref, first_ref, middle_ref, held, sems
+    swap_ref, where_ref, tokens_ref, arrived_ref, grad_ref, source, second_ref, pre_ref, inverse_ref, normed_own_ref, normed_other_ref, act_own_ref, act_other_ref, earlier_ref, first_ref, middle_ref, normed_ref, act_ref, held, sems
 ):
     weights = Weights(swap_ref, where_ref, source, held, sems, [(0, 0), (0, 1), (1, 0), (1, 1)])
     choose(swap_ref[1] > 0, arrived_ref, tokens_ref, first_ref, sems.at[4])
@@ -157,6 +159,10 @@
         act_ref[place] = act
         if layer == 0:
             forward_up(weights, 0, first_ref, act, second_ref)
+    act_own_ref[...], act_other_ref[...] = act_ref[0], act_ref[1]
+    for _, cols in chunks():
+        normed_own_ref[:, cols] = normed_ref[0, :, cols]
+        normed_other_ref[:, cols] = normed_ref[1, :, cols]
     weights.wait(1, 1)
     backward(weights, 1, second_ref, grad_ref, pre_ref[1], inverse_ref[1][:, :1], middle_ref)
     backward(weights, 0, first_ref, middle_ref, pre_ref[0], inverse_ref[0][:, :1], earlier_ref)
@@ -187,18 +193,27 @@
     sent_ref[...] = lax.select(even, high, low)
 
 
-def pick(places_ref, dense, keep_ref, send_ref):
+def by_step(values):
     step = pl.program_id(0)
-    pieces, slots = keep_ref.shape[1], keep_ref.shape[2]
-    count = places_ref.shape[0] // 2
-    for half, out_ref in enumerate((keep_ref, send_ref)):
-        for piece in range(pieces):
-            for slot in range(slots):
-                index = half * count + step * pieces * slots + piece * slots + slot
-                out_ref[0, piece, slot] = dense[places_ref[index]]
-
-
-def gradient_in_kernel(places_ref, own_ref, other_ref, dpre_own_ref, dpre_other_ref, keep_ref, send_ref, dense):
+    result = values[0]
+    for i, value in enumerate(values[1:], 1):
+        result = lax.select(step == i, jnp.int32(value), jnp.int32(result))
+    return result
+
+
+def pick(spots_ref, places_ref, strides, dense, keep_ref, send_ref):
+    slots = keep_ref.shape[2]
+    for which in range(2):
+        near = spots_ref[0] ^ by_step([group[step * 2 + which] for group in NEAR for step in range(2)])
+        for other in range(2):
+            far = spots_ref[1] ^ by_step([group[other] for group in FAR for _ in range(2)])
+            for half, out_ref in enumerate((keep_ref, send_ref)):
+                owner = near * strides[0] + far * strides[1] + (spots_ref[2] ^ half)
+                for slot in range(slots):
+                    out_ref[0, which * 2 + other, slot] = dense[places_ref[owner * slots + slot]]
+
+
+def gradient_in_kernel(spots_ref, places_ref, own_ref, other_ref, dpre_own_ref, dpre_other_ref, keep_ref, send_ref, dense):
     @pl.when(pl.program_id(0) == 0)
     def _():
         dense[NBLK] = jnp.zeros((BLOCK, BLOCK), jnp.bfloat16)
@@ -212,11 +227,11 @@
                         row * BLOCK : (row + 1) * BLOCK, col * BLOCK : (col + 1) * BLOCK
                     ]
 
-    pick(places_ref, dense, keep_ref, send_ref)
+    pick(spots_ref, places_ref, (Y, Z), dense, keep_ref, send_ref)
 
 
 def gradient_out_kernel(
-    places_ref, act_own_ref, act_other_ref, own_ref, other_ref, keep_ref, send_ref, dense, turned
+    spots_ref, places_ref, act_own_ref, act_other_ref, own_ref, other_ref, keep_ref, send_ref, dense, turned
 ):
     @pl.when(pl.program_id(0) == 0)
     def _():
@@ -232,7 +247,7 @@
                         row * BLOCK : (row + 1) * BLOCK, col * BLOCK : (col + 1) * BLOCK
                     ]
 
-    pick(places_ref, dense, keep_ref, send_ref)
+    pick(spots_ref, places_ref, (Z, Y), dense, keep_ref, send_ref)
 
 
 def whole(*shape):
@@ -248,19 +263,11 @@
     )
 
 
-def turn_axis(array, axis, start):
-    size = array.shape[axis]
-    return lax.dynamic_slice_in_dim(jnp.concatenate([array, array], axis), start, size, axis)
-
-
-def around(array, stride, distance):
-    if distance == 0:
+def across(array, stride, flip):
+    if flip == 0:
         return array
-    route = []
-    for i in range(lax.axis_size("dp")):
-        place = i // stride % RING
-        route.append((i, i + ((place + distance) % RING - place) * stride))
-    return lax.ppermute(array, "dp", route)
+    devices = range(lax.axis_size("dp"))
+    return lax.ppermute(array, "dp", [(i, i + ((i // stride % RING ^ flip) - i // stride % RING) * stride) for i in devices])
 
 
 def rounded_sum(*terms):
@@ -288,13 +295,11 @@
     named = places[..., None] == jnp.arange(NBLK, dtype=jnp.int32)
     where = jnp.max(jnp.where(named, codes[..., None], -1), axis=(2, 3)).reshape(-1)
     where = jnp.where(where < 0, owners * 8, where)
+    places_in, places_out = places[0, 0].reshape(-1), places[0, 1].reshape(-1)
     me = lax.axis_index("dp")
-    mine = places[0].reshape(2, RING, RING, 2, slots)
-    mine = turn_axis(mine, 1, me // Z)
-    mine = turn_axis(mine, 2, (me // Y) % RING)
-    mine = turn_axis(mine, 3, me % Y)
-    places_in = mine[0].transpose(2, 1, 0, 3).reshape(-1)
-    places_out = mine[1].transpose(2, 0, 1, 3).reshape(-1)
+    spot_z, spot_y, spot_core = me // Z, me // Y % RING, me % Y
+    spots_in = jnp.stack([spot_y, spot_z, spot_core]).astype(jnp.int32)
+    spots_out = jnp.stack([spot_z, spot_y, spot_core]).astype(jnp.int32)
 
     first_tokens = lax.dynamic_slice_in_dim(tokens, half, rows, 0)
     last_grads = lax.dynamic_slice_in_dim(cotangent, half, rows, 0)
@@ -331,8 +336,10 @@
             shape(rows, D),
             shape(2, rows, RANK, dtype=jnp.float32),
             shape(2, rows, BLOCK, dtype=jnp.float32),
-            shape(2, rows, D),
-            shape(2, rows, RANK),
+            shape(rows, D),
+            shape(rows, D),
+            shape(rows, RANK),
+            shape(rows, RANK),
             shape(rows, D),
         ),
         grid_spec=pltpu.PrefetchScalarGridSpec(
@@ -343,11 +350,15 @@
                 whole(rows, D),
                 whole(2, rows, RANK),
                 whole(2, rows, BLOCK),
-                whole(2, rows, D),
-                whole(2, rows, RANK),
+                whole(rows, D),
+                whole(rows, D),
+                whole(rows, RANK),
+                whole(rows, RANK),
                 whole(rows, D),
             ],
-            scratch_shapes=[pltpu.VMEM((rows, D), jnp.bfloat16)] * 2 + held(4),
+            scratch_shapes=[pltpu.VMEM((rows, D), jnp.bfloat16)] * 2
+            + [pltpu.VMEM((2, rows, D), jnp.bfloat16), pltpu.VMEM((2, rows, RANK), jnp.bfloat16)]
+            + held(4),
         ),
         name="turn_layers",
         **params(7 * work, moved),
@@ -381,7 +392,7 @@
     )
 
     halves = shape(RING, RING, slots, BLOCK, BLOCK)
-    half_spec = pl.BlockSpec((1, RING, slots, BLOCK, BLOCK), lambda step, _: (step, 0, 0, 0, 0))
+    half_spec = pl.BlockSpec((1, RING, slots, BLOCK, BLOCK), lambda step, *_: (step, 0, 0, 0, 0))
     dense = pltpu.VMEM((NBLK + 1, BLOCK, BLOCK), jnp.bfloat16)
 
     def gradient(kernel, name, in_specs, scratch):
@@ -389,7 +400,7 @@
             kernel,
             out_shape=(halves, halves),
             grid_spec=pltpu.PrefetchScalarGridSpec(
-                num_scalar_prefetch=1,
+                num_scalar_prefetch=2,
                 grid=(RING,),
                 in_specs=in_specs,
                 out_specs=(half_spec, half_spec),
@@ -413,22 +424,27 @@
         return [rounded_sum(keep[i], arrived[i]) for i in range(RING)]
 
     def scattered(pieces, near, far):
-        terms = [around(piece, near, distance) for distance, piece in enumerate(pieces)]
-        pieces = [rounded_sum(*[term[i] for term in terms]) for i in range(RING)]
-        return rounded_sum(*[around(piece, far, distance) for distance, piece in enumerate(pieces)])[None]
+        sums = []
+        for kept, sent, (_, second, first, _) in zip(pieces[::2], pieces[1::2], NEAR):
+            arrived = across(sent, near, first)
+            mine = rounded_sum(kept[:2], arrived[:2])
+            arrived = across(rounded_sum(kept[2:], arrived[2:]), near, second)
+            sums += [rounded_sum(mine[i], arrived[i]) for i in range(2)]
+        return rounded_sum(*[across(term, far, step) for term, step in zip(sums, FAR[0] + FAR[1])])[None]
 
     arrived = lax.ppermute(forward(swap, where, first_tokens, weights), "section", UP)
-    second, pre, inverse, normed, act, leaving = turn(swap, where, first_tokens, arrived, last_grads, weights)
+    second, pre, inverse, normed_own, normed_sent, act_own, act_sent, leaving = turn(swap, where, first_tokens, arrived, last_grads, weights)
     arrived = lax.ppermute(leaving, "section", DOWN)
-    arrived, normed_other, act_other = lax.optimization_barrier((arrived, swapped(normed[1]), swapped(act[1])))
+    normed_sent, act_other = lax.optimization_barrier((normed_sent, swapped(act_sent)))
+    arrived, normed_other = lax.optimization_barrier((arrived, swapped(normed_sent)))
 
     dpre_high, middle, grads_own, sent = high(swap, where, second, last_grads, arrived, pre, inverse, weights)
     grads_other = swapped(sent)
     dpre_own, dpre_sent = low(swap, where, middle, dpre_high, pre, weights)
     grads_other, dpre_other = lax.optimization_barrier((grads_other, swapped(dpre_sent)))
 
-    halves_in = gradient_in(places_in, normed[0], normed_other, dpre_own, dpre_other)
-    halves_out = gradient_out(places_out, act[0], act_other, grads_own, grads_other)
+    halves_in = gradient_in(spots_in, places_in, normed_own, normed_other, dpre_own, dpre_other)
+    halves_out = gradient_out(spots_out, places_out, act_own, act_other, grads_own, grads_other)
     pieces_in, pieces_out = core_sums(*halves_in), core_sums(*halves_out)
     sums_in = scattered(pieces_in, Y, Z)
     sums_out = scattered(pieces_out, Z, Y)

time: 340 us -> 321 us (0.944)
  the two profiles are of different devices: /device:TPU:0 before, /device:TPU:32 now
where the time goes in v7:
time: 321 us; the launch traced here: 315 us
  waiting for transfers between devices  151 us (47%)
  Pallas kernels  71.2 us (22%)
  starting transfers between devices  37.9 us (12%)
  blocking collectives  25 us (8%)
  between operations  14.7 us (5%)
  other arithmetic  9.02 us (3%)
  local copies, waits for them, and re-layouts  6.3 us (2%)
    all_gather x1, waiting for transfers between devices, per_device(): lax.all_gather(both, 'dp', axis=0)  54.5 us
    ppermute x1, waiting for transfers between devices, per_device(): arrived = lax.ppermute(leaving, 'section', DOWN)  28.5 us
    ppermute x7, waiting for transfers between devices, swapped(): return lax.ppermute(array, 'section', PAIR)  25.3 us
    all_gather x1, blocking collectives, per_device(): lax.all_gather(jnp.stack([own_places, swapped(own_places)]), 'dp', axis=0)  25 us
    ppermute x14, starting transfers between devices, across(): lax.ppermute(array, 'dp', [(i, i + ((i // stride % RING ^ flip) - i // st...  24.7 us
    pallas_call x1, Pallas kernels, per_device(): turn(swap, where, first_tokens, arrived, last_grads, weights)  22.2 us
    ppermute x1, waiting for transfers between devices, per_device(): lax.ppermute(forward(swap, where, first_tokens, weights), 'section', UP)  21.9 us
    ppermute x14, waiting for transfers between devices, across(): lax.ppermute(array, 'dp', [(i, i + ((i // stride % RING ^ flip) - i // st...  19.3 us
  transfers between devices with their start and end apart: 26, of which 16 were waited for; matrix products, arithmetic and copies ran while one was open for 3% of the time, Pallas kernels for 5%

profile of v7, /device:TPU:32, one launch (start us, length us, event | category | flops | bytes accessed | tf_op | source)
XLA Modules:
  0.0 315.2 jit_solution(5952754823290746540)
XLA Ops:
  7.2 1.6 collective-permute-start.2
  9.4 5.3 %collective-permute-done.2 = bf16[5,128,128]{2,1,0:T(8,128)(2,1)S(1)} collective-permute-done((bf16[5,128,128]{2,1,0:T(8,128)(2,1)}, bf16[5,128,128]{2,1,0:T(8,128)(2,1)S(1)}, u32[]{:S(2)}, u32[]{:S(2)}) %collective-permute-start.2) | collective-permute-done | bytes 163872 | tf_op jit(solution)/shard_map/ppermute | solution.py:278
  14.6 2.4 collective-permute-done.1
  17.0 1.9 pad_maximum_fusion
  19.0 1.6 collective-permute-start
  22.6 25.0 %all-gather = s32[64,2,5]{2,1,0:T(2,128)S(1)} all-gather(s32[2,2,5]{2,1,0:T(2,128)S(1)} %pad_add_fusion), channel_id=2, replica_groups=mesh['section'=4,'dp'=32] {'dp'}, dimensions={0}, use_global_device_ids=true | all-gather | bytes 2640 | tf_op jit(solution)/shard_map/all_gather | solution.py:293
  48.6 54.5 %all-gather.4.cloned.1.call-done = bf16[128,5,128,128]{3,2,1,0:T(8,128)(2,1)} async-done(((bf16[4,5,128,128]{3,2,1,0:T(8,128)(2,1)}), bf16[128,5,128,128]{3,2,1,0:T(8,128)(2,1)}) %all-gather.4.cloned.1.call-update) | async-done | bytes 20971536 | tf_op jit(solution)/shard_map/all_gather | solution.py:291
  103.0 12.2 %forward_layers.1 = bf16[64,8192]{1,0:T(8,128)(2,1)} custom-call(s32[2]{0:T(128)} %pad_add_fusion.2.swap_ref, s32[1024]{0:T(1024)} %compare_select_fusion.where_ref, bf16[64,8192]{1,0:T(8,128)(2,1)} %constant_dynamic-slice_fusion.1.first_ref.tokens_ref, bf16[32,2,2,5,128,128]{5,4,3,2,1,0:T(8,128)(2,1)} %bitcast.102), custom_call_target="tpu_custom_call" | custom-call | flops 2147483648 | bytes 20971520 | tf_op jit(solution)/shard_map/forward_layers/pallas_call | solution.py:435
  115.2 4.7 %collective-permute-start.3 = (bf16[64,8192]{1,0:T(8,128)(2,1)}, bf16[64,8192]{1,0:T(8,128)(2,1)S(1)}, u32[]{:S(2)}, u32[]{:S(2)}) collective-permute-start(bf16[64,8192]{1,0:T(8,128)(2,1)} %forward_layers.1), channel_id=1, source_target_pairs={{0,96},{32,64},{1,97},{33,65},{2,98},{34,66},{3,99},{35,67},{4,100... | collective-permute-start | bytes 3145736 | tf_op jit(solution)/shard_map/ppermute | solution.py:435
  121.0 21.9 %collective-permute-done.3.arrived_ref = bf16[64,8192]{1,0:T(8,128)(2,1)S(1)} collective-permute-done((bf16[64,8192]{1,0:T(8,128)(2,1)}, bf16[64,8192]{1,0:T(8,128)(2,1)S(1)}, u32[]{:S(2)}, u32[]{:S(2)}) %collective-permute-start.3) | collective-permute-done | bytes 1048608 | tf_op jit(solution)/shard_map/ppermute | solution.py:435
  144.0 22.2 %turn_layers.1 = (bf16[64,8192]{1,0:T(8,128)(2,1)}, f32[2,64,512]{2,1,0:T(8,128)}, f32[2,64,128]{2,1,0:T(8,128)}, bf16[64,8192]{1,0:T(8,128)(2,1)}, bf16[64,8192...) custom-call(s32[2]{0:T(128)} %pad_add_fusion.2.swap_ref, ...), custom_call_target="tpu_custom_call" | custom-call | flops 3758096384 | bytes 20971520 | tf_op jit(solution)/shard_map/turn_layers/pallas_call | solution.py:436
  167.7 3.0 collective-permute-done.5.act_other_ref
  170.9 28.5 %collective-permute-done.4.arrived_ref = bf16[64,8192]{1,0:T(8,128)(2,1)S(1)} collective-permute-done((bf16[64,8192]{1,0:T(8,128)(2,1)}, bf16[64,8192]{1,0:T(8,128)(2,1)S(1)}, u32[]{:S(2)}, u32[]{:S(2)}) %collective-permute-start.4) | collective-permute-done | bytes 1048608 | tf_op jit(solution)/shard_map/ppermute | solution.py:437
  200.5 13.8 %backward_high.1 = (bf16[64,512]{1,0:T(8,128)(2,1)}, bf16[64,8192]{1,0:T(8,128)(2,1)}, bf16[64,8192]{1,0:T(8,128)(2,1)}, bf16[64,8192]{1,0:T(8,128)(2,1)}) custom-call(s32[2]{0:T(128)} %pad_add_fusion.2.swap_ref, s32[1024]{0:T(1024)} %compare_select_fusion.where_ref, bf16[64,8192]{1,0:T(8,128)(2,1)} %get-tuple-element.32.hidden_ref, ...), custom_call_target="tpu_custom_call" | custom-call | flops 1073741824 | bytes 10485760 | tf_op jit(solution)/shard_map/backward_high/pallas_call | solution.py:441
  216.1 7.8 %backward_low.1 = (bf16[64,512]{1,0:T(8,128)(2,1)}, bf16[64,512]{1,0:T(8,128)(2,1)}) custom-call(s32[2]{0:T(128)} %pad_add_fusion.2.swap_ref, s32[1024]{0:T(1024)} %compare_select_fusion.where_ref, bf16[64,8192]{1,0:T(8,128)(2,1)} %get-tuple-element.36.middle_ref, bf16[64,512]{1,0:T(8,128)(2,1)} %get-tuple-element.37.high_ref, ...), custom_call_target="tpu_custom_call" | custom-call | flops 536870912 | bytes 20971520 | tf_op jit(solution)/shard_map/backward_low/pallas_call | solution.py:443
  225.7 14.2 %collective-permute-done.8.dpre_other_ref = bf16[64,512]{1,0:T(8,128)(2,1)S(1)} collective-permute-done((bf16[64,512]{1,0:T(8,128)(2,1)}, bf16[64,512]{1,0:T(8,128)(2,1)S(1)}, u32[]{:S(2)}, u32[]{:S(2)}) %collective-permute-start.8) | collective-permute-done | bytes 65568 | tf_op jit(solution)/shard_map/ppermute | solution.py:278
  240.5 7.5 %gradient_in.1 = (bf16[4,4,5,128,128]{4,3,2,1,0:T(8,128)(2,1)}, bf16[4,4,5,128,128]{4,3,2,1,0:T(8,128)(2,1)}) custom-call(s32[3]{0:T(128)} %get-tuple-element.74.spots_ref, s32[160]{0:T(256)} %reshape_squeeze.6.places_ref, bf16[64,8192]{1,0:T(8,128)(2,1)} %get-tuple-element.26.own_ref, bf16[64,8192]{1,0:T(8,128)(2,1)} %copy-done.9, ...), custom_call_target="tpu_custom_call" | custom-call | flops 1073741824 | bytes 62914560 | tf_op jit(solution)/shard_map/gradient_in/pallas_call | solution.py:446
  248.7 7.7 %gradient_out.1 = (bf16[4,4,5,128,128]{4,3,2,1,0:T(8,128)(2,1)}, bf16[4,4,5,128,128]{4,3,2,1,0:T(8,128)(2,1)}) custom-call(s32[3]{0:T(128)} %get-tuple-element.75.spots_ref, s32[160]{0:T(256)} %reshape_squeeze.7.places_ref, bf16[64,512]{1,0:T(8,128)(2,1)} %get-tuple-element.44.act_own_ref, bf16[64,512]{1,0:T(8,128)(2,1)} %copy-done.11, ...), custom_call_target="tpu_custom_call" | custom-call | flops 1073741824 | bytes 62914560 | tf_op jit(solution)/shard_map/gradient_out/pallas_call | solution.py:447
  258.2 1.9 collective-permute-start.13
  260.3 1.6 collective-permute-done.17
  263.3 1.6 collective-permute-start.21
  265.0 1.9 collective-permute-start.18
  266.8 9.3 %collective-permute-done.13 = bf16[4,5,128,128]{3,2,1,0:T(8,128)(2,1)S(1)} collective-permute-done((bf16[4,5,128,128]{3,2,1,0:T(8,128)(2,1)S(1)}, bf16[4,5,128,128]{3,2,1,0:T(8,128)(2,1)S(1)}, u32[]{:S(2)}, u32[]{:S(2)}) %collective-permute-start.13) | collective-permute-done | bytes 655392 | tf_op jit(solution)/shard_map/ppermute | solution.py:270
  276.6 1.9 collective-permute-start.11
  278.5 1.9 collective-permute-done.21
  280.6 2.4 collective-permute-start.22
  283.2 1.8 collective-permute-start.19
  286.5 1.9 collective-permute-start.16
  289.0 2.6 collective-permute-done.22
  291.7 1.6 collective-permute-start.23
  294.0 6.4 %collective-permute-start.24 = (bf16[5,128,128]{2,1,0:T(8,128)(2,1)S(1)}, bf16[5,128,128]{2,1,0:T(8,128)(2,1)S(1)}, u32[]{:S(2)}, u32[]{:S(2)}) collective-permute-start(bf16[5,128,128]{2,1,0:T(8,128)(2,1)S(1)} %get-tuple-element.67), channel_id=1, source_target_pairs={{0,4},{1,5},{2,6},{3,7},{4,0},{5,1},{6,2},{7,3},{8,12},{9,13},{10,... | collective-permute-start | bytes 491528 | tf_op jit(solution)/shard_map/ppermute | solution.py:270
  303.7 3.4 %collective-permute-done.20 = bf16[5,128,128]{2,1,0:T(8,128)(2,1)S(1)} collective-permute-done((bf16[5,128,128]{2,1,0:T(8,128)(2,1)S(1)}, bf16[5,128,128]{2,1,0:T(8,128)(2,1)S(1)}, u32[]{:S(2)}, u32[]{:S(2)}) %collective-permute-start.20) | collective-permute-done | bytes 163872 | tf_op jit(solution)/shard_map/ppermute | solution.py:270
  (83 shorter events, 24.7 us)
Async XLA Ops:
  7.2 14.0 %copy-start = (bf16[128,8192]{1,0:T(8,128)(2,1)S(1)}, bf16[128,8192]{1,0:T(8,128)(2,1)}, u32[]{:S(2)}) copy-start(bf16[128,8192]{1,0:T(8,128)(2,1)} %param.6) | copy-start | bytes 6291460
  7.2 11.8 %copy-start.7 = (s32[1,5]{1,0:T(1,128)S(1)}, s32[1,5]{1,0:T(1,128)}, u32[]{:S(2)}) copy-start(s32[1,5]{1,0:T(1,128)} %param.10) | copy-start | bytes 64
  7.2 95.8 %all-gather.4.cloned.1.call-start = ((), (), s32[]{:S(2)}) async-start(), calls=%async_computation | async-start | bytes 21626880 | tf_op jit(solution)/shard_map/all_gather | solution.py:291
  7.2 7.4 %collective-permute-start.2 = (bf16[5,128,128]{2,1,0:T(8,128)(2,1)}, bf16[5,128,128]{2,1,0:T(8,128)(2,1)S(1)}, u32[]{:S(2)}, u32[]{:S(2)}) collective-permute-start(bf16[5,128,128]{2,1,0:T(8,128)(2,1)} %bitcast.108), channel_id=1, source_target_pairs={{0,32},{32,0},{64,96},{96,64},{1,33},{33,1},{65,97},{97,65},{2,34}... | collective-permute-start | bytes 491528 | tf_op jit(solution)/shard_map/ppermute | solution.py:278
  8.8 8.2 %collective-permute-start.1 = (bf16[5,128,128]{2,1,0:T(8,128)(2,1)}, bf16[5,128,128]{2,1,0:T(8,128)(2,1)S(1)}, u32[]{:S(2)}, u32[]{:S(2)}) collective-permute-start(bf16[5,128,128]{2,1,0:T(8,128)(2,1)} %bitcast.109), channel_id=1, source_target_pairs={{0,32},{32,0},{64,96},{96,64},{1,33},{33,1},{65,97},{97,65},{2,34}... | collective-permute-start | bytes 491528 | tf_op jit(solution)/shard_map/ppermute | solution.py:278
  19.0 3.6 %collective-permute-start = (s32[2,5]{1,0:T(2,128)S(1)}, s32[2,5]{1,0:T(2,128)S(1)}, u32[]{:S(2)}, u32[]{:S(2)}) collective-permute-start(s32[2,5]{1,0:T(2,128)S(1)} %get-tuple-element.73), channel_id=1, source_target_pairs={{0,32},{32,0},{64,96},{96,64},{1,33},{33,1},{65,97},{97,65},{2,34}... | collective-permute-start | bytes 128 | tf_op jit(solution)/shard_map/ppermute | solution.py:278
  103.0 16.9 %copy-start.6 = (bf16[128,8192]{1,0:T(8,128)(2,1)S(1)}, bf16[128,8192]{1,0:T(8,128)(2,1)}, u32[]{:S(2)}) copy-start(bf16[128,8192]{1,0:T(8,128)(2,1)} %param.11) | copy-start | bytes 6291460
  115.2 27.7 %collective-permute-start.3 = (bf16[64,8192]{1,0:T(8,128)(2,1)}, bf16[64,8192]{1,0:T(8,128)(2,1)S(1)}, u32[]{:S(2)}, u32[]{:S(2)}) collective-permute-start(bf16[64,8192]{1,0:T(8,128)(2,1)} %forward_layers.1), channel_id=1, source_target_pairs={{0,96},{32,64},{1,97},{33,65},{2,98},{34,66},{3,99},{35,67},{4,100... | collective-permute-start | bytes 3145736 | tf_op jit(solution)/shard_map/ppermute | solution.py:435
  166.1 4.6 %collective-permute-start.5 = (bf16[64,512]{1,0:T(8,128)(2,1)}, bf16[64,512]{1,0:T(8,128)(2,1)S(1)}, u32[]{:S(2)}, u32[]{:S(2)}) collective-permute-start(bf16[64,512]{1,0:T(8,128)(2,1)} %get-tuple-element.29), channel_id=1, source_target_pairs={{0,32},{32,0},{64,96},{96,64},{1,33},{33,1},{65,97},{97,65},{2,34}... | collective-permute-start | bytes 196616 | tf_op jit(solution)/shard_map/ppermute | solution.py:278
  166.5 33.0 %collective-permute-start.4 = (bf16[64,8192]{1,0:T(8,128)(2,1)}, bf16[64,8192]{1,0:T(8,128)(2,1)S(1)}, u32[]{:S(2)}, u32[]{:S(2)}) collective-permute-start(bf16[64,8192]{1,0:T(8,128)(2,1)} %get-tuple-element.27), channel_id=1, source_target_pairs={{96,0},{64,32},{97,1},{65,33},{98,2},{66,34},{99,3},{67,35},{100,4... | collective-permute-start | bytes 3145736 | tf_op jit(solution)/shard_map/ppermute | solution.py:437
  170.7 43.6 %copy-start.11 = (bf16[64,512]{1,0:T(8,128)(2,1)}, bf16[64,512]{1,0:T(8,128)(2,1)S(1)}, u32[]{:S(2)}) copy-start(bf16[64,512]{1,0:T(8,128)(2,1)S(1)} %collective-permute-done.5.act_other_ref) | copy-start | bytes 196612
  170.7 28.7 %collective-permute-start.6 = (bf16[64,8192]{1,0:T(8,128)(2,1)}, bf16[64,8192]{1,0:T(8,128)(2,1)S(1)}, u32[]{:S(2)}, u32[]{:S(2)}) collective-permute-start(bf16[64,8192]{1,0:T(8,128)(2,1)} %get-tuple-element.30), channel_id=1, source_target_pairs={{0,32},{32,0},{64,96},{96,64},{1,33},{33,1},{65,97},{97,65},{2,34}... | collective-permute-start | bytes 3145736 | tf_op jit(solution)/shard_map/ppermute | solution.py:278
  199.4 14.9 %copy-start.9 = (bf16[64,8192]{1,0:T(8,128)(2,1)}, bf16[64,8192]{1,0:T(8,128)(2,1)S(1)}, u32[]{:S(2)}) copy-start(bf16[64,8192]{1,0:T(8,128)(2,1)S(1)} %collective-permute-done.6.other_ref) | copy-start | bytes 3145732
  214.3 25.6 %collective-permute-start.7 = (bf16[64,8192]{1,0:T(8,128)(2,1)}, bf16[64,8192]{1,0:T(8,128)(2,1)S(1)}, u32[]{:S(2)}, u32[]{:S(2)}) collective-permute-start(bf16[64,8192]{1,0:T(8,128)(2,1)} %get-tuple-element.39), channel_id=1, source_target_pairs={{0,32},{32,0},{64,96},{96,64},{1,33},{33,1},{65,97},{97,65},{2,34}... | collective-permute-start | bytes 3145736 | tf_op jit(solution)/shard_map/ppermute | solution.py:278
  224.0 15.9 %collective-permute-start.8 = (bf16[64,512]{1,0:T(8,128)(2,1)}, bf16[64,512]{1,0:T(8,128)(2,1)S(1)}, u32[]{:S(2)}, u32[]{:S(2)}) collective-permute-start(bf16[64,512]{1,0:T(8,128)(2,1)} %get-tuple-element.40), channel_id=1, source_target_pairs={{0,32},{32,0},{64,96},{96,64},{1,33},{33,1},{65,97},{97,65},{2,34}... | collective-permute-start | bytes 196616 | tf_op jit(solution)/shard_map/ppermute | solution.py:278
  248.0 9.1 %collective-permute-start.9 = (bf16[4,4,5,128,128]{4,3,2,1,0:T(8,128)(2,1)}, bf16[4,4,5,128,128]{4,3,2,1,0:T(8,128)(2,1)S(1)}, u32[]{:S(2)}, u32[]{:S(2)}) collective-permute-start(bf16[4,4,5,128,128]{4,3,2,1,0:T(8,128)(2,1)} %get-tuple-element.43), channel_id=1, source_target_pairs={{0,1},{1,0},{2,3},{3,2},{4,5},{5,4},{6,7},{7,6},{8,9},{9,8},{10,11... | collective-permute-start | bytes 7864328 | tf_op jit(solution)/shard_map/ppermute | solution.py:423
  256.4 5.5 %collective-permute-start.17 = (bf16[4,4,5,128,128]{4,3,2,1,0:T(8,128)(2,1)}, bf16[4,4,5,128,128]{4,3,2,1,0:T(8,128)(2,1)S(1)}, u32[]{:S(2)}, u32[]{:S(2)}) collective-permute-start(bf16[4,4,5,128,128]{4,3,2,1,0:T(8,128)(2,1)} %get-tuple-element.49), channel_id=1, source_target_pairs={{0,1},{1,0},{2,3},{3,2},{4,5},{5,4},{6,7},{7,6},{8,9},{9,8},{10,11... | collective-permute-start | bytes 7864328 | tf_op jit(solution)/shard_map/ppermute | solution.py:423
  258.2 18.0 %collective-permute-start.13 = (bf16[4,5,128,128]{3,2,1,0:T(8,128)(2,1)S(1)}, bf16[4,5,128,128]{3,2,1,0:T(8,128)(2,1)S(1)}, u32[]{:S(2)}, u32[]{:S(2)}) collective-permute-start(bf16[4,5,128,128]{3,2,1,0:T(8,128)(2,1)S(1)} %get-tuple-element.55), channel_id=1, source_target_pairs={{0,6},{1,7},{2,4},{3,5},{4,2},{5,3},{6,0},{7,1},{8,14},{9,15},{10,... | collective-permute-start | bytes 1966088 | tf_op jit(solution)/shard_map/ppermute | solution.py:270
  260.0 16.4 %collective-permute-start.10 = (bf16[4,5,128,128]{3,2,1,0:T(8,128)(2,1)S(1)}, bf16[4,5,128,128]{3,2,1,0:T(8,128)(2,1)S(1)}, u32[]{:S(2)}, u32[]{:S(2)}) collective-permute-start(bf16[4,5,128,128]{3,2,1,0:T(8,128)(2,1)S(1)} %get-tuple-element.57), channel_id=1, source_target_pairs={{0,2},{1,3},{2,0},{3,1},{4,6},{5,7},{6,4},{7,5},{8,10},{9,11},{10,... | collective-permute-start | bytes 1966088 | tf_op jit(solution)/shard_map/ppermute | solution.py:270
  263.3 17.1 %collective-permute-start.21 = (bf16[4,5,128,128]{3,2,1,0:T(8,128)(2,1)S(1)}, bf16[4,5,128,128]{3,2,1,0:T(8,128)(2,1)S(1)}, u32[]{:S(2)}, u32[]{:S(2)}) collective-permute-start(bf16[4,5,128,128]{3,2,1,0:T(8,128)(2,1)S(1)} %get-tuple-element.51), channel_id=1, source_target_pairs={{0,24},{1,25},{2,26},{3,27},{4,28},{5,29},{6,30},{7,31},{8,16},{9,... | collective-permute-start | bytes 1966088 | tf_op jit(solution)/shard_map/ppermute | solution.py:270
  265.0 18.1 %collective-permute-start.18 = (bf16[4,5,128,128]{3,2,1,0:T(8,128)(2,1)S(1)}, bf16[4,5,128,128]{3,2,1,0:T(8,128)(2,1)S(1)}, u32[]{:S(2)}, u32[]{:S(2)}) collective-permute-start(bf16[4,5,128,128]{3,2,1,0:T(8,128)(2,1)S(1)} %get-tuple-element.53), channel_id=1, source_target_pairs={{0,8},{1,9},{2,10},{3,11},{4,12},{5,13},{6,14},{7,15},{8,0},{9,1},... | collective-permute-start | bytes 1966088 | tf_op jit(solution)/shard_map/ppermute | solution.py:270
  276.3 8.9 %collective-permute-start.14 = (bf16[2,5,128,128]{3,2,1,0:T(8,128)(2,1)S(1)}, bf16[2,5,128,128]{3,2,1,0:T(8,128)(2,1)S(1)}, u32[]{:S(2)}, u32[]{:S(2)}) collective-permute-start(bf16[2,5,128,128]{3,2,1,0:T(8,128)(2,1)S(1)} %get-tuple-element.65), channel_id=1, source_target_pairs={{0,2},{1,3},{2,0},{3,1},{4,6},{5,7},{6,4},{7,5},{8,10},{9,11},{10,... | collective-permute-start | bytes 983048 | tf_op jit(solution)/shard_map/ppermute | solution.py:270
  276.6 11.8 %collective-permute-start.11 = (bf16[2,5,128,128]{3,2,1,0:T(8,128)(2,1)S(1)}, bf16[2,5,128,128]{3,2,1,0:T(8,128)(2,1)S(1)}, u32[]{:S(2)}, u32[]{:S(2)}) collective-permute-start(bf16[2,5,128,128]{3,2,1,0:T(8,128)(2,1)S(1)} %get-tuple-element.63), channel_id=1, source_target_pairs={{0,6},{1,7},{2,4},{3,5},{4,2},{5,3},{6,0},{7,1},{8,14},{9,15},{10,... | collective-permute-start | bytes 983048 | tf_op jit(solution)/shard_map/ppermute | solution.py:270
  280.6 11.0 %collective-permute-start.22 = (bf16[2,5,128,128]{3,2,1,0:T(8,128)(2,1)S(1)}, bf16[2,5,128,128]{3,2,1,0:T(8,128)(2,1)S(1)}, u32[]{:S(2)}, u32[]{:S(2)}) collective-permute-start(bf16[2,5,128,128]{3,2,1,0:T(8,128)(2,1)S(1)} %get-tuple-element.61), channel_id=1, source_target_pairs={{0,8},{1,9},{2,10},{3,11},{4,12},{5,13},{6,14},{7,15},{8,0},{9,1},... | collective-permute-start | bytes 983048 | tf_op jit(solution)/shard_map/ppermute | solution.py:270
  283.2 10.8 %collective-permute-start.19 = (bf16[2,5,128,128]{3,2,1,0:T(8,128)(2,1)S(1)}, bf16[2,5,128,128]{3,2,1,0:T(8,128)(2,1)S(1)}, u32[]{:S(2)}, u32[]{:S(2)}) collective-permute-start(bf16[2,5,128,128]{3,2,1,0:T(8,128)(2,1)S(1)} %get-tuple-element.59), channel_id=1, source_target_pairs={{0,24},{1,25},{2,26},{3,27},{4,28},{5,29},{6,30},{7,31},{8,16},{9,... | collective-permute-start | bytes 983048 | tf_op jit(solution)/shard_map/ppermute | solution.py:270
  285.3 15.2 %collective-permute-start.15 = (bf16[5,128,128]{2,1,0:T(8,128)(2,1)S(1)}, bf16[5,128,128]{2,1,0:T(8,128)(2,1)S(1)}, u32[]{:S(2)}, u32[]{:S(2)}) collective-permute-start(bf16[5,128,128]{2,1,0:T(8,128)(2,1)S(1)} %get-tuple-element.68), channel_id=1, source_target_pairs={{0,8},{1,9},{2,10},{3,11},{4,12},{5,13},{6,14},{7,15},{8,0},{9,1},... | collective-permute-start | bytes 491528 | tf_op jit(solution)/shard_map/ppermute | solution.py:270
  286.5 15.3 %collective-permute-start.16 = (bf16[5,128,128]{2,1,0:T(8,128)(2,1)S(1)}, bf16[5,128,128]{2,1,0:T(8,128)(2,1)S(1)}, u32[]{:S(2)}, u32[]{:S(2)}) collective-permute-start(bf16[5,128,128]{2,1,0:T(8,128)(2,1)S(1)} %get-tuple-element.69), channel_id=1, source_target_pairs={{0,16},{1,17},{2,18},{3,19},{4,20},{5,21},{6,22},{7,23},{8,24},{9,... | collective-permute-start | bytes 491528 | tf_op jit(solution)/shard_map/ppermute | solution.py:270
  288.5 13.4 %collective-permute-start.12 = (bf16[5,128,128]{2,1,0:T(8,128)(2,1)S(1)}, bf16[5,128,128]{2,1,0:T(8,128)(2,1)S(1)}, u32[]{:S(2)}, u32[]{:S(2)}) collective-permute-start(bf16[5,128,128]{2,1,0:T(8,128)(2,1)S(1)} %fusion.19), channel_id=1, source_target_pairs={{0,24},{1,25},{2,26},{3,27},{4,28},{5,29},{6,30},{7,31},{8,16},{9,... | collective-permute-start | bytes 491528 | tf_op jit(solution)/shard_map/ppermute | solution.py:270
  291.6 16.3 %copy-start.1 = (bf16[128,8192]{1,0:T(8,128)(2,1)S(1)}, bf16[128,8192]{1,0:T(8,128)(2,1)}, u32[]{:S(2)}) copy-start(bf16[128,8192]{1,0:T(8,128)(2,1)} %param.6) | copy-start | bytes 6291460
  291.7 10.9 %collective-permute-start.23 = (bf16[5,128,128]{2,1,0:T(8,128)(2,1)S(1)}, bf16[5,128,128]{2,1,0:T(8,128)(2,1)S(1)}, u32[]{:S(2)}, u32[]{:S(2)}) collective-permute-start(bf16[5,128,128]{2,1,0:T(8,128)(2,1)S(1)} %get-tuple-element.66), channel_id=1, source_target_pairs={{0,2},{1,3},{2,0},{3,1},{4,6},{5,7},{6,4},{7,5},{8,10},{9,11},{10,... | collective-permute-start | bytes 491528 | tf_op jit(solution)/shard_map/ppermute | solution.py:270
  294.0 9.7 %collective-permute-start.24 = (bf16[5,128,128]{2,1,0:T(8,128)(2,1)S(1)}, bf16[5,128,128]{2,1,0:T(8,128)(2,1)S(1)}, u32[]{:S(2)}, u32[]{:S(2)}) collective-permute-start(bf16[5,128,128]{2,1,0:T(8,128)(2,1)S(1)} %get-tuple-element.67), channel_id=1, source_target_pairs={{0,4},{1,5},{2,6},{3,7},{4,0},{5,1},{6,2},{7,3},{8,12},{9,13},{10,... | collective-permute-start | bytes 491528 | tf_op jit(solution)/shard_map/ppermute | solution.py:270
  300.5 6.6 %collective-permute-start.20 = (bf16[5,128,128]{2,1,0:T(8,128)(2,1)S(1)}, bf16[5,128,128]{2,1,0:T(8,128)(2,1)S(1)}, u32[]{:S(2)}, u32[]{:S(2)}) collective-permute-start(bf16[5,128,128]{2,1,0:T(8,128)(2,1)S(1)} %fusion.23), channel_id=1, source_target_pairs={{0,6},{1,7},{2,4},{3,5},{4,2},{5,3},{6,0},{7,1},{8,14},{9,15},{10,... | collective-permute-start | bytes 491528 | tf_op jit(solution)/shard_map/ppermute | solution.py:270
  (7 other events, 35.7 us)
Sparse Core Ops, SparseCore 0:
  19.1 83.9 all-gather.3

commit v8 on v7

--- a/solution.py
+++ b/solution.py
@@ -50,7 +50,9 @@
             held[i, owners, 0] = jnp.zeros(held.shape[3:], held.dtype)
 
     def wait(self, layer, matrix):
-        self.copies[layer, matrix].wait()
+        copy = self.copies.pop((layer, matrix), None)
+        if copy is not None:
+            copy.wait()
 
     def block(self, layer, matrix, number):
         code = self.where_ref[((layer ^ self.swap) * 2 + matrix) * NBLK + number]
@@ -104,6 +106,7 @@
 
 
 def backward(weights, layer, hidden_ref, upstream_ref, pre, inverse, earlier_ref):
+    weights.wait(layer, 1)
     dact = 0.0
     for chunk, cols in chunks():
         dact = dact + dot(upstream_ref[:, cols], weights.columns_out(layer, chunk), NT)
@@ -112,6 +115,7 @@
     if earlier_ref is not None:
         mean = jnp.sum(dpre.astype(jnp.float32) * pre, axis=-1, keepdims=True) / D
         pull = mean * inverse * inverse
+        weights.wait(layer, 0)
         for chunk, cols in chunks():
             dnorm = dot(dpre, weights.rows_in(layer, chunk), NT)
             hidden = hidden_ref[:, cols].astype(jnp.float32)
@@ -133,23 +137,31 @@
     forward_up(weights, 1, second_ref, silu(pre), last_ref)
 
 
-def choose(arrived, arrived_ref, here_ref, out_ref, sem):
-    @pl.when(arrived)
-    def _():
-        copy = pltpu.make_async_copy(arrived_ref, out_ref, sem)
-        copy.start()
-        copy.wait()
-
-    @pl.when(jnp.logical_not(arrived))
-    def _():
-        out_ref[...] = here_ref[...]
+class Choice:
+    def __init__(self, arrived, arrived_ref, here_ref, out_ref, sem):
+        self.arrived = arrived
+        self.copy = pltpu.make_async_copy(arrived_ref, out_ref, sem)
+
+        @pl.when(arrived)
+        def _():
+            self.copy.start()
+
+        @pl.when(jnp.logical_not(arrived))
+        def _():
+            out_ref[...] = here_ref[...]
+
+    def wait(self):
+        @pl.when(self.arrived)
+        def _():
+            self.copy.wait()
 
 
 def turn_kernel(
     swap_ref, where_ref, tokens_ref, arrived_ref, grad_ref, source, second_ref, pre_ref, inverse_ref, normed_own_ref, normed_other_ref, act_own_ref, act_other_ref, earlier_ref, first_ref, middle_ref, normed_ref, act_ref, held, sems
 ):
+    choice = Choice(swap_ref[1] > 0, arrived_ref, tokens_ref, first_ref, sems.at[4])
     weights = Weights(swap_ref, where_ref, source, held, sems, [(0, 0), (0, 1), (1, 0), (1, 1)])
-    choose(swap_ref[1] > 0, arrived_ref, tokens_ref, first_ref, sems.at[4])
+    choice.wait()
     for layer, hidden_ref in enumerate((first_ref, second_ref)):
         place = layer ^ swap_ref[0]
         pre, inverse = forward_down(weights, layer, hidden_ref, normed_ref.at[place])
@@ -163,7 +175,6 @@
     for _, cols in chunks():
         normed_own_ref[:, cols] = normed_ref[0, :, cols]
         normed_other_ref[:, cols] = normed_ref[1, :, cols]
-    weights.wait(1, 1)
     backward(weights, 1, second_ref, grad_ref, pre_ref[1], inverse_ref[1][:, :1], middle_ref)
     backward(weights, 0, first_ref, middle_ref, pre_ref[0], inverse_ref[0][:, :1], earlier_ref)
 
@@ -171,11 +182,10 @@
 def high_kernel(
     swap_ref, where_ref, hidden_ref, grad_ref, arrived_ref, pre_ref, inverse_ref, source, dpre_ref, middle_ref, own_ref, sent_ref, upstream_ref, held, sems
 ):
+    choice = Choice(swap_ref[1] == 0, arrived_ref, grad_ref, upstream_ref, sems.at[2])
     weights = Weights(swap_ref, where_ref, source, held, sems, [(1, 1), (1, 0)])
     even = swap_ref[0] == 0
-    choose(swap_ref[1] == 0, arrived_ref, grad_ref, upstream_ref, sems.at[2])
-    weights.wait(1, 1)
-    weights.wait(1, 0)
+    choice.wait()
     dpre_ref[...] = backward(weights, 1, hidden_ref, upstream_ref, pre_ref[1], inverse_ref[1][:, :1], middle_ref)
     for _, cols in chunks():
         upper, lower = upstream_ref[:, cols], middle_ref[:, cols]
@@ -186,7 +196,6 @@
 def low_kernel(swap_ref, where_ref, middle_ref, high_ref, pre_ref, source, own_ref, sent_ref, held, sems):
     weights = Weights(swap_ref, where_ref, source, held, sems, [(0, 1)])
     even = swap_ref[0] == 0
-    weights.wait(0, 1)
     low = backward(weights, 0, None, middle_ref, pre_ref[0], None, None)
     high = high_ref[...]
     own_ref[...] = lax.select(even, low, high)

time: 321 us -> 314 us (0.978)
  waiting for transfers between devices: 151 us -> 146 us
    ppermute x1, waiting for transfers between devices: 28.5 us -> 23.3 us  [per_device(): arrived = lax.ppermute(leaving, 'section', DOWN)]
  transfers between devices with their start and end apart: 26 -> 26, of which waited for: 16 -> 17; matrix products, arithmetic and copies ran while one was open for 3% -> 3% of each run, Pallas kernels for 5% -> 5%
where the time goes in v8:
time: 314 us; the launch traced here: 308 us
  waiting for transfers between devices  146 us (46%)
  Pallas kernels  70 us (22%)
  starting transfers between devices  37.9 us (12%)
  blocking collectives  25 us (8%)
  between operations  14.7 us (5%)
  other arithmetic  9.02 us (3%)
  local copies, waits for them, and re-layouts  6.24 us (2%)
    all_gather x1, waiting for transfers between devices, per_device(): lax.all_gather(both, 'dp', axis=0)  54.5 us
    all_gather x1, blocking collectives, per_device(): lax.all_gather(jnp.stack([own_places, swapped(own_places)]), 'dp', axis=0)  25 us
    ppermute x7, waiting for transfers between devices, swapped(): return lax.ppermute(array, 'section', PAIR)  24.9 us
    ppermute x14, starting transfers between devices, across(): lax.ppermute(array, 'dp', [(i, i + ((i // stride % RING ^ flip) - i // st...  24.7 us
    ppermute x1, waiting for transfers between devices, per_device(): arrived = lax.ppermute(leaving, 'section', DOWN)  23.3 us
    pallas_call x1, Pallas kernels, per_device(): turn(swap, where, first_tokens, arrived, last_grads, weights)  22.4 us
    ppermute x1, waiting for transfers between devices, per_device(): lax.ppermute(forward(swap, where, first_tokens, weights), 'section', UP)  21.9 us
    ppermute x14, waiting for transfers between devices, across(): lax.ppermute(array, 'dp', [(i, i + ((i // stride % RING ^ flip) - i // st...  19.3 us
  transfers between devices with their start and end apart: 26, of which 17 were waited for; matrix products, arithmetic and copies ran while one was open for 3% of the time, Pallas kernels for 5%

profile of v8, /device:TPU:32, one launch (start us, length us, event | category | flops | bytes accessed | tf_op | source)
XLA Modules:
  0.0 308.4 jit_solution(18120719589709731696)
XLA Ops:
  7.2 1.6 collective-permute-start.2
  9.4 5.3 %collective-permute-done.2 = bf16[5,128,128]{2,1,0:T(8,128)(2,1)S(1)} collective-permute-done((bf16[5,128,128]{2,1,0:T(8,128)(2,1)}, bf16[5,128,128]{2,1,0:T(8,128)(2,1)S(1)}, u32[]{:S(2)}, u32[]{:S(2)}) %collective-permute-start.2) | collective-permute-done | bytes 163872 | tf_op jit(solution)/shard_map/ppermute | solution.py:287
  14.6 2.4 collective-permute-done.1
  17.0 1.9 pad_maximum_fusion
  19.0 1.6 collective-permute-start
  22.6 25.0 %all-gather = s32[64,2,5]{2,1,0:T(2,128)S(1)} all-gather(s32[2,2,5]{2,1,0:T(2,128)S(1)} %pad_add_fusion), channel_id=2, replica_groups=mesh['section'=4,'dp'=32] {'dp'}, dimensions={0}, use_global_device_ids=true | all-gather | bytes 2640 | tf_op jit(solution)/shard_map/all_gather | solution.py:302
  48.6 54.5 %all-gather.4.cloned.1.call-done = bf16[128,5,128,128]{3,2,1,0:T(8,128)(2,1)} async-done(((bf16[4,5,128,128]{3,2,1,0:T(8,128)(2,1)}), bf16[128,5,128,128]{3,2,1,0:T(8,128)(2,1)}) %all-gather.4.cloned.1.call-update) | async-done | bytes 20971536 | tf_op jit(solution)/shard_map/all_gather | solution.py:300
  103.0 12.2 %forward_layers.1 = bf16[64,8192]{1,0:T(8,128)(2,1)} custom-call(s32[2]{0:T(128)} %pad_add_fusion.2.swap_ref, s32[1024]{0:T(1024)} %compare_select_fusion.where_ref, bf16[64,8192]{1,0:T(8,128)(2,1)} %constant_dynamic-slice_fusion.1.first_ref.tokens_ref, bf16[32,2,2,5,128,128]{5,4,3,2,1,0:T(8,128)(2,1)} %bitcast.102), custom_call_target="tpu_custom_call" | custom-call | flops 2147483648 | bytes 20971520 | tf_op jit(solution)/shard_map/forward_layers/pallas_call | solution.py:444
  115.2 4.7 %collective-permute-start.3 = (bf16[64,8192]{1,0:T(8,128)(2,1)}, bf16[64,8192]{1,0:T(8,128)(2,1)S(1)}, u32[]{:S(2)}, u32[]{:S(2)}) collective-permute-start(bf16[64,8192]{1,0:T(8,128)(2,1)} %forward_layers.1), channel_id=1, source_target_pairs={{0,96},{32,64},{1,97},{33,65},{2,98},{34,66},{3,99},{35,67},{4,100... | collective-permute-start | bytes 3145736 | tf_op jit(solution)/shard_map/ppermute | solution.py:444
  121.0 21.9 %collective-permute-done.3.arrived_ref = bf16[64,8192]{1,0:T(8,128)(2,1)S(1)} collective-permute-done((bf16[64,8192]{1,0:T(8,128)(2,1)}, bf16[64,8192]{1,0:T(8,128)(2,1)S(1)}, u32[]{:S(2)}, u32[]{:S(2)}) %collective-permute-start.3) | collective-permute-done | bytes 1048608 | tf_op jit(solution)/shard_map/ppermute | solution.py:444
  144.0 22.4 %turn_layers.1 = (bf16[64,8192]{1,0:T(8,128)(2,1)}, f32[2,64,512]{2,1,0:T(8,128)}, f32[2,64,128]{2,1,0:T(8,128)}, bf16[64,8192]{1,0:T(8,128)(2,1)}, bf16[64,8192...) custom-call(s32[2]{0:T(128)} %pad_add_fusion.2.swap_ref, ...), custom_call_target="tpu_custom_call" | custom-call | flops 3758096384 | bytes 20971520 | tf_op jit(solution)/shard_map/turn_layers/pallas_call | solution.py:445
  168.0 2.9 collective-permute-done.5.act_other_ref
  171.2 23.3 %collective-permute-done.4.arrived_ref = bf16[64,8192]{1,0:T(8,128)(2,1)S(1)} collective-permute-done((bf16[64,8192]{1,0:T(8,128)(2,1)}, bf16[64,8192]{1,0:T(8,128)(2,1)S(1)}, u32[]{:S(2)}, u32[]{:S(2)}) %collective-permute-start.4) | collective-permute-done | bytes 1048608 | tf_op jit(solution)/shard_map/ppermute | solution.py:446
  195.5 12.4 %backward_high.1 = (bf16[64,512]{1,0:T(8,128)(2,1)}, bf16[64,8192]{1,0:T(8,128)(2,1)}, bf16[64,8192]{1,0:T(8,128)(2,1)}, bf16[64,8192]{1,0:T(8,128)(2,1)}) custom-call(s32[2]{0:T(128)} %pad_add_fusion.2.swap_ref, s32[1024]{0:T(1024)} %compare_select_fusion.where_ref, bf16[64,8192]{1,0:T(8,128)(2,1)} %get-tuple-element.32.hidden_ref, ...), custom_call_target="tpu_custom_call" | custom-call | flops 1073741824 | bytes 10485760 | tf_op jit(solution)/shard_map/backward_high/pallas_call | solution.py:450
  209.7 7.8 %backward_low.1 = (bf16[64,512]{1,0:T(8,128)(2,1)}, bf16[64,512]{1,0:T(8,128)(2,1)}) custom-call(s32[2]{0:T(128)} %pad_add_fusion.2.swap_ref, s32[1024]{0:T(1024)} %compare_select_fusion.where_ref, bf16[64,8192]{1,0:T(8,128)(2,1)} %get-tuple-element.36.middle_ref, bf16[64,512]{1,0:T(8,128)(2,1)} %get-tuple-element.37.high_ref, ...), custom_call_target="tpu_custom_call" | custom-call | flops 536870912 | bytes 20971520 | tf_op jit(solution)/shard_map/backward_low/pallas_call | solution.py:452
  219.2 13.9 %collective-permute-done.8.dpre_other_ref = bf16[64,512]{1,0:T(8,128)(2,1)S(1)} collective-permute-done((bf16[64,512]{1,0:T(8,128)(2,1)}, bf16[64,512]{1,0:T(8,128)(2,1)S(1)}, u32[]{:S(2)}, u32[]{:S(2)}) %collective-permute-start.8) | collective-permute-done | bytes 65568 | tf_op jit(solution)/shard_map/ppermute | solution.py:287
  233.7 7.5 %gradient_in.1 = (bf16[4,4,5,128,128]{4,3,2,1,0:T(8,128)(2,1)}, bf16[4,4,5,128,128]{4,3,2,1,0:T(8,128)(2,1)}) custom-call(s32[3]{0:T(128)} %get-tuple-element.74.spots_ref, s32[160]{0:T(256)} %reshape_squeeze.6.places_ref, bf16[64,8192]{1,0:T(8,128)(2,1)} %get-tuple-element.26.own_ref, bf16[64,8192]{1,0:T(8,128)(2,1)} %copy-done.9, ...), custom_call_target="tpu_custom_call" | custom-call | flops 1073741824 | bytes 62914560 | tf_op jit(solution)/shard_map/gradient_in/pallas_call | solution.py:455
  241.9 7.7 %gradient_out.1 = (bf16[4,4,5,128,128]{4,3,2,1,0:T(8,128)(2,1)}, bf16[4,4,5,128,128]{4,3,2,1,0:T(8,128)(2,1)}) custom-call(s32[3]{0:T(128)} %get-tuple-element.75.spots_ref, s32[160]{0:T(256)} %reshape_squeeze.7.places_ref, bf16[64,512]{1,0:T(8,128)(2,1)} %get-tuple-element.44.act_own_ref, bf16[64,512]{1,0:T(8,128)(2,1)} %copy-done.11, ...), custom_call_target="tpu_custom_call" | custom-call | flops 1073741824 | bytes 62914560 | tf_op jit(solution)/shard_map/gradient_out/pallas_call | solution.py:456
  251.4 1.9 collective-permute-start.13
  253.5 1.6 collective-permute-done.17
  256.5 1.6 collective-permute-start.21
  258.2 1.9 collective-permute-start.18
  260.0 9.3 %collective-permute-done.13 = bf16[4,5,128,128]{3,2,1,0:T(8,128)(2,1)S(1)} collective-permute-done((bf16[4,5,128,128]{3,2,1,0:T(8,128)(2,1)S(1)}, bf16[4,5,128,128]{3,2,1,0:T(8,128)(2,1)S(1)}, u32[]{:S(2)}, u32[]{:S(2)}) %collective-permute-start.13) | collective-permute-done | bytes 655392 | tf_op jit(solution)/shard_map/ppermute | solution.py:279
  269.8 1.9 collective-permute-start.11
  271.7 1.9 collective-permute-done.21
  273.8 2.4 collective-permute-start.22
  276.4 1.8 collective-permute-start.19
  279.7 1.9 collective-permute-start.16
  282.2 2.6 collective-permute-done.22
  284.9 1.6 collective-permute-start.23
  287.2 6.4 %collective-permute-start.24 = (bf16[5,128,128]{2,1,0:T(8,128)(2,1)S(1)}, bf16[5,128,128]{2,1,0:T(8,128)(2,1)S(1)}, u32[]{:S(2)}, u32[]{:S(2)}) collective-permute-start(bf16[5,128,128]{2,1,0:T(8,128)(2,1)S(1)} %get-tuple-element.67), channel_id=1, source_target_pairs={{0,4},{1,5},{2,6},{3,7},{4,0},{5,1},{6,2},{7,3},{8,12},{9,13},{10,... | collective-permute-start | bytes 491528 | tf_op jit(solution)/shard_map/ppermute | solution.py:279
  296.9 3.4 %collective-permute-done.20 = bf16[5,128,128]{2,1,0:T(8,128)(2,1)S(1)} collective-permute-done((bf16[5,128,128]{2,1,0:T(8,128)(2,1)S(1)}, bf16[5,128,128]{2,1,0:T(8,128)(2,1)S(1)}, u32[]{:S(2)}, u32[]{:S(2)}) %collective-permute-start.20) | collective-permute-done | bytes 163872 | tf_op jit(solution)/shard_map/ppermute | solution.py:279
  (83 shorter events, 24.7 us)
Async XLA Ops:
  7.2 14.0 %copy-start = (bf16[128,8192]{1,0:T(8,128)(2,1)S(1)}, bf16[128,8192]{1,0:T(8,128)(2,1)}, u32[]{:S(2)}) copy-start(bf16[128,8192]{1,0:T(8,128)(2,1)} %param.6) | copy-start | bytes 6291460
  7.2 11.8 %copy-start.7 = (s32[1,5]{1,0:T(1,128)S(1)}, s32[1,5]{1,0:T(1,128)}, u32[]{:S(2)}) copy-start(s32[1,5]{1,0:T(1,128)} %param.10) | copy-start | bytes 64
  7.2 95.8 %all-gather.4.cloned.1.call-start = ((), (), s32[]{:S(2)}) async-start(), calls=%async_computation | async-start | bytes 21626880 | tf_op jit(solution)/shard_map/all_gather | solution.py:300
  7.2 7.4 %collective-permute-start.2 = (bf16[5,128,128]{2,1,0:T(8,128)(2,1)}, bf16[5,128,128]{2,1,0:T(8,128)(2,1)S(1)}, u32[]{:S(2)}, u32[]{:S(2)}) collective-permute-start(bf16[5,128,128]{2,1,0:T(8,128)(2,1)} %bitcast.108), channel_id=1, source_target_pairs={{0,32},{32,0},{64,96},{96,64},{1,33},{33,1},{65,97},{97,65},{2,34}... | collective-permute-start | bytes 491528 | tf_op jit(solution)/shard_map/ppermute | solution.py:287
  8.8 8.2 %collective-permute-start.1 = (bf16[5,128,128]{2,1,0:T(8,128)(2,1)}, bf16[5,128,128]{2,1,0:T(8,128)(2,1)S(1)}, u32[]{:S(2)}, u32[]{:S(2)}) collective-permute-start(bf16[5,128,128]{2,1,0:T(8,128)(2,1)} %bitcast.109), channel_id=1, source_target_pairs={{0,32},{32,0},{64,96},{96,64},{1,33},{33,1},{65,97},{97,65},{2,34}... | collective-permute-start | bytes 491528 | tf_op jit(solution)/shard_map/ppermute | solution.py:287
  19.0 3.6 %collective-permute-start = (s32[2,5]{1,0:T(2,128)S(1)}, s32[2,5]{1,0:T(2,128)S(1)}, u32[]{:S(2)}, u32[]{:S(2)}) collective-permute-start(s32[2,5]{1,0:T(2,128)S(1)} %get-tuple-element.73), channel_id=1, source_target_pairs={{0,32},{32,0},{64,96},{96,64},{1,33},{33,1},{65,97},{97,65},{2,34}... | collective-permute-start | bytes 128 | tf_op jit(solution)/shard_map/ppermute | solution.py:287
  103.0 16.9 %copy-start.6 = (bf16[128,8192]{1,0:T(8,128)(2,1)S(1)}, bf16[128,8192]{1,0:T(8,128)(2,1)}, u32[]{:S(2)}) copy-start(bf16[128,8192]{1,0:T(8,128)(2,1)} %param.11) | copy-start | bytes 6291460
  115.2 27.7 %collective-permute-start.3 = (bf16[64,8192]{1,0:T(8,128)(2,1)}, bf16[64,8192]{1,0:T(8,128)(2,1)S(1)}, u32[]{:S(2)}, u32[]{:S(2)}) collective-permute-start(bf16[64,8192]{1,0:T(8,128)(2,1)} %forward_layers.1), channel_id=1, source_target_pairs={{0,96},{32,64},{1,97},{33,65},{2,98},{34,66},{3,99},{35,67},{4,100... | collective-permute-start | bytes 3145736 | tf_op jit(solution)/shard_map/ppermute | solution.py:444
  166.4 4.6 %collective-permute-start.5 = (bf16[64,512]{1,0:T(8,128)(2,1)}, bf16[64,512]{1,0:T(8,128)(2,1)S(1)}, u32[]{:S(2)}, u32[]{:S(2)}) collective-permute-start(bf16[64,512]{1,0:T(8,128)(2,1)} %get-tuple-element.29), channel_id=1, source_target_pairs={{0,32},{32,0},{64,96},{96,64},{1,33},{33,1},{65,97},{97,65},{2,34}... | collective-permute-start | bytes 196616 | tf_op jit(solution)/shard_map/ppermute | solution.py:287
  166.7 27.7 %collective-permute-start.4 = (bf16[64,8192]{1,0:T(8,128)(2,1)}, bf16[64,8192]{1,0:T(8,128)(2,1)S(1)}, u32[]{:S(2)}, u32[]{:S(2)}) collective-permute-start(bf16[64,8192]{1,0:T(8,128)(2,1)} %get-tuple-element.27), channel_id=1, source_target_pairs={{96,0},{64,32},{97,1},{65,33},{98,2},{66,34},{99,3},{67,35},{100,4... | collective-permute-start | bytes 3145736 | tf_op jit(solution)/shard_map/ppermute | solution.py:446
  170.9 36.9 %copy-start.11 = (bf16[64,512]{1,0:T(8,128)(2,1)}, bf16[64,512]{1,0:T(8,128)(2,1)S(1)}, u32[]{:S(2)}) copy-start(bf16[64,512]{1,0:T(8,128)(2,1)S(1)} %collective-permute-done.5.act_other_ref) | copy-start | bytes 196612
  170.9 23.6 %collective-permute-start.6 = (bf16[64,8192]{1,0:T(8,128)(2,1)}, bf16[64,8192]{1,0:T(8,128)(2,1)S(1)}, u32[]{:S(2)}, u32[]{:S(2)}) collective-permute-start(bf16[64,8192]{1,0:T(8,128)(2,1)} %get-tuple-element.30), channel_id=1, source_target_pairs={{0,32},{32,0},{64,96},{96,64},{1,33},{33,1},{65,97},{97,65},{2,34}... | collective-permute-start | bytes 3145736 | tf_op jit(solution)/shard_map/ppermute | solution.py:287
  194.5 13.4 %copy-start.9 = (bf16[64,8192]{1,0:T(8,128)(2,1)}, bf16[64,8192]{1,0:T(8,128)(2,1)S(1)}, u32[]{:S(2)}) copy-start(bf16[64,8192]{1,0:T(8,128)(2,1)S(1)} %collective-permute-done.6.other_ref) | copy-start | bytes 3145732
  207.9 25.2 %collective-permute-start.7 = (bf16[64,8192]{1,0:T(8,128)(2,1)}, bf16[64,8192]{1,0:T(8,128)(2,1)S(1)}, u32[]{:S(2)}, u32[]{:S(2)}) collective-permute-start(bf16[64,8192]{1,0:T(8,128)(2,1)} %get-tuple-element.39), channel_id=1, source_target_pairs={{0,32},{32,0},{64,96},{96,64},{1,33},{33,1},{65,97},{97,65},{2,34}... | collective-permute-start | bytes 3145736 | tf_op jit(solution)/shard_map/ppermute | solution.py:287
  217.5 15.5 %collective-permute-start.8 = (bf16[64,512]{1,0:T(8,128)(2,1)}, bf16[64,512]{1,0:T(8,128)(2,1)S(1)}, u32[]{:S(2)}, u32[]{:S(2)}) collective-permute-start(bf16[64,512]{1,0:T(8,128)(2,1)} %get-tuple-element.40), channel_id=1, source_target_pairs={{0,32},{32,0},{64,96},{96,64},{1,33},{33,1},{65,97},{97,65},{2,34}... | collective-permute-start | bytes 196616 | tf_op jit(solution)/shard_map/ppermute | solution.py:287
  241.2 9.1 %collective-permute-start.9 = (bf16[4,4,5,128,128]{4,3,2,1,0:T(8,128)(2,1)}, bf16[4,4,5,128,128]{4,3,2,1,0:T(8,128)(2,1)S(1)}, u32[]{:S(2)}, u32[]{:S(2)}) collective-permute-start(bf16[4,4,5,128,128]{4,3,2,1,0:T(8,128)(2,1)} %get-tuple-element.43), channel_id=1, source_target_pairs={{0,1},{1,0},{2,3},{3,2},{4,5},{5,4},{6,7},{7,6},{8,9},{9,8},{10,11... | collective-permute-start | bytes 7864328 | tf_op jit(solution)/shard_map/ppermute | solution.py:432
  249.6 5.5 %collective-permute-start.17 = (bf16[4,4,5,128,128]{4,3,2,1,0:T(8,128)(2,1)}, bf16[4,4,5,128,128]{4,3,2,1,0:T(8,128)(2,1)S(1)}, u32[]{:S(2)}, u32[]{:S(2)}) collective-permute-start(bf16[4,4,5,128,128]{4,3,2,1,0:T(8,128)(2,1)} %get-tuple-element.49), channel_id=1, source_target_pairs={{0,1},{1,0},{2,3},{3,2},{4,5},{5,4},{6,7},{7,6},{8,9},{9,8},{10,11... | collective-permute-start | bytes 7864328 | tf_op jit(solution)/shard_map/ppermute | solution.py:432
  251.4 18.0 %collective-permute-start.13 = (bf16[4,5,128,128]{3,2,1,0:T(8,128)(2,1)S(1)}, bf16[4,5,128,128]{3,2,1,0:T(8,128)(2,1)S(1)}, u32[]{:S(2)}, u32[]{:S(2)}) collective-permute-start(bf16[4,5,128,128]{3,2,1,0:T(8,128)(2,1)S(1)} %get-tuple-element.55), channel_id=1, source_target_pairs={{0,6},{1,7},{2,4},{3,5},{4,2},{5,3},{6,0},{7,1},{8,14},{9,15},{10,... | collective-permute-start | bytes 1966088 | tf_op jit(solution)/shard_map/ppermute | solution.py:279
  253.2 16.4 %collective-permute-start.10 = (bf16[4,5,128,128]{3,2,1,0:T(8,128)(2,1)S(1)}, bf16[4,5,128,128]{3,2,1,0:T(8,128)(2,1)S(1)}, u32[]{:S(2)}, u32[]{:S(2)}) collective-permute-start(bf16[4,5,128,128]{3,2,1,0:T(8,128)(2,1)S(1)} %get-tuple-element.57), channel_id=1, source_target_pairs={{0,2},{1,3},{2,0},{3,1},{4,6},{5,7},{6,4},{7,5},{8,10},{9,11},{10,... | collective-permute-start | bytes 1966088 | tf_op jit(solution)/shard_map/ppermute | solution.py:279
  256.5 17.1 %collective-permute-start.21 = (bf16[4,5,128,128]{3,2,1,0:T(8,128)(2,1)S(1)}, bf16[4,5,128,128]{3,2,1,0:T(8,128)(2,1)S(1)}, u32[]{:S(2)}, u32[]{:S(2)}) collective-permute-start(bf16[4,5,128,128]{3,2,1,0:T(8,128)(2,1)S(1)} %get-tuple-element.51), channel_id=1, source_target_pairs={{0,24},{1,25},{2,26},{3,27},{4,28},{5,29},{6,30},{7,31},{8,16},{9,... | collective-permute-start | bytes 1966088 | tf_op jit(solution)/shard_map/ppermute | solution.py:279
  258.2 18.1 %collective-permute-start.18 = (bf16[4,5,128,128]{3,2,1,0:T(8,128)(2,1)S(1)}, bf16[4,5,128,128]{3,2,1,0:T(8,128)(2,1)S(1)}, u32[]{:S(2)}, u32[]{:S(2)}) collective-permute-start(bf16[4,5,128,128]{3,2,1,0:T(8,128)(2,1)S(1)} %get-tuple-element.53), channel_id=1, source_target_pairs={{0,8},{1,9},{2,10},{3,11},{4,12},{5,13},{6,14},{7,15},{8,0},{9,1},... | collective-permute-start | bytes 1966088 | tf_op jit(solution)/shard_map/ppermute | solution.py:279
  269.5 8.9 %collective-permute-start.14 = (bf16[2,5,128,128]{3,2,1,0:T(8,128)(2,1)S(1)}, bf16[2,5,128,128]{3,2,1,0:T(8,128)(2,1)S(1)}, u32[]{:S(2)}, u32[]{:S(2)}) collective-permute-start(bf16[2,5,128,128]{3,2,1,0:T(8,128)(2,1)S(1)} %get-tuple-element.65), channel_id=1, source_target_pairs={{0,2},{1,3},{2,0},{3,1},{4,6},{5,7},{6,4},{7,5},{8,10},{9,11},{10,... | collective-permute-start | bytes 983048 | tf_op jit(solution)/shard_map/ppermute | solution.py:279
  269.8 11.8 %collective-permute-start.11 = (bf16[2,5,128,128]{3,2,1,0:T(8,128)(2,1)S(1)}, bf16[2,5,128,128]{3,2,1,0:T(8,128)(2,1)S(1)}, u32[]{:S(2)}, u32[]{:S(2)}) collective-permute-start(bf16[2,5,128,128]{3,2,1,0:T(8,128)(2,1)S(1)} %get-tuple-element.63), channel_id=1, source_target_pairs={{0,6},{1,7},{2,4},{3,5},{4,2},{5,3},{6,0},{7,1},{8,14},{9,15},{10,... | collective-permute-start | bytes 983048 | tf_op jit(solution)/shard_map/ppermute | solution.py:279
  273.8 11.0 %collective-permute-start.22 = (bf16[2,5,128,128]{3,2,1,0:T(8,128)(2,1)S(1)}, bf16[2,5,128,128]{3,2,1,0:T(8,128)(2,1)S(1)}, u32[]{:S(2)}, u32[]{:S(2)}) collective-permute-start(bf16[2,5,128,128]{3,2,1,0:T(8,128)(2,1)S(1)} %get-tuple-element.61), channel_id=1, source_target_pairs={{0,8},{1,9},{2,10},{3,11},{4,12},{5,13},{6,14},{7,15},{8,0},{9,1},... | collective-permute-start | bytes 983048 | tf_op jit(solution)/shard_map/ppermute | solution.py:279
  276.4 10.8 %collective-permute-start.19 = (bf16[2,5,128,128]{3,2,1,0:T(8,128)(2,1)S(1)}, bf16[2,5,128,128]{3,2,1,0:T(8,128)(2,1)S(1)}, u32[]{:S(2)}, u32[]{:S(2)}) collective-permute-start(bf16[2,5,128,128]{3,2,1,0:T(8,128)(2,1)S(1)} %get-tuple-element.59), channel_id=1, source_target_pairs={{0,24},{1,25},{2,26},{3,27},{4,28},{5,29},{6,30},{7,31},{8,16},{9,... | collective-permute-start | bytes 983048 | tf_op jit(solution)/shard_map/ppermute | solution.py:279
  278.5 15.2 %collective-permute-start.15 = (bf16[5,128,128]{2,1,0:T(8,128)(2,1)S(1)}, bf16[5,128,128]{2,1,0:T(8,128)(2,1)S(1)}, u32[]{:S(2)}, u32[]{:S(2)}) collective-permute-start(bf16[5,128,128]{2,1,0:T(8,128)(2,1)S(1)} %get-tuple-element.68), channel_id=1, source_target_pairs={{0,8},{1,9},{2,10},{3,11},{4,12},{5,13},{6,14},{7,15},{8,0},{9,1},... | collective-permute-start | bytes 491528 | tf_op jit(solution)/shard_map/ppermute | solution.py:279
  279.7 15.3 %collective-permute-start.16 = (bf16[5,128,128]{2,1,0:T(8,128)(2,1)S(1)}, bf16[5,128,128]{2,1,0:T(8,128)(2,1)S(1)}, u32[]{:S(2)}, u32[]{:S(2)}) collective-permute-start(bf16[5,128,128]{2,1,0:T(8,128)(2,1)S(1)} %get-tuple-element.69), channel_id=1, source_target_pairs={{0,16},{1,17},{2,18},{3,19},{4,20},{5,21},{6,22},{7,23},{8,24},{9,... | collective-permute-start | bytes 491528 | tf_op jit(solution)/shard_map/ppermute | solution.py:279
  281.7 13.3 %collective-permute-start.12 = (bf16[5,128,128]{2,1,0:T(8,128)(2,1)S(1)}, bf16[5,128,128]{2,1,0:T(8,128)(2,1)S(1)}, u32[]{:S(2)}, u32[]{:S(2)}) collective-permute-start(bf16[5,128,128]{2,1,0:T(8,128)(2,1)S(1)} %fusion.19), channel_id=1, source_target_pairs={{0,24},{1,25},{2,26},{3,27},{4,28},{5,29},{6,30},{7,31},{8,16},{9,... | collective-permute-start | bytes 491528 | tf_op jit(solution)/shard_map/ppermute | solution.py:279
  284.8 16.3 %copy-start.1 = (bf16[128,8192]{1,0:T(8,128)(2,1)S(1)}, bf16[128,8192]{1,0:T(8,128)(2,1)}, u32[]{:S(2)}) copy-start(bf16[128,8192]{1,0:T(8,128)(2,1)} %param.6) | copy-start | bytes 6291460
  284.9 10.9 %collective-permute-start.23 = (bf16[5,128,128]{2,1,0:T(8,128)(2,1)S(1)}, bf16[5,128,128]{2,1,0:T(8,128)(2,1)S(1)}, u32[]{:S(2)}, u32[]{:S(2)}) collective-permute-start(bf16[5,128,128]{2,1,0:T(8,128)(2,1)S(1)} %get-tuple-element.66), channel_id=1, source_target_pairs={{0,2},{1,3},{2,0},{3,1},{4,6},{5,7},{6,4},{7,5},{8,10},{9,11},{10,... | collective-permute-start | bytes 491528 | tf_op jit(solution)/shard_map/ppermute | solution.py:279
  287.2 9.7 %collective-permute-start.24 = (bf16[5,128,128]{2,1,0:T(8,128)(2,1)S(1)}, bf16[5,128,128]{2,1,0:T(8,128)(2,1)S(1)}, u32[]{:S(2)}, u32[]{:S(2)}) collective-permute-start(bf16[5,128,128]{2,1,0:T(8,128)(2,1)S(1)} %get-tuple-element.67), channel_id=1, source_target_pairs={{0,4},{1,5},{2,6},{3,7},{4,0},{5,1},{6,2},{7,3},{8,12},{9,13},{10,... | collective-permute-start | bytes 491528 | tf_op jit(solution)/shard_map/ppermute | solution.py:279
  293.7 6.6 %collective-permute-start.20 = (bf16[5,128,128]{2,1,0:T(8,128)(2,1)S(1)}, bf16[5,128,128]{2,1,0:T(8,128)(2,1)S(1)}, u32[]{:S(2)}, u32[]{:S(2)}) collective-permute-start(bf16[5,128,128]{2,1,0:T(8,128)(2,1)S(1)} %fusion.23), channel_id=1, source_target_pairs={{0,6},{1,7},{2,4},{3,5},{4,2},{5,3},{6,0},{7,1},{8,14},{9,15},{10,... | collective-permute-start | bytes 491528 | tf_op jit(solution)/shard_map/ppermute | solution.py:279
  (7 other events, 35.7 us)
Sparse Core Ops, SparseCore 0:
  19.1 83.9 all-gather.3

commit v9 on v8

--- a/solution.py
+++ b/solution.py
@@ -309,6 +309,9 @@
     spot_z, spot_y, spot_core = me // Z, me // Y % RING, me % Y
     spots_in = jnp.stack([spot_y, spot_z, spot_core]).astype(jnp.int32)
     spots_out = jnp.stack([spot_z, spot_y, spot_core]).astype(jnp.int32)
+    where, places_in, places_out, spots_in, spots_out = lax.optimization_barrier(
+        (where, places_in, places_out, spots_in, spots_out)
+    )
 
     first_tokens = lax.dynamic_slice_in_dim(tokens, half, rows, 0)
     last_grads = lax.dynamic_slice_in_dim(cotangent, half, rows, 0)

time: 314 us -> 314 us (level)
  transfers between devices with their start and end apart: 26 -> 26, of which waited for: 17 -> 15; matrix products, arithmetic and copies ran while one was open for 3% -> 3% of each run, Pallas kernels for 5% -> 5%
where the time goes in v9:
time: 314 us; the launch traced here: 307 us
  waiting for transfers between devices  145 us (46%)
  Pallas kernels  70 us (22%)
  starting transfers between devices  37.7 us (12%)
  blocking collectives  25 us (8%)
  between operations  14.7 us (5%)
  other arithmetic  9.05 us (3%)
  local copies, waits for them, and re-layouts  6.2 us (2%)
    all_gather x1, waiting for transfers between devices, per_device(): lax.all_gather(both, 'dp', axis=0)  52.9 us
    ppermute x7, waiting for transfers between devices, swapped(): return lax.ppermute(array, 'section', PAIR)  25.8 us
    all_gather x1, blocking collectives, per_device(): lax.all_gather(jnp.stack([own_places, swapped(own_places)]), 'dp', axis=0)  25 us
    ppermute x14, starting transfers between devices, across(): lax.ppermute(array, 'dp', [(i, i + ((i // stride % RING ^ flip) - i // st...  24.8 us
    ppermute x1, waiting for transfers between devices, per_device(): arrived = lax.ppermute(leaving, 'section', DOWN)  23.3 us
    pallas_call x1, Pallas kernels, per_device(): turn(swap, where, first_tokens, arrived, last_grads, weights)  22.4 us
    ppermute x1, waiting for transfers between devices, per_device(): lax.ppermute(forward(swap, where, first_tokens, weights), 'section', UP)  21.9 us
    ppermute x14, waiting for transfers between devices, across(): lax.ppermute(array, 'dp', [(i, i + ((i // stride % RING ^ flip) - i // st...  19.4 us
  transfers between devices with their start and end apart: 26, of which 15 were waited for; matrix products, arithmetic and copies ran while one was open for 3% of the time, Pallas kernels for 5%

profile of v9, /device:TPU:32, one launch (start us, length us, event | category | flops | bytes accessed | tf_op | source)
XLA Modules:
  0.0 307.3 jit_solution(1004956742642319374)
XLA Ops:
  7.2 1.6 collective-permute-start.2
  9.4 5.3 %collective-permute-done.2 = bf16[5,128,128]{2,1,0:T(8,128)(2,1)S(1)} collective-permute-done((bf16[5,128,128]{2,1,0:T(8,128)(2,1)}, bf16[5,128,128]{2,1,0:T(8,128)(2,1)S(1)}, u32[]{:S(2)}, u32[]{:S(2)}) %collective-permute-start.2) | collective-permute-done | bytes 163872 | tf_op jit(solution)/shard_map/ppermute | solution.py:287
  14.6 2.4 collective-permute-done.1
  17.0 1.9 pad_maximum_fusion
  19.0 1.6 collective-permute-start
  23.0 25.0 %all-gather = s32[64,2,5]{2,1,0:T(2,128)S(1)} all-gather(s32[2,2,5]{2,1,0:T(2,128)S(1)} %pad_add_fusion), channel_id=2, replica_groups=mesh['section'=4,'dp'=32] {'dp'}, dimensions={0}, use_global_device_ids=true | all-gather | bytes 2640 | tf_op jit(solution)/shard_map/all_gather | solution.py:302
  50.2 52.9 %all-gather.4.cloned.1.call-done = bf16[128,5,128,128]{3,2,1,0:T(8,128)(2,1)} async-done(((bf16[4,5,128,128]{3,2,1,0:T(8,128)(2,1)}), bf16[128,5,128,128]{3,2,1,0:T(8,128)(2,1)}) %all-gather.4.cloned.1.call-update) | async-done | bytes 20971536 | tf_op jit(solution)/shard_map/all_gather | solution.py:300
  103.0 12.2 %forward_layers.1 = bf16[64,8192]{1,0:T(8,128)(2,1)} custom-call(s32[2]{0:T(128)} %pad_add_fusion.2.swap_ref, s32[1024]{0:T(1024)} %compare_select_fusion.where_ref, bf16[64,8192]{1,0:T(8,128)(2,1)} %constant_dynamic-slice_fusion.1.first_ref.tokens_ref, bf16[32,2,2,5,128,128]{5,4,3,2,1,0:T(8,128)(2,1)} %bitcast.102), custom_call_target="tpu_custom_call" | custom-call | flops 2147483648 | bytes 20971520 | tf_op jit(solution)/shard_map/forward_layers/pallas_call | solution.py:447
  115.2 4.7 %collective-permute-start.3 = (bf16[64,8192]{1,0:T(8,128)(2,1)}, bf16[64,8192]{1,0:T(8,128)(2,1)S(1)}, u32[]{:S(2)}, u32[]{:S(2)}) collective-permute-start(bf16[64,8192]{1,0:T(8,128)(2,1)} %forward_layers.1), channel_id=1, source_target_pairs={{0,96},{32,64},{1,97},{33,65},{2,98},{34,66},{3,99},{35,67},{4,100... | collective-permute-start | bytes 3145736 | tf_op jit(solution)/shard_map/ppermute | solution.py:447
  121.0 21.9 %collective-permute-done.3.arrived_ref = bf16[64,8192]{1,0:T(8,128)(2,1)S(1)} collective-permute-done((bf16[64,8192]{1,0:T(8,128)(2,1)}, bf16[64,8192]{1,0:T(8,128)(2,1)S(1)}, u32[]{:S(2)}, u32[]{:S(2)}) %collective-permute-start.3) | collective-permute-done | bytes 1048608 | tf_op jit(solution)/shard_map/ppermute | solution.py:447
  143.9 22.4 %turn_layers.1 = (bf16[64,8192]{1,0:T(8,128)(2,1)}, f32[2,64,512]{2,1,0:T(8,128)}, f32[2,64,128]{2,1,0:T(8,128)}, bf16[64,8192]{1,0:T(8,128)(2,1)}, bf16[64,8192...) custom-call(s32[2]{0:T(128)} %pad_add_fusion.2.swap_ref, ...), custom_call_target="tpu_custom_call" | custom-call | flops 3758096384 | bytes 20971520 | tf_op jit(solution)/shard_map/turn_layers/pallas_call | solution.py:448
  166.7 1.3 collective-permute-start.4
  168.0 2.9 collective-permute-done.5.act_other_ref
  171.2 23.3 %collective-permute-done.4.arrived_ref = bf16[64,8192]{1,0:T(8,128)(2,1)S(1)} collective-permute-done((bf16[64,8192]{1,0:T(8,128)(2,1)}, bf16[64,8192]{1,0:T(8,128)(2,1)S(1)}, u32[]{:S(2)}, u32[]{:S(2)}) %collective-permute-start.4) | collective-permute-done | bytes 1048608 | tf_op jit(solution)/shard_map/ppermute | solution.py:449
  195.5 12.3 %backward_high.1 = (bf16[64,512]{1,0:T(8,128)(2,1)}, bf16[64,8192]{1,0:T(8,128)(2,1)}, bf16[64,8192]{1,0:T(8,128)(2,1)}, bf16[64,8192]{1,0:T(8,128)(2,1)}) custom-call(s32[2]{0:T(128)} %pad_add_fusion.2.swap_ref, s32[1024]{0:T(1024)} %compare_select_fusion.where_ref, bf16[64,8192]{1,0:T(8,128)(2,1)} %get-tuple-element.40.hidden_ref, ...), custom_call_target="tpu_custom_call" | custom-call | flops 1073741824 | bytes 10485760 | tf_op jit(solution)/shard_map/backward_high/pallas_call | solution.py:453
  209.1 7.8 %backward_low.1 = (bf16[64,512]{1,0:T(8,128)(2,1)}, bf16[64,512]{1,0:T(8,128)(2,1)}) custom-call(s32[2]{0:T(128)} %pad_add_fusion.2.swap_ref, s32[1024]{0:T(1024)} %compare_select_fusion.where_ref, bf16[64,8192]{1,0:T(8,128)(2,1)} %get-tuple-element.44.middle_ref, bf16[64,512]{1,0:T(8,128)(2,1)} %get-tuple-element.45.high_ref, ...), custom_call_target="tpu_custom_call" | custom-call | flops 536870912 | bytes 20971520 | tf_op jit(solution)/shard_map/backward_low/pallas_call | solution.py:455
  217.9 15.1 %collective-permute-done.8.dpre_other_ref = bf16[64,512]{1,0:T(8,128)(2,1)S(1)} collective-permute-done((bf16[64,512]{1,0:T(8,128)(2,1)}, bf16[64,512]{1,0:T(8,128)(2,1)S(1)}, u32[]{:S(2)}, u32[]{:S(2)}) %collective-permute-start.8) | collective-permute-done | bytes 65568 | tf_op jit(solution)/shard_map/ppermute | solution.py:287
  233.7 7.5 %gradient_in.1 = (bf16[4,4,5,128,128]{4,3,2,1,0:T(8,128)(2,1)}, bf16[4,4,5,128,128]{4,3,2,1,0:T(8,128)(2,1)}) custom-call(s32[3]{0:T(128)} %get-tuple-element.31.spots_ref, s32[160]{0:T(256)} %reshape_squeeze.6.places_ref, bf16[64,8192]{1,0:T(8,128)(2,1)} %get-tuple-element.34.own_ref, bf16[64,8192]{1,0:T(8,128)(2,1)} %copy-done.9, ...), custom_call_target="tpu_custom_call" | custom-call | flops 1073741824 | bytes 62914560 | tf_op jit(solution)/shard_map/gradient_in/pallas_call | solution.py:458
  241.2 7.7 %gradient_out.1 = (bf16[4,4,5,128,128]{4,3,2,1,0:T(8,128)(2,1)}, bf16[4,4,5,128,128]{4,3,2,1,0:T(8,128)(2,1)}) custom-call(s32[3]{0:T(128)} %get-tuple-element.52.spots_ref, s32[160]{0:T(256)} %reshape_squeeze.7.places_ref, bf16[64,512]{1,0:T(8,128)(2,1)} %get-tuple-element.54.act_own_ref, bf16[64,512]{1,0:T(8,128)(2,1)} %copy-done.11, ...), custom_call_target="tpu_custom_call" | custom-call | flops 1073741824 | bytes 62914560 | tf_op jit(solution)/shard_map/gradient_out/pallas_call | solution.py:459
  250.6 2.1 collective-permute-start.13
  255.4 1.6 collective-permute-start.21
  257.0 1.9 collective-permute-start.18
  258.9 9.9 %collective-permute-done.13 = bf16[4,5,128,128]{3,2,1,0:T(8,128)(2,1)S(1)} collective-permute-done((bf16[4,5,128,128]{3,2,1,0:T(8,128)(2,1)S(1)}, bf16[4,5,128,128]{3,2,1,0:T(8,128)(2,1)S(1)}, u32[]{:S(2)}, u32[]{:S(2)}) %collective-permute-start.13) | collective-permute-done | bytes 655392 | tf_op jit(solution)/shard_map/ppermute | solution.py:279
  269.3 1.9 collective-permute-start.11
  271.1 1.4 collective-permute-done.21
  272.7 2.4 collective-permute-start.22
  275.3 1.8 collective-permute-start.19
  279.1 1.9 collective-permute-start.16
  281.6 2.0 collective-permute-done.22
  283.8 1.6 collective-permute-start.23
  286.1 6.4 %collective-permute-start.24 = (bf16[5,128,128]{2,1,0:T(8,128)(2,1)S(1)}, bf16[5,128,128]{2,1,0:T(8,128)(2,1)S(1)}, u32[]{:S(2)}, u32[]{:S(2)}) collective-permute-start(bf16[5,128,128]{2,1,0:T(8,128)(2,1)S(1)} %get-tuple-element.77), channel_id=1, source_target_pairs={{0,4},{1,5},{2,6},{3,7},{4,0},{5,1},{6,2},{7,3},{8,12},{9,13},{10,... | collective-permute-start | bytes 491528 | tf_op jit(solution)/shard_map/ppermute | solution.py:279
  295.8 3.4 %collective-permute-done.20 = bf16[5,128,128]{2,1,0:T(8,128)(2,1)S(1)} collective-permute-done((bf16[5,128,128]{2,1,0:T(8,128)(2,1)S(1)}, bf16[5,128,128]{2,1,0:T(8,128)(2,1)S(1)}, u32[]{:S(2)}, u32[]{:S(2)}) %collective-permute-start.20) | collective-permute-done | bytes 163872 | tf_op jit(solution)/shard_map/ppermute | solution.py:279
  (83 shorter events, 24.5 us)
Async XLA Ops:
  7.2 14.7 %copy-start = (bf16[128,8192]{1,0:T(8,128)(2,1)S(1)}, bf16[128,8192]{1,0:T(8,128)(2,1)}, u32[]{:S(2)}) copy-start(bf16[128,8192]{1,0:T(8,128)(2,1)} %param.6) | copy-start | bytes 6291460
  7.2 11.8 %copy-start.7 = (s32[1,5]{1,0:T(1,128)S(1)}, s32[1,5]{1,0:T(1,128)}, u32[]{:S(2)}) copy-start(s32[1,5]{1,0:T(1,128)} %param.10) | copy-start | bytes 64
  7.2 95.8 %all-gather.4.cloned.1.call-start = ((), (), s32[]{:S(2)}) async-start(), calls=%async_computation | async-start | bytes 21626880 | tf_op jit(solution)/shard_map/all_gather | solution.py:300
  7.2 7.4 %collective-permute-start.2 = (bf16[5,128,128]{2,1,0:T(8,128)(2,1)}, bf16[5,128,128]{2,1,0:T(8,128)(2,1)S(1)}, u32[]{:S(2)}, u32[]{:S(2)}) collective-permute-start(bf16[5,128,128]{2,1,0:T(8,128)(2,1)} %bitcast.108), channel_id=1, source_target_pairs={{0,32},{32,0},{64,96},{96,64},{1,33},{33,1},{65,97},{97,65},{2,34}... | collective-permute-start | bytes 491528 | tf_op jit(solution)/shard_map/ppermute | solution.py:287
  8.8 8.2 %collective-permute-start.1 = (bf16[5,128,128]{2,1,0:T(8,128)(2,1)}, bf16[5,128,128]{2,1,0:T(8,128)(2,1)S(1)}, u32[]{:S(2)}, u32[]{:S(2)}) collective-permute-start(bf16[5,128,128]{2,1,0:T(8,128)(2,1)} %bitcast.109), channel_id=1, source_target_pairs={{0,32},{32,0},{64,96},{96,64},{1,33},{33,1},{65,97},{97,65},{2,34}... | collective-permute-start | bytes 491528 | tf_op jit(solution)/shard_map/ppermute | solution.py:287
  19.0 4.0 %collective-permute-start = (s32[2,5]{1,0:T(2,128)S(1)}, s32[2,5]{1,0:T(2,128)S(1)}, u32[]{:S(2)}, u32[]{:S(2)}) collective-permute-start(s32[2,5]{1,0:T(2,128)S(1)} %get-tuple-element.83), channel_id=1, source_target_pairs={{0,32},{32,0},{64,96},{96,64},{1,33},{33,1},{65,97},{97,65},{2,34}... | collective-permute-start | bytes 128 | tf_op jit(solution)/shard_map/ppermute | solution.py:287
  103.0 16.9 %copy-start.6 = (bf16[128,8192]{1,0:T(8,128)(2,1)S(1)}, bf16[128,8192]{1,0:T(8,128)(2,1)}, u32[]{:S(2)}) copy-start(bf16[128,8192]{1,0:T(8,128)(2,1)} %param.11) | copy-start | bytes 6291460
  115.2 27.7 %collective-permute-start.3 = (bf16[64,8192]{1,0:T(8,128)(2,1)}, bf16[64,8192]{1,0:T(8,128)(2,1)S(1)}, u32[]{:S(2)}, u32[]{:S(2)}) collective-permute-start(bf16[64,8192]{1,0:T(8,128)(2,1)} %forward_layers.1), channel_id=1, source_target_pairs={{0,96},{32,64},{1,97},{33,65},{2,98},{34,66},{3,99},{35,67},{4,100... | collective-permute-start | bytes 3145736 | tf_op jit(solution)/shard_map/ppermute | solution.py:447
  166.4 4.6 %collective-permute-start.5 = (bf16[64,512]{1,0:T(8,128)(2,1)}, bf16[64,512]{1,0:T(8,128)(2,1)S(1)}, u32[]{:S(2)}, u32[]{:S(2)}) collective-permute-start(bf16[64,512]{1,0:T(8,128)(2,1)} %get-tuple-element.37), channel_id=1, source_target_pairs={{0,32},{32,0},{64,96},{96,64},{1,33},{33,1},{65,97},{97,65},{2,34}... | collective-permute-start | bytes 196616 | tf_op jit(solution)/shard_map/ppermute | solution.py:287
  166.7 27.7 %collective-permute-start.4 = (bf16[64,8192]{1,0:T(8,128)(2,1)}, bf16[64,8192]{1,0:T(8,128)(2,1)S(1)}, u32[]{:S(2)}, u32[]{:S(2)}) collective-permute-start(bf16[64,8192]{1,0:T(8,128)(2,1)} %get-tuple-element.35), channel_id=1, source_target_pairs={{96,0},{64,32},{97,1},{65,33},{98,2},{66,34},{99,3},{67,35},{100,4... | collective-permute-start | bytes 3145736 | tf_op jit(solution)/shard_map/ppermute | solution.py:449
  170.9 36.9 %copy-start.11 = (bf16[64,512]{1,0:T(8,128)(2,1)}, bf16[64,512]{1,0:T(8,128)(2,1)S(1)}, u32[]{:S(2)}) copy-start(bf16[64,512]{1,0:T(8,128)(2,1)S(1)} %collective-permute-done.5.act_other_ref) | copy-start | bytes 196612
  170.9 23.5 %collective-permute-start.6 = (bf16[64,8192]{1,0:T(8,128)(2,1)}, bf16[64,8192]{1,0:T(8,128)(2,1)S(1)}, u32[]{:S(2)}, u32[]{:S(2)}) collective-permute-start(bf16[64,8192]{1,0:T(8,128)(2,1)} %get-tuple-element.38), channel_id=1, source_target_pairs={{0,32},{32,0},{64,96},{96,64},{1,33},{33,1},{65,97},{97,65},{2,34}... | collective-permute-start | bytes 3145736 | tf_op jit(solution)/shard_map/ppermute | solution.py:287
  194.5 13.4 %copy-start.9 = (bf16[64,8192]{1,0:T(8,128)(2,1)}, bf16[64,8192]{1,0:T(8,128)(2,1)S(1)}, u32[]{:S(2)}) copy-start(bf16[64,8192]{1,0:T(8,128)(2,1)S(1)} %collective-permute-done.6.other_ref) | copy-start | bytes 3145732
  207.9 25.2 %collective-permute-start.7 = (bf16[64,8192]{1,0:T(8,128)(2,1)}, bf16[64,8192]{1,0:T(8,128)(2,1)S(1)}, u32[]{:S(2)}, u32[]{:S(2)}) collective-permute-start(bf16[64,8192]{1,0:T(8,128)(2,1)} %get-tuple-element.47), channel_id=1, source_target_pairs={{0,32},{32,0},{64,96},{96,64},{1,33},{33,1},{65,97},{97,65},{2,34}... | collective-permute-start | bytes 3145736 | tf_op jit(solution)/shard_map/ppermute | solution.py:287
  216.9 16.2 %collective-permute-start.8 = (bf16[64,512]{1,0:T(8,128)(2,1)}, bf16[64,512]{1,0:T(8,128)(2,1)S(1)}, u32[]{:S(2)}, u32[]{:S(2)}) collective-permute-start(bf16[64,512]{1,0:T(8,128)(2,1)} %get-tuple-element.48), channel_id=1, source_target_pairs={{0,32},{32,0},{64,96},{96,64},{1,33},{33,1},{65,97},{97,65},{2,34}... | collective-permute-start | bytes 196616 | tf_op jit(solution)/shard_map/ppermute | solution.py:287
  241.2 8.2 %collective-permute-start.9 = (bf16[4,4,5,128,128]{4,3,2,1,0:T(8,128)(2,1)}, bf16[4,4,5,128,128]{4,3,2,1,0:T(8,128)(2,1)S(1)}, u32[]{:S(2)}, u32[]{:S(2)}) collective-permute-start(bf16[4,4,5,128,128]{4,3,2,1,0:T(8,128)(2,1)} %get-tuple-element.51), channel_id=1, source_target_pairs={{0,1},{1,0},{2,3},{3,2},{4,5},{5,4},{6,7},{7,6},{8,9},{9,8},{10,11... | collective-permute-start | bytes 7864328 | tf_op jit(solution)/shard_map/ppermute | solution.py:435
  248.9 5.2 %collective-permute-start.17 = (bf16[4,4,5,128,128]{4,3,2,1,0:T(8,128)(2,1)}, bf16[4,4,5,128,128]{4,3,2,1,0:T(8,128)(2,1)S(1)}, u32[]{:S(2)}, u32[]{:S(2)}) collective-permute-start(bf16[4,4,5,128,128]{4,3,2,1,0:T(8,128)(2,1)} %get-tuple-element.59), channel_id=1, source_target_pairs={{0,1},{1,0},{2,3},{3,2},{4,5},{5,4},{6,7},{7,6},{8,9},{9,8},{10,11... | collective-permute-start | bytes 7864328 | tf_op jit(solution)/shard_map/ppermute | solution.py:435
  250.6 18.2 %collective-permute-start.13 = (bf16[4,5,128,128]{3,2,1,0:T(8,128)(2,1)S(1)}, bf16[4,5,128,128]{3,2,1,0:T(8,128)(2,1)S(1)}, u32[]{:S(2)}, u32[]{:S(2)}) collective-permute-start(bf16[4,5,128,128]{3,2,1,0:T(8,128)(2,1)S(1)} %get-tuple-element.65), channel_id=1, source_target_pairs={{0,6},{1,7},{2,4},{3,5},{4,2},{5,3},{6,0},{7,1},{8,14},{9,15},{10,... | collective-permute-start | bytes 1966088 | tf_op jit(solution)/shard_map/ppermute | solution.py:279
  252.7 16.4 %collective-permute-start.10 = (bf16[4,5,128,128]{3,2,1,0:T(8,128)(2,1)S(1)}, bf16[4,5,128,128]{3,2,1,0:T(8,128)(2,1)S(1)}, u32[]{:S(2)}, u32[]{:S(2)}) collective-permute-start(bf16[4,5,128,128]{3,2,1,0:T(8,128)(2,1)S(1)} %get-tuple-element.67), channel_id=1, source_target_pairs={{0,2},{1,3},{2,0},{3,1},{4,6},{5,7},{6,4},{7,5},{8,10},{9,11},{10,... | collective-permute-start | bytes 1966088 | tf_op jit(solution)/shard_map/ppermute | solution.py:279
  255.4 17.1 %collective-permute-start.21 = (bf16[4,5,128,128]{3,2,1,0:T(8,128)(2,1)S(1)}, bf16[4,5,128,128]{3,2,1,0:T(8,128)(2,1)S(1)}, u32[]{:S(2)}, u32[]{:S(2)}) collective-permute-start(bf16[4,5,128,128]{3,2,1,0:T(8,128)(2,1)S(1)} %get-tuple-element.61), channel_id=1, source_target_pairs={{0,24},{1,25},{2,26},{3,27},{4,28},{5,29},{6,30},{7,31},{8,16},{9,... | collective-permute-start | bytes 1966088 | tf_op jit(solution)/shard_map/ppermute | solution.py:279
  257.0 18.1 %collective-permute-start.18 = (bf16[4,5,128,128]{3,2,1,0:T(8,128)(2,1)S(1)}, bf16[4,5,128,128]{3,2,1,0:T(8,128)(2,1)S(1)}, u32[]{:S(2)}, u32[]{:S(2)}) collective-permute-start(bf16[4,5,128,128]{3,2,1,0:T(8,128)(2,1)S(1)} %get-tuple-element.63), channel_id=1, source_target_pairs={{0,8},{1,9},{2,10},{3,11},{4,12},{5,13},{6,14},{7,15},{8,0},{9,1},... | collective-permute-start | bytes 1966088 | tf_op jit(solution)/shard_map/ppermute | solution.py:279
  268.9 8.9 %collective-permute-start.14 = (bf16[2,5,128,128]{3,2,1,0:T(8,128)(2,1)S(1)}, bf16[2,5,128,128]{3,2,1,0:T(8,128)(2,1)S(1)}, u32[]{:S(2)}, u32[]{:S(2)}) collective-permute-start(bf16[2,5,128,128]{3,2,1,0:T(8,128)(2,1)S(1)} %get-tuple-element.75), channel_id=1, source_target_pairs={{0,2},{1,3},{2,0},{3,1},{4,6},{5,7},{6,4},{7,5},{8,10},{9,11},{10,... | collective-permute-start | bytes 983048 | tf_op jit(solution)/shard_map/ppermute | solution.py:279
  269.3 11.8 %collective-permute-start.11 = (bf16[2,5,128,128]{3,2,1,0:T(8,128)(2,1)S(1)}, bf16[2,5,128,128]{3,2,1,0:T(8,128)(2,1)S(1)}, u32[]{:S(2)}, u32[]{:S(2)}) collective-permute-start(bf16[2,5,128,128]{3,2,1,0:T(8,128)(2,1)S(1)} %get-tuple-element.73), channel_id=1, source_target_pairs={{0,6},{1,7},{2,4},{3,5},{4,2},{5,3},{6,0},{7,1},{8,14},{9,15},{10,... | collective-permute-start | bytes 983048 | tf_op jit(solution)/shard_map/ppermute | solution.py:279
  272.7 11.0 %collective-permute-start.22 = (bf16[2,5,128,128]{3,2,1,0:T(8,128)(2,1)S(1)}, bf16[2,5,128,128]{3,2,1,0:T(8,128)(2,1)S(1)}, u32[]{:S(2)}, u32[]{:S(2)}) collective-permute-start(bf16[2,5,128,128]{3,2,1,0:T(8,128)(2,1)S(1)} %get-tuple-element.71), channel_id=1, source_target_pairs={{0,8},{1,9},{2,10},{3,11},{4,12},{5,13},{6,14},{7,15},{8,0},{9,1},... | collective-permute-start | bytes 983048 | tf_op jit(solution)/shard_map/ppermute | solution.py:279
  275.3 10.8 %collective-permute-start.19 = (bf16[2,5,128,128]{3,2,1,0:T(8,128)(2,1)S(1)}, bf16[2,5,128,128]{3,2,1,0:T(8,128)(2,1)S(1)}, u32[]{:S(2)}, u32[]{:S(2)}) collective-permute-start(bf16[2,5,128,128]{3,2,1,0:T(8,128)(2,1)S(1)} %get-tuple-element.69), channel_id=1, source_target_pairs={{0,24},{1,25},{2,26},{3,27},{4,28},{5,29},{6,30},{7,31},{8,16},{9,... | collective-permute-start | bytes 983048 | tf_op jit(solution)/shard_map/ppermute | solution.py:279
  277.9 14.7 %collective-permute-start.15 = (bf16[5,128,128]{2,1,0:T(8,128)(2,1)S(1)}, bf16[5,128,128]{2,1,0:T(8,128)(2,1)S(1)}, u32[]{:S(2)}, u32[]{:S(2)}) collective-permute-start(bf16[5,128,128]{2,1,0:T(8,128)(2,1)S(1)} %get-tuple-element.78), channel_id=1, source_target_pairs={{0,8},{1,9},{2,10},{3,11},{4,12},{5,13},{6,14},{7,15},{8,0},{9,1},... | collective-permute-start | bytes 491528 | tf_op jit(solution)/shard_map/ppermute | solution.py:279
  279.1 14.7 %collective-permute-start.16 = (bf16[5,128,128]{2,1,0:T(8,128)(2,1)S(1)}, bf16[5,128,128]{2,1,0:T(8,128)(2,1)S(1)}, u32[]{:S(2)}, u32[]{:S(2)}) collective-permute-start(bf16[5,128,128]{2,1,0:T(8,128)(2,1)S(1)} %get-tuple-element.79), channel_id=1, source_target_pairs={{0,16},{1,17},{2,18},{3,19},{4,20},{5,21},{6,22},{7,23},{8,24},{9,... | collective-permute-start | bytes 491528 | tf_op jit(solution)/shard_map/ppermute | solution.py:279
  281.1 12.8 %collective-permute-start.12 = (bf16[5,128,128]{2,1,0:T(8,128)(2,1)S(1)}, bf16[5,128,128]{2,1,0:T(8,128)(2,1)S(1)}, u32[]{:S(2)}, u32[]{:S(2)}) collective-permute-start(bf16[5,128,128]{2,1,0:T(8,128)(2,1)S(1)} %fusion.19), channel_id=1, source_target_pairs={{0,24},{1,25},{2,26},{3,27},{4,28},{5,29},{6,30},{7,31},{8,16},{9,... | collective-permute-start | bytes 491528 | tf_op jit(solution)/shard_map/ppermute | solution.py:279
  283.7 16.3 %copy-start.1 = (bf16[128,8192]{1,0:T(8,128)(2,1)S(1)}, bf16[128,8192]{1,0:T(8,128)(2,1)}, u32[]{:S(2)}) copy-start(bf16[128,8192]{1,0:T(8,128)(2,1)} %param.6) | copy-start | bytes 6291460
  283.8 10.9 %collective-permute-start.23 = (bf16[5,128,128]{2,1,0:T(8,128)(2,1)S(1)}, bf16[5,128,128]{2,1,0:T(8,128)(2,1)S(1)}, u32[]{:S(2)}, u32[]{:S(2)}) collective-permute-start(bf16[5,128,128]{2,1,0:T(8,128)(2,1)S(1)} %get-tuple-element.76), channel_id=1, source_target_pairs={{0,2},{1,3},{2,0},{3,1},{4,6},{5,7},{6,4},{7,5},{8,10},{9,11},{10,... | collective-permute-start | bytes 491528 | tf_op jit(solution)/shard_map/ppermute | solution.py:279
  286.1 9.7 %collective-permute-start.24 = (bf16[5,128,128]{2,1,0:T(8,128)(2,1)S(1)}, bf16[5,128,128]{2,1,0:T(8,128)(2,1)S(1)}, u32[]{:S(2)}, u32[]{:S(2)}) collective-permute-start(bf16[5,128,128]{2,1,0:T(8,128)(2,1)S(1)} %get-tuple-element.77), channel_id=1, source_target_pairs={{0,4},{1,5},{2,6},{3,7},{4,0},{5,1},{6,2},{7,3},{8,12},{9,13},{10,... | collective-permute-start | bytes 491528 | tf_op jit(solution)/shard_map/ppermute | solution.py:279
  292.6 6.6 %collective-permute-start.20 = (bf16[5,128,128]{2,1,0:T(8,128)(2,1)S(1)}, bf16[5,128,128]{2,1,0:T(8,128)(2,1)S(1)}, u32[]{:S(2)}, u32[]{:S(2)}) collective-permute-start(bf16[5,128,128]{2,1,0:T(8,128)(2,1)S(1)} %fusion.23), channel_id=1, source_target_pairs={{0,6},{1,7},{2,4},{3,5},{4,2},{5,3},{6,0},{7,1},{8,14},{9,15},{10,... | collective-permute-start | bytes 491528 | tf_op jit(solution)/shard_map/ppermute | solution.py:279
  (7 other events, 35.5 us)
Sparse Core Ops, SparseCore 0:
  19.1 83.9 all-gather.3
